TPU v7x, 32 devices: a whole 2x2x4 slice. The times are simulated.
32 devices in a mesh: chain: 4 (over z), rows: 8 (over y, x, core).
Axes of the slice: x: 2, y: 2, z: 4, core: 2. Of those that a mesh axis runs over, the one named last changes fastest.
Arguments:
- right_side: bfloat16 [8192, 768], P(('chain', 'rows')), may hold values from -6 to 6
- entering: float32 [8192, 256], P(('chain', 'rows')), may hold values from -6 to 6
- first_updates: float32 [2048, 512], P('rows'), may hold values from -6 to 6
- diag_inverse: bfloat16 [4, 2048, 2048], P('chain', 'rows'), may hold values from -2 to 2, as said below
- tile_blocks: bfloat16 [4, 8, 128, 2048], P('chain', 'rows'), may hold values from -0.1875 to 0.1875
- target_row_blocks: int32 [4, 8], P('chain', 'rows'), may hold values from 0 to 15
- tile_usage_order: int32 [4, 8], P('chain'), may hold values from 0 to 7, each once within a row
- live_tile_count: int32 [4], P('chain'), may hold values from 2 to 8
Outputs:
- solution: float32 [8192, 768], P(('chain', 'rows'))
- updates: float32 [8192, 768], P(('chain', 'rows'))
Inputs may be any that keep to these rules, and one draw needn't show every extreme that they name: `diag_inverse`: lower triangular. `tile_usage_order`: each row names each of the 8 slots once; the first live_tile_count[s] entries name the live slots of supernode s.
All inputs are finite; a program needn't handle non-finite values.
Results may differ from a plain program's by a relative error of at most 0.013.
Values may be sent and summed in bfloat16 or wider, within the bound.
No kernel may reach another device: no remote copies, remote signals or barrier semaphores. Data moves between devices by JAX's collectives and lax.ppermute only.
A program may use at most 64 MiB of HBM per device.

v0:
```python
import jax
import jax.numpy as jnp
from jax import lax
from jax.sharding import PartitionSpec as P

PW = 256


def shifted(block, axis, distance):
    devices = range(lax.axis_size(axis))
    route = [(i - distance, i) for i in devices if i - distance in devices]
    return lax.ppermute(block, axis, route)


def active_slot_list(tile_usage_order, live_tile_count, leading_part, slot_entries):
    every_slot = tile_usage_order.shape[1]
    positions = lax.broadcasted_iota(jnp.int32, (1, every_slot), 1)
    counted = positions < live_tile_count[0]
    wanted = leading_part + lax.broadcasted_iota(jnp.int32, (slot_entries, 1), 0)
    matches = jnp.logical_and(tile_usage_order[0][None, :] == wanted, counted)
    return jnp.sum(matches.astype(jnp.float32), axis=1)


def multiply(matrix, vector):
    return jnp.dot(matrix, vector, preferred_element_type=jnp.float32)


def nothing(matrix, vector):
    return jnp.zeros((matrix.shape[0], vector.shape[1]), jnp.float32)


def body(
    right_side,
    entering,
    first_updates,
    diag_inverse,
    tile_blocks,
    target_row_blocks,
    tile_usage_order,
    live_tile_count,
):
    slot_entries = tile_blocks.shape[1]
    tile_height = tile_blocks.shape[2]
    separator = tile_blocks.shape[3]
    ticks_total = right_side.shape[1] // PW
    row_blocks = separator // tile_height
    is_first = (lax.axis_index("chain") == 0).astype(jnp.float32)
    leading_part = lax.axis_index("rows") * slot_entries
    slot_alive_flags = active_slot_list(
        tile_usage_order, live_tile_count, leading_part, slot_entries
    )
    block_grid = lax.broadcasted_iota(jnp.int32, (row_blocks, slot_entries), 0)
    tile_placement_map = (block_grid == target_row_blocks[0][None, :]).astype(
        jnp.float32
    ) * slot_alive_flags[None, :]
    inverse_rows = diag_inverse[0]
    own_tiles = tile_blocks[0]
    solved_list = []
    passed_list = []
    incoming = entering
    for tick in range(ticks_total):
        head_rows = (
            right_side[:, tick * PW : (tick + 1) * PW].astype(jnp.float32) - incoming
        ).astype(jnp.bfloat16)
        portion = lax.all_gather(head_rows, "rows", axis=0, tiled=True)
        solved = jnp.dot(inverse_rows, portion, preferred_element_type=jnp.float32)
        slot_terms = [lax.cond(slot_alive_flags[0] > 0, multiply, nothing, own_tiles[0], portion)]
        products = jnp.stack(slot_terms)
        one_solved = solved
        partial_value = jnp.einsum(
            "bm,mtp->btp", tile_placement_map, products, precision=lax.Precision.HIGHEST
        ).reshape(separator, PW)
        passed = lax.psum_scatter(
            partial_value.astype(jnp.bfloat16), "rows", scatter_dimension=0, tiled=True
        ).astype(jnp.float32)
        solved, passed = (one_solved, passed)
        solved_list.append(solved)
        passed_list.append(passed)
        if tick + 1 < ticks_total:
            moved = shifted(passed.astype(jnp.bfloat16), "chain", 1).astype(passed.dtype)
            incoming = moved + is_first * first_updates[:, tick * PW : (tick + 1) * PW]
    return (jnp.concatenate(solved_list, axis=1), jnp.concatenate(passed_list, axis=1))


def solution(mesh):
    placed = (
        P(("chain", "rows"), None),
        P(("chain", "rows"), None),
        P("rows", None),
        P("chain", "rows", None),
        P("chain", "rows", None, None),
        P("chain", "rows"),
        P("chain", None),
        P("chain"),
    )
    return jax.shard_map(
        body,
        mesh=mesh,
        in_specs=placed,
        out_specs=(P(("chain", "rows"), None), P(("chain", "rows"), None)),
        check_vma=False,
    )
```

profile of v0, /device:TPU:0, one launch (start us, length us, event | category | flops | bytes accessed | tf_op | source)
XLA Modules:
  0.0 226.0 jit_solution(15644400745650187902)
XLA Ops:
  7.2 0.0 copy-start
  7.2 0.0 all-gather.4.cloned.1.call-start
  7.2 1.7 subtract_convert_fusion.2
  9.0 0.0 all-gather.4.cloned.1.call-update
  9.0 0.0 reduce-scatter.4.cloned.1.call-start
  10.3 1.3 fusion.3
  12.3 0.6 compare_select_fusion
  12.9 23.8 %all-gather.4.cloned.1.call-done = bf16[2048,256]{1,0:T(8,128)(2,1)} async-done(((bf16[256,256]{1,0:T(8,128)(2,1)}), bf16[2048,256]{1,0:T(8,128)(2,1)}) %all-gather.4.cloned.1.call-update) | async-done | bytes 1048592 | tf_op jit(solution)/shard_map/all_gather | solution.py:65
  36.7 0.0 copy-start.5
  36.7 0.0 copy-start.6
  36.7 1.3 multiply_convert_fusion.2
  38.0 0.0 copy-start.1
  38.0 0.0 reduce-scatter.4.cloned.1.call-update
  38.0 0.0 all-gather.6.cloned.1.call-start
  38.1 37.8 %reduce-scatter.4.cloned.1.call-done = bf16[256,256]{1,0:T(8,128)(2,1)} async-done(((bf16[2048,256]{1,0:T(8,128)(2,1)}), bf16[256,256]{1,0:T(8,128)(2,1)}) %reduce-scatter.4.cloned.1.call-update) | async-done | bytes 131088 | tf_op jit(solution)/shard_map/reduce_scatter | solution.py:73
  75.9 3.4 %collective-permute-start = (bf16[256,256]{1,0:T(8,128)(2,1)}, bf16[256,256]{1,0:T(8,128)(2,1)S(1)}, u32[]{:S(2)}, u32[]{:S(2)}) collective-permute-start(bf16[256,256]{1,0:T(8,128)(2,1)} %reduce-scatter.4.cloned.1.call-done), channel_id=1, source_target_pairs={{0,8},{8,16},{16,24},{1,9},{9,17},{17,25},{2,10},{10,18},{18,26},{... | collective-permute-start | bytes 393224 | tf_op jit(solution)/shard_map/ppermute | solution.py:12
  79.3 2.9 %collective-permute-done = bf16[256,256]{1,0:T(8,128)(2,1)S(1)} collective-permute-done((bf16[256,256]{1,0:T(8,128)(2,1)}, bf16[256,256]{1,0:T(8,128)(2,1)S(1)}, u32[]{:S(2)}, u32[]{:S(2)}) %collective-permute-start) | collective-permute-done | bytes 131104 | tf_op jit(solution)/shard_map/ppermute | solution.py:12
  82.2 0.0 copy-done.5
  82.2 0.0 copy-done.6
  82.3 0.7 subtract_convert_fusion.1
  83.0 0.0 all-gather.6.cloned.1.call-update
  83.0 0.0 reduce-scatter.6.cloned.1.call-start
  83.0 24.5 %all-gather.6.cloned.1.call-done = bf16[2048,256]{1,0:T(8,128)(2,1)} async-done(((bf16[256,256]{1,0:T(8,128)(2,1)}), bf16[2048,256]{1,0:T(8,128)(2,1)}) %all-gather.6.cloned.1.call-update) | async-done | bytes 1048592 | tf_op jit(solution)/shard_map/all_gather | solution.py:65
  107.5 0.0 copy-done.1
  107.5 1.3 multiply_convert_fusion.1
  108.8 0.0 reduce-scatter.6.cloned.1.call-update
  108.8 0.0 all-gather.8.cloned.1.call-start
  108.9 37.7 %reduce-scatter.6.cloned.1.call-done = bf16[256,256]{1,0:T(8,128)(2,1)} async-done(((bf16[2048,256]{1,0:T(8,128)(2,1)}), bf16[256,256]{1,0:T(8,128)(2,1)}) %reduce-scatter.6.cloned.1.call-update) | async-done | bytes 131088 | tf_op jit(solution)/shard_map/reduce_scatter | solution.py:73
  146.6 3.4 %collective-permute-start.1 = (bf16[256,256]{1,0:T(8,128)(2,1)}, bf16[256,256]{1,0:T(8,128)(2,1)S(1)}, u32[]{:S(2)}, u32[]{:S(2)}) collective-permute-start(bf16[256,256]{1,0:T(8,128)(2,1)} %reduce-scatter.6.cloned.1.call-done), channel_id=1, source_target_pairs={{0,8},{8,16},{16,24},{1,9},{9,17},{17,25},{2,10},{10,18},{18,26},{... | collective-permute-start | bytes 393224 | tf_op jit(solution)/shard_map/ppermute | solution.py:12
  150.0 2.9 %collective-permute-done.1 = bf16[256,256]{1,0:T(8,128)(2,1)S(1)} collective-permute-done((bf16[256,256]{1,0:T(8,128)(2,1)}, bf16[256,256]{1,0:T(8,128)(2,1)S(1)}, u32[]{:S(2)}, u32[]{:S(2)}) %collective-permute-start.1) | collective-permute-done | bytes 131104 | tf_op jit(solution)/shard_map/ppermute | solution.py:12
  152.9 0.7 subtract_convert_fusion
  153.6 0.0 all-gather.8.cloned.1.call-update
  153.7 0.0 reduce-scatter.8.cloned.1.call-start
  153.7 24.5 %all-gather.8.cloned.1.call-done = bf16[2048,256]{1,0:T(8,128)(2,1)} async-done(((bf16[256,256]{1,0:T(8,128)(2,1)}), bf16[2048,256]{1,0:T(8,128)(2,1)}) %all-gather.8.cloned.1.call-update) | async-done | bytes 1048592 | tf_op jit(solution)/shard_map/all_gather | solution.py:65
  178.2 0.0 copy-start.2
  178.2 1.3 multiply_convert_fusion
  179.5 0.0 reduce-scatter.8.cloned.1.call-update
  179.5 0.0 copy-done
  179.5 0.0 copy-done.2
  179.5 0.0 copy-start.3
  179.5 0.5 convolution_bitcast_fusion.2
  180.0 0.7 copy-done.3
  180.7 0.0 copy-start.4
  180.7 0.5 convolution_bitcast_fusion.1
  181.2 0.7 copy-done.4
  182.0 0.5 convolution_bitcast_fusion
  182.5 0.1 pad_maximum_fusion
  182.5 0.0 copy-start.7
  182.5 0.0 copy-start.8
  182.5 1.1 copy.10
  183.7 33.6 %reduce-scatter.8.cloned.1.call-done = bf16[256,256]{1,0:T(8,128)(2,1)} async-done(((bf16[2048,256]{1,0:T(8,128)(2,1)}), bf16[256,256]{1,0:T(8,128)(2,1)}) %reduce-scatter.8.cloned.1.call-update) | async-done | bytes 131088 | tf_op jit(solution)/shard_map/reduce_scatter | solution.py:73
  217.3 0.0 copy-done.7
  217.3 0.0 copy-done.8
  217.3 1.8 maximum_convert_fusion
  (6 shorter events, 0.1 us)
Async XLA Ops:
  7.2 172.3 %copy-start = (bf16[1,256,2048]{2,1,0:T(8,128)(2,1)S(1)}, bf16[1,256,2048]{2,1,0:T(8,128)(2,1)}, u32[]{:S(2)}) copy-start(bf16[1,256,2048]{2,1,0:T(8,128)(2,1)} %param.17) | copy-start | bytes 3145732
  7.2 29.5 %all-gather.4.cloned.1.call-start = ((), (), s32[]{:S(2)}) async-start(), calls=%async_computation.3 | async-start | bytes 1179648 | tf_op jit(solution)/shard_map/all_gather | solution.py:65
  9.0 66.9 %reduce-scatter.4.cloned.1.call-start = ((), (), s32[]{:S(2)}) async-start(), calls=%async_computation.4 | async-start | bytes 1179648 | tf_op jit(solution)/shard_map/reduce_scatter | solution.py:73
  36.7 45.5 %copy-start.5 = (f32[256,512]{1,0:T(8,128)S(1)}, f32[256,512]{1,0:T(8,128)}, u32[]{:S(2)}) copy-start(f32[256,512]{1,0:T(8,128)} %param.16) | copy-start | bytes 1572868
  36.7 45.5 %copy-start.6 = (bf16[256,768]{1,0:T(8,128)(2,1)S(1)}, bf16[256,768]{1,0:T(8,128)(2,1)}, u32[]{:S(2)}) copy-start(bf16[256,768]{1,0:T(8,128)(2,1)} %param.14) | copy-start | bytes 1179652
  38.0 69.5 %copy-start.1 = (bf16[1,1,128,2048]{3,2,1,0:T(8,128)(2,1)S(1)}, bf16[1,1,128,2048]{3,2,1,0:T(8,128)(2,1)}, u32[]{:S(2)}) copy-start(bf16[1,1,128,2048]{3,2,1,0:T(8,128)(2,1)} %param.18) | copy-start | bytes 1572868
  38.0 69.5 %all-gather.6.cloned.1.call-start = ((), (), s32[]{:S(2)}) async-start(), calls=%async_computation.5 | async-start | bytes 1179648 | tf_op jit(solution)/shard_map/all_gather | solution.py:65
  75.9 6.3 %collective-permute-start = (bf16[256,256]{1,0:T(8,128)(2,1)}, bf16[256,256]{1,0:T(8,128)(2,1)S(1)}, u32[]{:S(2)}, u32[]{:S(2)}) collective-permute-start(bf16[256,256]{1,0:T(8,128)(2,1)} %reduce-scatter.4.cloned.1.call-done), channel_id=1, source_target_pairs={{0,8},{8,16},{16,24},{1,9},{9,17},{17,25},{2,10},{10,18},{18,26},{... | collective-permute-start | bytes 393224 | tf_op jit(solution)/shard_map/ppermute | solution.py:12
  83.0 63.6 %reduce-scatter.6.cloned.1.call-start = ((), (), s32[]{:S(2)}) async-start(), calls=%async_computation.6 | async-start | bytes 1179648 | tf_op jit(solution)/shard_map/reduce_scatter | solution.py:73
  108.8 69.3 %all-gather.8.cloned.1.call-start = ((), (), s32[]{:S(2)}) async-start(), calls=%async_computation.7 | async-start | bytes 1179648 | tf_op jit(solution)/shard_map/all_gather | solution.py:65
  146.6 6.3 %collective-permute-start.1 = (bf16[256,256]{1,0:T(8,128)(2,1)}, bf16[256,256]{1,0:T(8,128)(2,1)S(1)}, u32[]{:S(2)}, u32[]{:S(2)}) collective-permute-start(bf16[256,256]{1,0:T(8,128)(2,1)} %reduce-scatter.6.cloned.1.call-done), channel_id=1, source_target_pairs={{0,8},{8,16},{16,24},{1,9},{9,17},{17,25},{2,10},{10,18},{18,26},{... | collective-permute-start | bytes 393224 | tf_op jit(solution)/shard_map/ppermute | solution.py:12
  153.7 63.6 %reduce-scatter.8.cloned.1.call-start = ((), (), s32[]{:S(2)}) async-start(), calls=%async_computation.8 | async-start | bytes 1179648 | tf_op jit(solution)/shard_map/reduce_scatter | solution.py:73
  178.2 1.3 copy-start.2
  179.5 1.2 copy-start.3
  180.7 1.2 copy-start.4
  182.5 34.8 %copy-start.7 = (bf16[256,256]{1,0:T(8,128)(2,1)S(1)}, bf16[256,256]{1,0:T(8,128)(2,1)}, u32[]{:S(2)}) copy-start(bf16[256,256]{1,0:T(8,128)(2,1)} %reduce-scatter.4.cloned.1.call-done) | copy-start | bytes 393220
  182.5 34.7 %copy-start.8 = (bf16[256,256]{1,0:T(8,128)(2,1)S(1)}, bf16[256,256]{1,0:T(8,128)(2,1)}, u32[]{:S(2)}) copy-start(bf16[256,256]{1,0:T(8,128)(2,1)} %reduce-scatter.6.cloned.1.call-done) | copy-start | bytes 393220
Sparse Core Ops, SparseCore 0:
  10.5 26.1 all-gather.3
  39.9 36.0 reduce-scatter.3
  83.1 24.3 all-gather.5
  110.5 36.0 reduce-scatter.5
  153.8 24.3 all-gather.7
  181.2 36.0 reduce-scatter.7
where the time goes:
time: 226 us
  waiting for transfers between devices  188 us (83%)
  between operations  16.2 us (7%)
  other arithmetic  10.8 us (5%)
  starting transfers between devices  7.02 us (3%)
  local copies, waits for them, and re-layouts  2.68 us (1%)
    reduce_scatter x3, waiting for transfers between devices, body(): lax.psum_scatter(partial_value.astype(jnp.bfloat16), 'rows', scatter_dime...  109 us
    all_gather x3, waiting for transfers between devices, body(): portion = lax.all_gather(head_rows, 'rows', axis=0, tiled=True)  72.7 us
    ppermute x2, starting transfers between devices, shifted(): return lax.ppermute(block, axis, route)  6.77 us
    ppermute x2, waiting for transfers between devices, shifted(): return lax.ppermute(block, axis, route)  5.83 us
  transfers between devices with their start and end apart: 8, of which 8 were waited for; matrix products, arithmetic and copies ran while one was open for 2% of the time, Pallas kernels for 0%

commit v1 on v0

v1 whole, which is shorter than its diff:
```python
import functools

import jax
import jax.numpy as jnp
from jax import lax
from jax.experimental import pallas as pl
from jax.experimental.pallas import tpu as pltpu
from jax.sharding import PartitionSpec as P

PW = 256
NOTE = 16
CORES = 2
WIDE = jnp.float32
NARROW = jnp.bfloat16


def partner(chip, offset, chips):
    if chips & (chips - 1) == 0:
        return chip ^ offset
    return (chip + offset) % chips


def multiply(matrix, vector):
    return jnp.dot(matrix, vector, preferred_element_type=WIDE)


def hop(block, offset_of, step, ends):
    chips, chain = ends
    route = []
    for stage in range(chain - step):
        for chip in range(chips):
            for core in range(CORES):
                goal = partner(chip, offset_of(core), chips)
                source = (stage * chips + chip) * CORES + core
                target = ((stage + step) * chips + goal) * CORES + core
                route.append((source, target))
    return lax.ppermute(block, ("chain", "rows"), route)


def swap(block, rows):
    return lax.ppermute(block, "rows", [(i, i ^ 1) for i in range(rows)])


def place():
    me = lax.axis_index("rows")
    return me, lax.div(me, CORES), lax.rem(me, CORES)


def source_row(index, chips):
    _, chip, core = place()
    offset, side = divmod(index, CORES)
    other = partner(chip, (chips - offset) % chips if chips & (chips - 1) else offset, chips)
    return other * CORES + (core if side == 0 else 1 - core)


def lay_out(whole, columns, pieces, chips):
    height = pieces[0].shape[0]
    for index, piece in enumerate(pieces):
        row = source_row(index, chips)
        whole[pl.ds(pl.multiple_of(row * height, height), height), columns] = piece[...]


def is_live(order, count, slot):
    found = jnp.int32(0)
    for k in range(order.shape[1]):
        hit = jnp.logical_and(order[0, k] == slot, k < count[0])
        found = jnp.where(hit, jnp.int32(1), found)
    return found


def write_tiles(out, products, targets, order, count, slots, tile):
    me, _, core = place()
    for side in range(CORES):
        row = me if side == 0 else me + 1 - 2 * core
        for slot in range(slots):
            base = (side * slots + slot) * (tile + NOTE)
            live = is_live(order, count, row * slots + slot)
            product = products[(side * slots + slot) * tile : (side * slots + slot + 1) * tile]
            out[base : base + tile] = jnp.where(live > 0, product, 0.0).astype(NARROW)
            note = jnp.full((NOTE, PW), targets[side][0, slot], jnp.int32)
            out[base + tile : base + tile + NOTE] = note.astype(WIDE).astype(NARROW)


def read_targets(sent, tile):
    found = []
    for index in range(sent.shape[0] // (tile + NOTE)):
        base = index * (tile + NOTE) + tile
        note = sent[base : base + NOTE, 0:128].astype(WIDE).astype(jnp.int32)
        found.append(note[0, 0])
    return found


def read_tiles(sent, tile):
    count = sent.shape[0] // (tile + NOTE)
    return jnp.concatenate(
        [sent[i * (tile + NOTE) : i * (tile + NOTE) + tile] for i in range(count)], axis=0
    )


def spread(matrices, sent, tile):
    targets = read_targets(sent, tile)
    picked = [
        jnp.concatenate(
            [m[:, pl.ds(pl.multiple_of(t * tile, tile), tile)] for t in targets], axis=1
        )
        for m in matrices
    ]
    return multiply(jnp.concatenate(picked, axis=0), read_tiles(sent, tile))


def first_kernel(chips, slots, tile, *refs):
    own, mate, own_target, mate_target, order, count = refs[:6]
    pieces, out, whole = refs[6:-2], refs[-2], refs[-1]
    lay_out(whole, slice(0, PW), pieces, chips)
    tiles = jnp.concatenate([own[...], mate[...]], axis=0)
    products = multiply(tiles, whole[...])
    write_tiles(out, products, (own_target, mate_target), order, count, slots, tile)


def ahead_kernel(chips, *refs):
    own, mate = refs[:2]
    pieces, out, whole = refs[2:-2], refs[-2], refs[-1]
    lay_out(whole, slice(0, whole.shape[1]), pieces, chips)
    tiles = jnp.concatenate([own[...], mate[...]], axis=0)
    out[...] = multiply(tiles, whole[...])


def next_kernel(tick, slots, tile, *refs):
    own, mate, own_target, mate_target, order, count, ahead = refs[:7]
    sent, out = refs[7:-1], refs[-1]
    products = ahead[:, (tick - 1) * PW : tick * PW]
    for one in sent:
        products = products - spread((own, mate), one, tile)
    write_tiles(out, products, (own_target, mate_target), order, count, slots, tile)


def solve_kernel(chips, tile, ticks, *refs):
    inverse = refs[0]
    parts = CORES * chips
    first, later = refs[1 : 1 + parts], refs[1 + parts : 1 + 2 * parts]
    sent, out, whole = refs[1 + 2 * parts : -2], refs[-2], refs[-1]
    lay_out(whole, slice(0, PW), first, chips)
    lay_out(whole, slice(PW, ticks * PW), later, chips)
    for tick in range(ticks):
        columns = slice(tick * PW, (tick + 1) * PW)
        solved = multiply(inverse[...], whole[:, columns])
        if tick:
            for one in sent[(tick - 1) * chips : tick * chips]:
                solved = solved - spread((inverse,), one, tile)
        out[:, columns] = solved


def update_kernel(chips, tile, ticks, *refs):
    sent, out = refs[:-1], refs[-1]
    height = out.shape[0]
    me, _, _ = place()
    out[...] = jnp.zeros(out.shape, out.dtype)
    for tick in range(ticks):
        columns = slice(tick * PW, (tick + 1) * PW)
        for one in sent[tick * chips : (tick + 1) * chips]:
            for index, target in enumerate(read_targets(one, tile)):
                base = index * (tile + NOTE)
                if height >= tile:
                    held = height // tile
                    spot = target - me * held

                    @pl.when(jnp.logical_and(spot >= 0, spot < held))
                    def _(one=one, base=base, spot=spot, columns=columns):
                        rows = pl.ds(pl.multiple_of(spot * tile, tile), tile)
                        out[rows, columns] += one[base : base + tile].astype(WIDE)

                else:
                    shares = tile // height
                    start = base + lax.rem(me, shares) * height

                    @pl.when(target == lax.div(me, shares))
                    def _(one=one, start=start, columns=columns):
                        rows = pl.ds(pl.multiple_of(start, NOTE), height)
                        out[:, columns] += one[rows].astype(WIDE)


def call(kernel, out_shape, args, scratch=(), flops=0):
    in_specs = [
        pl.BlockSpec(memory_space=pltpu.SMEM if a.dtype == jnp.int32 else pltpu.VMEM)
        for a in args
    ]
    moved = sum(a.size * a.dtype.itemsize for a in args)
    return pl.pallas_call(
        kernel,
        out_shape=out_shape,
        in_specs=in_specs,
        out_specs=pl.BlockSpec(memory_space=pltpu.VMEM),
        scratch_shapes=list(scratch),
        compiler_params=pltpu.CompilerParams(vmem_limit_bytes=40 * 1024 * 1024),
        cost_estimate=pl.CostEstimate(flops=flops, bytes_accessed=moved, transcendentals=0),
    )(*args)


def body(
    right_side,
    entering,
    first_updates,
    diag_inverse,
    tile_blocks,
    target_row_blocks,
    tile_usage_order,
    live_tile_count,
):
    rows, chain = lax.axis_size("rows"), lax.axis_size("chain")
    chips = rows // CORES
    slots, tile, separator = tile_blocks.shape[1:]
    height = right_side.shape[0]
    ticks = right_side.shape[1] // PW
    is_first = (lax.axis_index("chain") == 0).astype(WIDE)
    inverse = diag_inverse[0]
    own = tile_blocks[0].reshape(slots * tile, separator)
    ends = (chips, chain)

    def gather(block):
        pieces = [block, swap(block, rows)]
        for offset in range(1, chips):
            came = hop(block, lambda core, offset=offset: offset, 0, ends)
            pieces += [came, swap(came, rows)]
        return pieces

    def pass_on(block):
        half, found = chips // 2, []
        for i in range(half):
            came = hop(block, lambda core, i=i: core * half + i, 1, ends)
            found += [came, swap(came, rows)]
        return found

    def share(block):
        found = [block]
        offset = 1
        while offset < chips:
            if offset + 1 < chips:
                came = hop(block, lambda core, offset=offset: offset + core, 0, ends)
                found += [came, swap(came, rows)]
                offset += 2
            else:
                found.append(hop(block, lambda core, offset=offset: offset, 0, ends))
                offset += 1
        return found

    mate = swap(own, rows)
    mate_target = swap(target_row_blocks, rows)
    lists = (target_row_blocks, mate_target, tile_usage_order, live_tile_count)
    head = (right_side[:, :PW].astype(WIDE) - entering).astype(NARROW)
    later = (right_side[:, PW:].astype(WIDE) - is_first * first_updates).astype(NARROW)
    heads = gather(head)
    laters = gather(later)
    block_shape = jax.ShapeDtypeStruct((CORES * slots * (tile + NOTE), PW), NARROW)
    tile_rows = CORES * slots * tile
    work = 2 * tile_rows * separator * PW
    product = call(
        functools.partial(first_kernel, chips, slots, tile),
        block_shape,
        (own, mate, *lists, *heads),
        [pltpu.VMEM((separator, PW), NARROW)],
        work,
    )
    ahead = call(
        functools.partial(ahead_kernel, chips),
        jax.ShapeDtypeStruct((tile_rows, (ticks - 1) * PW), WIDE),
        (own, mate, *laters),
        [pltpu.VMEM((separator, (ticks - 1) * PW), NARROW)],
        work * (ticks - 1),
    )
    shared, came = [], []
    for tick in range(ticks):
        shared += share(product)
        if tick + 1 < ticks:
            sent = pass_on(product)
            came += sent
            product = call(
                functools.partial(next_kernel, tick + 1, slots, tile),
                block_shape,
                (own, mate, *lists, ahead, *sent),
                (),
                work // 2,
            )
    out_shape = jax.ShapeDtypeStruct((height, ticks * PW), WIDE)
    solved = call(
        functools.partial(solve_kernel, chips, tile, ticks),
        out_shape,
        (inverse, *heads, *laters, *came),
        [pltpu.VMEM((separator, ticks * PW), NARROW)],
        2 * height * separator * ticks * PW,
    )
    passed = call(
        functools.partial(update_kernel, chips, tile, ticks),
        out_shape,
        tuple(shared),
        (),
        height * ticks * PW,
    )
    return solved, passed


def solution(mesh):
    placed = (
        P(("chain", "rows"), None),
        P(("chain", "rows"), None),
        P("rows", None),
        P("chain", "rows", None),
        P("chain", "rows", None, None),
        P("chain", "rows"),
        P("chain", None),
        P("chain"),
    )
    return jax.shard_map(
        body,
        mesh=mesh,
        in_specs=placed,
        out_specs=(P(("chain", "rows"), None), P(("chain", "rows"), None)),
        check_vma=False,
    )
```

time: 226 us -> 78.6 us (0.35)
  waiting for transfers between devices: 188 us -> 29.9 us
  starting transfers between devices: 7.02 us -> 34.8 us
  between operations: 16.2 us -> 2.12 us
  Pallas kernels: 0 us -> 9.28 us
  other arithmetic: 10.8 us -> 2.25 us
  local copies, waits for them, and re-layouts: 2.68 us -> 0.02 us
    reduce_scatter x3 -> x0, waiting for transfers between devices: 109 us -> none  [body(): lax.psum_scatter(partial_value.astype(jnp.bfloat16), 'rows', scatter_dime...]
    all_gather x3 -> x0, waiting for transfers between devices: 72.7 us -> none  [body(): portion = lax.all_gather(head_rows, 'rows', axis=0, tiled=True)]
    ppermute x2 -> x33, starting transfers between devices: 6.77 us -> 34.8 us  [the longest x16 32.1 us: hop(): return lax.ppermute(block, ('chain', 'rows'), route)]
    ppermute x2 -> x33, waiting for transfers between devices: 5.83 us -> 29.9 us  [the longest x16 28 us: hop(): return lax.ppermute(block, ('chain', 'rows'), route)]
    pallas_call x0 -> x6, Pallas kernels: none -> 9.28 us  [call(): pl.pallas_call(kernel, out_shape=out_shape, in_specs=in_specs, out_specs=...]
    convert_element_type x6 -> x2, other arithmetic: 6.96 us -> 2.25 us  [the longest x1 1.18 us: body(): (right_side[:, PW:].astype(WIDE) - is_first * first_updates).astype(NARROW)]
    unnamed x19 -> x6, local copies, waits for them, and re-layouts: 2.66 us -> 0.02 us
  transfers between devices with their start and end apart: 8 -> 33, of which waited for: 8 -> 13; matrix products, arithmetic and copies ran while one was open for 2% -> 2% of each run, Pallas kernels for 0% -> 8%
where the time goes in v1:
time: 78.6 us; the launch traced here: 78.3 us
  starting transfers between devices  34.8 us (44%)
  waiting for transfers between devices  29.9 us (38%)
  Pallas kernels  9.28 us (12%)
  other arithmetic  2.25 us (3%)
  between operations  2.12 us (3%)
    ppermute x16, starting transfers between devices, hop(): return lax.ppermute(block, ('chain', 'rows'), route)  32.1 us
    ppermute x16, waiting for transfers between devices, hop(): return lax.ppermute(block, ('chain', 'rows'), route)  28 us
    pallas_call x6, Pallas kernels, call(): pl.pallas_call(kernel, out_shape=out_shape, in_specs=in_specs, out_specs=...  9.28 us
    ppermute x17, starting transfers between devices, swap(): return lax.ppermute(block, 'rows', [(i, i ^ 1) for i in range(rows)])  2.62 us
    ppermute x17, waiting for transfers between devices, swap(): return lax.ppermute(block, 'rows', [(i, i ^ 1) for i in range(rows)])  1.92 us
  transfers between devices with their start and end apart: 33, of which 13 were waited for; matrix products, arithmetic and copies ran while one was open for 2% of the time, Pallas kernels for 8%

profile of v1, /device:TPU:0, one launch (start us, length us, event | category | flops | bytes accessed | tf_op | source)
XLA Modules:
  0.0 78.3 jit_solution(7101395519251219357)
XLA Ops:
  0.6 1.1 %subtract_convert_fusion.1.refs_6_.refs_1_ = bf16[256,256]{1,0:T(8,128)(2,1)S(1)} fusion(f32[256,256]{1,0:T(8,128)} %param.9, bf16[256,768]{1,0:T(8,128)(2,1)} %param.8), kind=kLoop, calls=%fused_computation.1 | loop fusion | flops 196608 | bytes 524288 | tf_op jit(solution)/shard_map/convert_element_type | solution.py:249
  1.7 3.0 %collective-permute-start.1 = (bf16[256,256]{1,0:T(8,128)(2,1)S(1)}, bf16[256,256]{1,0:T(8,128)(2,1)S(1)}, u32[]{:S(2)}, u32[]{:S(2)}) collective-permute-start(bf16[256,256]{1,0:T(8,128)(2,1)S(1)} %subtract_convert_fusion.1.refs_6_.refs_1_), channel_id=1, source_target_pairs={{0,2},{1,3},{2,0},{3,1},{4,6},{5,7},{6,4},{7,5},{8,10},{9,11},{10,... | collective-permute-start | bytes 393224 | tf_op jit(solution)/shard_map/ppermute | solution.py:37
  4.7 1.5 %collective-permute-start.3 = (bf16[256,256]{1,0:T(8,128)(2,1)S(1)}, bf16[256,256]{1,0:T(8,128)(2,1)S(1)}, u32[]{:S(2)}, u32[]{:S(2)}) collective-permute-start(bf16[256,256]{1,0:T(8,128)(2,1)S(1)} %subtract_convert_fusion.1.refs_6_.refs_1_), channel_id=1, source_target_pairs={{0,4},{1,5},{2,6},{3,7},{4,0},{5,1},{6,2},{7,3},{8,12},{9,13},{10,... | collective-permute-start | bytes 393224 | tf_op jit(solution)/shard_map/ppermute | solution.py:37
  6.2 0.0 collective-permute-start.5
  6.3 0.0 collective-permute-start.14
  6.3 0.5 collective-permute-start.15
  6.8 1.4 %collective-permute-done.15.refs_3_ = s32[1,1]{1,0:T(1,128)} collective-permute-done((s32[1,1]{1,0:T(1,128)}, s32[1,1]{1,0:T(1,128)}, u32[]{:S(2)}, u32[]{:S(2)}) %collective-permute-start.15) | collective-permute-done | bytes 36 | tf_op jit(solution)/shard_map/ppermute | solution.py:41
  8.2 0.2 collective-permute-start
  8.4 0.2 collective-permute-done.1.refs_8_.refs_3_
  8.6 0.1 collective-permute-start.2
  8.7 3.8 %collective-permute-done.3.refs_10_.refs_5_ = bf16[256,256]{1,0:T(8,128)(2,1)S(1)} collective-permute-done((bf16[256,256]{1,0:T(8,128)(2,1)S(1)}, bf16[256,256]{1,0:T(8,128)(2,1)S(1)}, u32[]{:S(2)}, u32[]{:S(2)}) %collective-permute-start.3) | collective-permute-done | bytes 131104 | tf_op jit(solution)/shard_map/ppermute | solution.py:37
  12.5 0.0 collective-permute-start.4
  12.5 0.5 collective-permute-start.6
  13.0 1.2 %subtract_convert_fusion.refs_2_.refs_9_ = bf16[256,512]{1,0:T(8,128)(2,1)S(1)} fusion(f32[256,512]{1,0:T(8,128)} %param.10, f32[]{:T(128)S(6)} %convert_element_type.18, bf16[256,768]{1,0:T(8,128)(2,1)} %param.8), kind=kLoop, calls=%fused_computation | loop fusion | flops 524288 | bytes 1048580 | tf_op jit(solution)/shard_map/convert_element_type | solution.py:250
  14.2 0.0 collective-permute-done.refs_7_.refs_2_
  14.2 0.8 collective-permute-start.8
  15.0 1.3 %collective-permute-start.10 = (bf16[256,512]{1,0:T(8,128)(2,1)S(1)}, bf16[256,512]{1,0:T(8,128)(2,1)S(1)}, u32[]{:S(2)}, u32[]{:S(2)}) collective-permute-start(bf16[256,512]{1,0:T(8,128)(2,1)S(1)} %subtract_convert_fusion.refs_2_.refs_9_), channel_id=1, source_target_pairs={{0,4},{1,5},{2,6},{3,7},{4,0},{5,1},{6,2},{7,3},{8,12},{9,13},{10,... | collective-permute-start | bytes 786440 | tf_op jit(solution)/shard_map/ppermute | solution.py:37
  16.3 1.4 %collective-permute-start.12 = (bf16[256,512]{1,0:T(8,128)(2,1)S(1)}, bf16[256,512]{1,0:T(8,128)(2,1)S(1)}, u32[]{:S(2)}, u32[]{:S(2)}) collective-permute-start(bf16[256,512]{1,0:T(8,128)(2,1)S(1)} %subtract_convert_fusion.refs_2_.refs_9_), channel_id=1, source_target_pairs={{0,6},{1,7},{2,4},{3,5},{4,2},{5,3},{6,0},{7,1},{8,14},{9,15},{10,... | collective-permute-start | bytes 786440 | tf_op jit(solution)/shard_map/ppermute | solution.py:37
  17.8 0.0 collective-permute-done.6.refs_13_.refs_8_
  18.4 0.0 copy-start.2
  19.1 4.3 %collective-permute-done.8.refs_4_.refs_11_ = bf16[256,512]{1,0:T(8,128)(2,1)S(1)} collective-permute-done((bf16[256,512]{1,0:T(8,128)(2,1)S(1)}, bf16[256,512]{1,0:T(8,128)(2,1)S(1)}, u32[]{:S(2)}, u32[]{:S(2)}) %collective-permute-start.8) | collective-permute-done | bytes 262176 | tf_op jit(solution)/shard_map/ppermute | solution.py:37
  23.4 0.0 collective-permute-start.9
  23.4 4.0 %collective-permute-done.10.refs_6_.refs_13_ = bf16[256,512]{1,0:T(8,128)(2,1)S(1)} collective-permute-done((bf16[256,512]{1,0:T(8,128)(2,1)S(1)}, bf16[256,512]{1,0:T(8,128)(2,1)S(1)}, u32[]{:S(2)}, u32[]{:S(2)}) %collective-permute-start.10) | collective-permute-done | bytes 262176 | tf_op jit(solution)/shard_map/ppermute | solution.py:37
  27.4 0.0 collective-permute-start.11
  27.4 1.6 %collective-permute-done.12.refs_8_.refs_15_ = bf16[256,512]{1,0:T(8,128)(2,1)S(1)} collective-permute-done((bf16[256,512]{1,0:T(8,128)(2,1)S(1)}, bf16[256,512]{1,0:T(8,128)(2,1)S(1)}, u32[]{:S(2)}, u32[]{:S(2)}) %collective-permute-start.12) | collective-permute-done | bytes 262176 | tf_op jit(solution)/shard_map/ppermute | solution.py:37
  29.0 0.0 collective-permute-done.14.refs_1_
  29.1 1.6 %shard_map.95.refs_0_ = bf16[288,256]{1,0:T(8,128)(2,1)S(1)} custom-call(bf16[128,2048]{1,0:T(8,128)(2,1)S(1)} %bitcast.3, bf16[128,2048]{1,0:T(8,128)(2,1)S(1)} %collective-permute-done.14.refs_1_, s32[1,1]{1,0:T(1,128)S(6)} %copy.10.refs_2_, s32[1,1]{1,0:T(1,128)} %collective-permute-done.15.refs_3_, s32[1,8]{1,0:T(1,128)S(1)} %copy-done.2, ...), custom_call_target="tpu_custom_call" | custom-call | flops 268435456 | bytes 2097196 | tf_op jit(solution)/shard_map/pallas_call | solution.py:188
  30.7 3.5 %collective-permute-start.16 = (bf16[288,256]{1,0:T(8,128)(2,1)S(1)}, bf16[288,256]{1,0:T(8,128)(2,1)S(1)}, u32[]{:S(2)}, u32[]{:S(2)}) collective-permute-start(bf16[288,256]{1,0:T(8,128)(2,1)S(1)} %shard_map.95.refs_0_), channel_id=1, source_target_pairs={{0,8},{1,13},{2,10},{3,15},{4,12},{5,9},{6,14},{7,11},{8,16},{9,21... | collective-permute-start | bytes 442376 | tf_op jit(solution)/shard_map/ppermute | solution.py:37
  34.2 0.0 collective-permute-done.7.refs_3_.refs_10_
  34.2 4.2 %collective-permute-start.18 = (bf16[288,256]{1,0:T(8,128)(2,1)S(1)}, bf16[288,256]{1,0:T(8,128)(2,1)S(1)}, u32[]{:S(2)}, u32[]{:S(2)}) collective-permute-start(bf16[288,256]{1,0:T(8,128)(2,1)S(1)} %shard_map.95.refs_0_), channel_id=1, source_target_pairs={{0,10},{1,15},{2,8},{3,13},{4,14},{5,11},{6,12},{7,9},{8,18},{9,23... | collective-permute-start | bytes 442376 | tf_op jit(solution)/shard_map/ppermute | solution.py:37
  38.4 0.0 collective-permute-done.16.refs_7_.refs_17_
  38.4 0.4 collective-permute-start.17
  38.9 3.4 %collective-permute-done.18.refs_9_.refs_19_ = bf16[288,256]{1,0:T(8,128)(2,1)S(1)} collective-permute-done((bf16[288,256]{1,0:T(8,128)(2,1)S(1)}, bf16[288,256]{1,0:T(8,128)(2,1)S(1)}, u32[]{:S(2)}, u32[]{:S(2)}) %collective-permute-start.18) | collective-permute-done | bytes 147488 | tf_op jit(solution)/shard_map/ppermute | solution.py:37
  42.3 0.0 collective-permute-start.19
  42.3 0.0 collective-permute-done.9.refs_5_.refs_12_
  42.3 0.0 collective-permute-done.11.refs_7_.refs_14_
  42.3 0.8 %shard_map.96.refs_6_ = f32[256,512]{1,0:T(8,128)S(1)} custom-call(bf16[128,2048]{1,0:T(8,128)(2,1)S(1)} %bitcast.4, bf16[128,2048]{1,0:T(8,128)(2,1)S(1)} %collective-permute-done.14.refs_1_, bf16[256,512]{1,0:T(8,128)(2,1)S(1)} %subtract_convert_fusion.refs_2_.refs_9_, bf16[256,512]{1,0:T(8,128)(2,1)S(1)} %collective-permute-done.7.refs_3_.refs_10_, ...), custom_call_target="tpu_custom_call" | custom-call | flops 536870912 | bytes 3145728 | tf_op jit(solution)/shard_map/pallas_call | solution.py:188
  43.2 0.0 collective-permute-done.17.refs_8_.refs_18_
  43.2 0.5 collective-permute-done.19.refs_10_.refs_20_
  43.7 1.4 %shard_map.97.refs_4_ = bf16[288,256]{1,0:T(8,128)(2,1)S(1)} custom-call(bf16[128,2048]{1,0:T(8,128)(2,1)S(1)} %bitcast.5, bf16[128,2048]{1,0:T(8,128)(2,1)S(1)} %collective-permute-done.14.refs_1_, s32[1,1]{1,0:T(1,128)S(6)} %copy.10.refs_2_, s32[1,1]{1,0:T(1,128)} %collective-permute-done.15.refs_3_, s32[1,8]{1,0:T(1,128)S(1)} %copy-done.2, ...), custom_call_target="tpu_custom_call" | custom-call | flops 134217728 | bytes 2162732 | tf_op jit(solution)/shard_map/pallas_call | solution.py:188
  45.1 0.0 copy-start.1
  45.1 4.9 %collective-permute-start.20 = (bf16[288,256]{1,0:T(8,128)(2,1)S(1)}, bf16[288,256]{1,0:T(8,128)(2,1)S(1)}, u32[]{:S(2)}, u32[]{:S(2)}) collective-permute-start(bf16[288,256]{1,0:T(8,128)(2,1)S(1)} %shard_map.97.refs_4_), channel_id=1, source_target_pairs={{0,8},{1,13},{2,10},{3,15},{4,12},{5,9},{6,14},{7,11},{8,16},{9,21... | collective-permute-start | bytes 442376 | tf_op jit(solution)/shard_map/ppermute | solution.py:37
  50.0 4.1 %collective-permute-start.22 = (bf16[288,256]{1,0:T(8,128)(2,1)S(1)}, bf16[288,256]{1,0:T(8,128)(2,1)S(1)}, u32[]{:S(2)}, u32[]{:S(2)}) collective-permute-start(bf16[288,256]{1,0:T(8,128)(2,1)S(1)} %shard_map.97.refs_4_), channel_id=1, source_target_pairs={{0,10},{1,15},{2,8},{3,13},{4,14},{5,11},{6,12},{7,9},{8,18},{9,23... | collective-permute-start | bytes 442376 | tf_op jit(solution)/shard_map/ppermute | solution.py:37
  54.1 0.8 collective-permute-start.21
  54.9 3.4 %collective-permute-done.22.refs_23_.refs_9_ = bf16[288,256]{1,0:T(8,128)(2,1)S(1)} collective-permute-done((bf16[288,256]{1,0:T(8,128)(2,1)S(1)}, bf16[288,256]{1,0:T(8,128)(2,1)S(1)}, u32[]{:S(2)}, u32[]{:S(2)}) %collective-permute-start.22) | collective-permute-done | bytes 147488 | tf_op jit(solution)/shard_map/ppermute | solution.py:37
  58.3 0.1 collective-permute-start.23
  58.4 0.5 collective-permute-start.24
  59.0 2.1 %collective-permute-start.26 = (bf16[288,256]{1,0:T(8,128)(2,1)S(1)}, bf16[288,256]{1,0:T(8,128)(2,1)S(1)}, u32[]{:S(2)}, u32[]{:S(2)}) collective-permute-start(bf16[288,256]{1,0:T(8,128)(2,1)S(1)} %shard_map.95.refs_0_), channel_id=1, source_target_pairs={{0,6},{1,7},{2,4},{3,5},{4,2},{5,3},{6,0},{7,1},{8,14},{9,15},{10,... | collective-permute-start | bytes 442376 | tf_op jit(solution)/shard_map/ppermute | solution.py:37
  61.0 0.7 collective-permute-start.27
  61.7 0.0 collective-permute-done.21.refs_22_.refs_8_
  61.8 0.0 collective-permute-done.23.refs_24_.refs_10_
  61.8 1.4 %shard_map.99.refs_8_ = bf16[288,256]{1,0:T(8,128)(2,1)S(1)} custom-call(bf16[128,2048]{1,0:T(8,128)(2,1)S(1)} %bitcast.6, bf16[128,2048]{1,0:T(8,128)(2,1)S(1)} %collective-permute-done.14.refs_1_, s32[1,1]{1,0:T(1,128)S(6)} %copy.10.refs_2_, s32[1,1]{1,0:T(1,128)} %collective-permute-done.15.refs_3_, s32[1,8]{1,0:T(1,128)S(1)} %copy-done.2, ...), custom_call_target="tpu_custom_call" | custom-call | flops 134217728 | bytes 2162732 | tf_op jit(solution)/shard_map/pallas_call | solution.py:188
  63.2 1.4 %collective-permute-start.30 = (bf16[288,256]{1,0:T(8,128)(2,1)S(1)}, bf16[288,256]{1,0:T(8,128)(2,1)S(1)}, u32[]{:S(2)}, u32[]{:S(2)}) collective-permute-start(bf16[288,256]{1,0:T(8,128)(2,1)S(1)} %shard_map.99.refs_8_), channel_id=1, source_target_pairs={{0,2},{1,5},{2,0},{3,7},{4,6},{5,1},{6,4},{7,3},{8,10},{9,13},{10,... | collective-permute-start | bytes 442376 | tf_op jit(solution)/shard_map/ppermute | solution.py:37
  64.6 0.0 collective-permute-done.24.refs_1_
  64.6 1.2 %collective-permute-start.29 = (bf16[288,256]{1,0:T(8,128)(2,1)S(1)}, bf16[288,256]{1,0:T(8,128)(2,1)S(1)}, u32[]{:S(2)}, u32[]{:S(2)}) collective-permute-start(bf16[288,256]{1,0:T(8,128)(2,1)S(1)} %shard_map.97.refs_4_), channel_id=1, source_target_pairs={{0,6},{1,7},{2,4},{3,5},{4,2},{5,3},{6,0},{7,1},{8,14},{9,15},{10,... | collective-permute-start | bytes 442376 | tf_op jit(solution)/shard_map/ppermute | solution.py:37
  65.8 2.7 %collective-permute-done.27.refs_5_ = bf16[288,256]{1,0:T(8,128)(2,1)S(1)} collective-permute-done((bf16[288,256]{1,0:T(8,128)(2,1)S(1)}, bf16[288,256]{1,0:T(8,128)(2,1)S(1)}, u32[]{:S(2)}, u32[]{:S(2)}) %collective-permute-start.27) | collective-permute-done | bytes 147488 | tf_op jit(solution)/shard_map/ppermute | solution.py:37
  68.4 0.0 collective-permute-start.28
  68.4 0.0 collective-permute-done.26.refs_3_
  68.4 1.5 %collective-permute-start.32 = (bf16[288,256]{1,0:T(8,128)(2,1)S(1)}, bf16[288,256]{1,0:T(8,128)(2,1)S(1)}, u32[]{:S(2)}, u32[]{:S(2)}) collective-permute-start(bf16[288,256]{1,0:T(8,128)(2,1)S(1)} %shard_map.99.refs_8_), channel_id=1, source_target_pairs={{0,6},{1,7},{2,4},{3,5},{4,2},{5,3},{6,0},{7,1},{8,14},{9,15},{10,... | collective-permute-start | bytes 442376 | tf_op jit(solution)/shard_map/ppermute | solution.py:37
  69.9 1.6 %collective-permute-done.30.refs_9_ = bf16[288,256]{1,0:T(8,128)(2,1)S(1)} collective-permute-done((bf16[288,256]{1,0:T(8,128)(2,1)S(1)}, bf16[288,256]{1,0:T(8,128)(2,1)S(1)}, u32[]{:S(2)}, u32[]{:S(2)}) %collective-permute-start.30) | collective-permute-done | bytes 147488 | tf_op jit(solution)/shard_map/ppermute | solution.py:37
  71.5 2.4 %shard_map.98 = f32[256,768]{1,0:T(8,128)} custom-call(bf16[256,2048]{1,0:T(8,128)(2,1)S(1)} %bitcast.7, bf16[256,256]{1,0:T(8,128)(2,1)S(1)} %subtract_convert_fusion.1.refs_6_.refs_1_, bf16[256,256]{1,0:T(8,128)(2,1)S(1)} %collective-permute-done.refs_7_.refs_2_, bf16[256,256]{1,0:T(8,128)(2,1)S(1)} %collective-permute-done.1.refs_8_.refs_3_, ...), custom_call_target="tpu_custom_call" | custom-call | flops 805306368 | bytes 5373952 | tf_op jit(solution)/shard_map/pallas_call | solution.py:188
  73.9 0.8 %collective-permute-done.29.refs_7_ = bf16[288,256]{1,0:T(8,128)(2,1)S(1)} collective-permute-done((bf16[288,256]{1,0:T(8,128)(2,1)S(1)}, bf16[288,256]{1,0:T(8,128)(2,1)S(1)}, u32[]{:S(2)}, u32[]{:S(2)}) %collective-permute-start.29) | collective-permute-done | bytes 147488 | tf_op jit(solution)/shard_map/ppermute | solution.py:37
  74.7 2.0 %collective-permute-done.32.refs_11_ = bf16[288,256]{1,0:T(8,128)(2,1)S(1)} collective-permute-done((bf16[288,256]{1,0:T(8,128)(2,1)S(1)}, bf16[288,256]{1,0:T(8,128)(2,1)S(1)}, u32[]{:S(2)}, u32[]{:S(2)}) %collective-permute-start.32) | collective-permute-done | bytes 147488 | tf_op jit(solution)/shard_map/ppermute | solution.py:37
  76.8 1.5 %shard_map.100 = f32[256,768]{1,0:T(8,128)} custom-call(bf16[288,256]{1,0:T(8,128)(2,1)S(1)} %shard_map.95.refs_0_, bf16[288,256]{1,0:T(8,128)(2,1)S(1)} %collective-permute-done.24.refs_1_, bf16[288,256]{1,0:T(8,128)(2,1)S(1)} %collective-permute-done.25.refs_2_, bf16[288,256]{1,0:T(8,128)(2,1)S(1)} %collective-permute-done.26.refs_3_, ...), custom_call_target="tpu_custom_call" | custom-call | flops 196608 | bytes 1769472 | tf_op jit(solution)/shard_map/pallas_call | solution.py:188
  (16 shorter events, 0.0 us)
Async XLA Ops:
  0.6 5.6 %copy-start = (bf16[1,1,128,2048]{3,2,1,0:T(8,128)(2,1)S(1)}, bf16[1,1,128,2048]{3,2,1,0:T(8,128)(2,1)}, u32[]{:S(2)}) copy-start(bf16[1,1,128,2048]{3,2,1,0:T(8,128)(2,1)} %param.12) | copy-start | bytes 1572868
  1.7 6.9 %collective-permute-start.1 = (bf16[256,256]{1,0:T(8,128)(2,1)S(1)}, bf16[256,256]{1,0:T(8,128)(2,1)S(1)}, u32[]{:S(2)}, u32[]{:S(2)}) collective-permute-start(bf16[256,256]{1,0:T(8,128)(2,1)S(1)} %subtract_convert_fusion.1.refs_6_.refs_1_), channel_id=1, source_target_pairs={{0,2},{1,3},{2,0},{3,1},{4,6},{5,7},{6,4},{7,5},{8,10},{9,11},{10,... | collective-permute-start | bytes 393224 | tf_op jit(solution)/shard_map/ppermute | solution.py:37
  4.7 7.8 %collective-permute-start.3 = (bf16[256,256]{1,0:T(8,128)(2,1)S(1)}, bf16[256,256]{1,0:T(8,128)(2,1)S(1)}, u32[]{:S(2)}, u32[]{:S(2)}) collective-permute-start(bf16[256,256]{1,0:T(8,128)(2,1)S(1)} %subtract_convert_fusion.1.refs_6_.refs_1_), channel_id=1, source_target_pairs={{0,4},{1,5},{2,6},{3,7},{4,0},{5,1},{6,2},{7,3},{8,12},{9,13},{10,... | collective-permute-start | bytes 393224 | tf_op jit(solution)/shard_map/ppermute | solution.py:37
  6.2 6.3 %collective-permute-start.5 = (bf16[256,256]{1,0:T(8,128)(2,1)S(1)}, bf16[256,256]{1,0:T(8,128)(2,1)S(1)}, u32[]{:S(2)}, u32[]{:S(2)}) collective-permute-start(bf16[256,256]{1,0:T(8,128)(2,1)S(1)} %subtract_convert_fusion.1.refs_6_.refs_1_), channel_id=1, source_target_pairs={{0,6},{1,7},{2,4},{3,5},{4,2},{5,3},{6,0},{7,1},{8,14},{9,15},{10,... | collective-permute-start | bytes 393224 | tf_op jit(solution)/shard_map/ppermute | solution.py:37
  6.3 22.8 %collective-permute-start.14 = (bf16[128,2048]{1,0:T(8,128)(2,1)S(1)}, bf16[128,2048]{1,0:T(8,128)(2,1)S(1)}, u32[]{:S(2)}, u32[]{:S(2)}) collective-permute-start(bf16[128,2048]{1,0:T(8,128)(2,1)S(1)} %bitcast.2), channel_id=1, source_target_pairs={{0,1},{1,0},{2,3},{3,2},{4,5},{5,4},{6,7},{7,6},{8,9},{9,8},{10,11... | collective-permute-start | bytes 1572872 | tf_op jit(solution)/shard_map/ppermute | solution.py:41
  6.3 1.9 %collective-permute-start.15 = (s32[1,1]{1,0:T(1,128)}, s32[1,1]{1,0:T(1,128)}, u32[]{:S(2)}, u32[]{:S(2)}) collective-permute-start(s32[1,1]{1,0:T(1,128)} %param.13), channel_id=1, source_target_pairs={{0,1},{1,0},{2,3},{3,2},{4,5},{5,4},{6,7},{7,6},{8,9},{9,8},{10,11... | collective-permute-start | bytes 20 | tf_op jit(solution)/shard_map/ppermute | solution.py:41
  8.2 6.0 %collective-permute-start = (bf16[256,256]{1,0:T(8,128)(2,1)S(1)}, bf16[256,256]{1,0:T(8,128)(2,1)S(1)}, u32[]{:S(2)}, u32[]{:S(2)}) collective-permute-start(bf16[256,256]{1,0:T(8,128)(2,1)S(1)} %subtract_convert_fusion.1.refs_6_.refs_1_), channel_id=1, source_target_pairs={{0,1},{1,0},{2,3},{3,2},{4,5},{5,4},{6,7},{7,6},{8,9},{9,8},{10,11... | collective-permute-start | bytes 393224 | tf_op jit(solution)/shard_map/ppermute | solution.py:41
  8.6 6.4 %collective-permute-start.2 = (bf16[256,256]{1,0:T(8,128)(2,1)S(1)}, bf16[256,256]{1,0:T(8,128)(2,1)S(1)}, u32[]{:S(2)}, u32[]{:S(2)}) collective-permute-start(bf16[256,256]{1,0:T(8,128)(2,1)S(1)} %collective-permute-done.1.refs_8_.refs_3_), channel_id=1, source_target_pairs={{0,1},{1,0},{2,3},{3,2},{4,5},{5,4},{6,7},{7,6},{8,9},{9,8},{10,11... | collective-permute-start | bytes 393224 | tf_op jit(solution)/shard_map/ppermute | solution.py:41
  12.5 3.8 %collective-permute-start.4 = (bf16[256,256]{1,0:T(8,128)(2,1)S(1)}, bf16[256,256]{1,0:T(8,128)(2,1)S(1)}, u32[]{:S(2)}, u32[]{:S(2)}) collective-permute-start(bf16[256,256]{1,0:T(8,128)(2,1)S(1)} %collective-permute-done.3.refs_10_.refs_5_), channel_id=1, source_target_pairs={{0,1},{1,0},{2,3},{3,2},{4,5},{5,4},{6,7},{7,6},{8,9},{9,8},{10,11... | collective-permute-start | bytes 393224 | tf_op jit(solution)/shard_map/ppermute | solution.py:41
  12.5 5.3 %collective-permute-start.6 = (bf16[256,256]{1,0:T(8,128)(2,1)S(1)}, bf16[256,256]{1,0:T(8,128)(2,1)S(1)}, u32[]{:S(2)}, u32[]{:S(2)}) collective-permute-start(bf16[256,256]{1,0:T(8,128)(2,1)S(1)} %collective-permute-done.5.refs_12_.refs_7_), channel_id=1, source_target_pairs={{0,1},{1,0},{2,3},{3,2},{4,5},{5,4},{6,7},{7,6},{8,9},{9,8},{10,11... | collective-permute-start | bytes 393224 | tf_op jit(solution)/shard_map/ppermute | solution.py:41
  14.2 9.2 %collective-permute-start.8 = (bf16[256,512]{1,0:T(8,128)(2,1)S(1)}, bf16[256,512]{1,0:T(8,128)(2,1)S(1)}, u32[]{:S(2)}, u32[]{:S(2)}) collective-permute-start(bf16[256,512]{1,0:T(8,128)(2,1)S(1)} %subtract_convert_fusion.refs_2_.refs_9_), channel_id=1, source_target_pairs={{0,2},{1,3},{2,0},{3,1},{4,6},{5,7},{6,4},{7,5},{8,10},{9,11},{10,... | collective-permute-start | bytes 786440 | tf_op jit(solution)/shard_map/ppermute | solution.py:37
  15.0 12.4 %collective-permute-start.10 = (bf16[256,512]{1,0:T(8,128)(2,1)S(1)}, bf16[256,512]{1,0:T(8,128)(2,1)S(1)}, u32[]{:S(2)}, u32[]{:S(2)}) collective-permute-start(bf16[256,512]{1,0:T(8,128)(2,1)S(1)} %subtract_convert_fusion.refs_2_.refs_9_), channel_id=1, source_target_pairs={{0,4},{1,5},{2,6},{3,7},{4,0},{5,1},{6,2},{7,3},{8,12},{9,13},{10,... | collective-permute-start | bytes 786440 | tf_op jit(solution)/shard_map/ppermute | solution.py:37
  16.3 12.7 %collective-permute-start.12 = (bf16[256,512]{1,0:T(8,128)(2,1)S(1)}, bf16[256,512]{1,0:T(8,128)(2,1)S(1)}, u32[]{:S(2)}, u32[]{:S(2)}) collective-permute-start(bf16[256,512]{1,0:T(8,128)(2,1)S(1)} %subtract_convert_fusion.refs_2_.refs_9_), channel_id=1, source_target_pairs={{0,6},{1,7},{2,4},{3,5},{4,2},{5,3},{6,0},{7,1},{8,14},{9,15},{10,... | collective-permute-start | bytes 786440 | tf_op jit(solution)/shard_map/ppermute | solution.py:37
  17.8 16.4 %collective-permute-start.7 = (bf16[256,512]{1,0:T(8,128)(2,1)S(1)}, bf16[256,512]{1,0:T(8,128)(2,1)S(1)}, u32[]{:S(2)}, u32[]{:S(2)}) collective-permute-start(bf16[256,512]{1,0:T(8,128)(2,1)S(1)} %subtract_convert_fusion.refs_2_.refs_9_), channel_id=1, source_target_pairs={{0,1},{1,0},{2,3},{3,2},{4,5},{5,4},{6,7},{7,6},{8,9},{9,8},{10,11... | collective-permute-start | bytes 786440 | tf_op jit(solution)/shard_map/ppermute | solution.py:41
  18.4 10.6 %copy-start.2 = (s32[1,8]{1,0:T(1,128)S(1)}, s32[1,8]{1,0:T(1,128)}, u32[]{:S(2)}) copy-start(s32[1,8]{1,0:T(1,128)} %refs_4_.5) | copy-start | bytes 100
  23.4 18.9 %collective-permute-start.9 = (bf16[256,512]{1,0:T(8,128)(2,1)S(1)}, bf16[256,512]{1,0:T(8,128)(2,1)S(1)}, u32[]{:S(2)}, u32[]{:S(2)}) collective-permute-start(bf16[256,512]{1,0:T(8,128)(2,1)S(1)} %collective-permute-done.8.refs_4_.refs_11_), channel_id=1, source_target_pairs={{0,1},{1,0},{2,3},{3,2},{4,5},{5,4},{6,7},{7,6},{8,9},{9,8},{10,11... | collective-permute-start | bytes 786440 | tf_op jit(solution)/shard_map/ppermute | solution.py:41
  27.4 14.9 %collective-permute-start.11 = (bf16[256,512]{1,0:T(8,128)(2,1)S(1)}, bf16[256,512]{1,0:T(8,128)(2,1)S(1)}, u32[]{:S(2)}, u32[]{:S(2)}) collective-permute-start(bf16[256,512]{1,0:T(8,128)(2,1)S(1)} %collective-permute-done.10.refs_6_.refs_13_), channel_id=1, source_target_pairs={{0,1},{1,0},{2,3},{3,2},{4,5},{5,4},{6,7},{7,6},{8,9},{9,8},{10,11... | collective-permute-start | bytes 786440 | tf_op jit(solution)/shard_map/ppermute | solution.py:41
  29.0 13.3 %collective-permute-start.13 = (bf16[256,512]{1,0:T(8,128)(2,1)S(1)}, bf16[256,512]{1,0:T(8,128)(2,1)S(1)}, u32[]{:S(2)}, u32[]{:S(2)}) collective-permute-start(bf16[256,512]{1,0:T(8,128)(2,1)S(1)} %collective-permute-done.12.refs_8_.refs_15_), channel_id=1, source_target_pairs={{0,1},{1,0},{2,3},{3,2},{4,5},{5,4},{6,7},{7,6},{8,9},{9,8},{10,11... | collective-permute-start | bytes 786440 | tf_op jit(solution)/shard_map/ppermute | solution.py:41
  30.7 7.8 %collective-permute-start.16 = (bf16[288,256]{1,0:T(8,128)(2,1)S(1)}, bf16[288,256]{1,0:T(8,128)(2,1)S(1)}, u32[]{:S(2)}, u32[]{:S(2)}) collective-permute-start(bf16[288,256]{1,0:T(8,128)(2,1)S(1)} %shard_map.95.refs_0_), channel_id=1, source_target_pairs={{0,8},{1,13},{2,10},{3,15},{4,12},{5,9},{6,14},{7,11},{8,16},{9,21... | collective-permute-start | bytes 442376 | tf_op jit(solution)/shard_map/ppermute | solution.py:37
  34.2 8.1 %collective-permute-start.18 = (bf16[288,256]{1,0:T(8,128)(2,1)S(1)}, bf16[288,256]{1,0:T(8,128)(2,1)S(1)}, u32[]{:S(2)}, u32[]{:S(2)}) collective-permute-start(bf16[288,256]{1,0:T(8,128)(2,1)S(1)} %shard_map.95.refs_0_), channel_id=1, source_target_pairs={{0,10},{1,15},{2,8},{3,13},{4,14},{5,11},{6,12},{7,9},{8,18},{9,23... | collective-permute-start | bytes 442376 | tf_op jit(solution)/shard_map/ppermute | solution.py:37
  38.4 4.7 %collective-permute-start.17 = (bf16[288,256]{1,0:T(8,128)(2,1)S(1)}, bf16[288,256]{1,0:T(8,128)(2,1)S(1)}, u32[]{:S(2)}, u32[]{:S(2)}) collective-permute-start(bf16[288,256]{1,0:T(8,128)(2,1)S(1)} %collective-permute-done.16.refs_7_.refs_17_), channel_id=1, source_target_pairs={{0,1},{1,0},{2,3},{3,2},{4,5},{5,4},{6,7},{7,6},{8,9},{9,8},{10,11... | collective-permute-start | bytes 442376 | tf_op jit(solution)/shard_map/ppermute | solution.py:41
  42.3 1.4 %collective-permute-start.19 = (bf16[288,256]{1,0:T(8,128)(2,1)S(1)}, bf16[288,256]{1,0:T(8,128)(2,1)S(1)}, u32[]{:S(2)}, u32[]{:S(2)}) collective-permute-start(bf16[288,256]{1,0:T(8,128)(2,1)S(1)} %collective-permute-done.18.refs_9_.refs_19_), channel_id=1, source_target_pairs={{0,1},{1,0},{2,3},{3,2},{4,5},{5,4},{6,7},{7,6},{8,9},{9,8},{10,11... | collective-permute-start | bytes 442376 | tf_op jit(solution)/shard_map/ppermute | solution.py:41
  45.1 26.4 %copy-start.1 = (bf16[1,256,2048]{2,1,0:T(8,128)(2,1)S(1)}, bf16[1,256,2048]{2,1,0:T(8,128)(2,1)}, u32[]{:S(2)}) copy-start(bf16[1,256,2048]{2,1,0:T(8,128)(2,1)} %param.11) | copy-start | bytes 3145732
  45.1 9.0 %collective-permute-start.20 = (bf16[288,256]{1,0:T(8,128)(2,1)S(1)}, bf16[288,256]{1,0:T(8,128)(2,1)S(1)}, u32[]{:S(2)}, u32[]{:S(2)}) collective-permute-start(bf16[288,256]{1,0:T(8,128)(2,1)S(1)} %shard_map.97.refs_4_), channel_id=1, source_target_pairs={{0,8},{1,13},{2,10},{3,15},{4,12},{5,9},{6,14},{7,11},{8,16},{9,21... | collective-permute-start | bytes 442376 | tf_op jit(solution)/shard_map/ppermute | solution.py:37
  50.0 8.3 %collective-permute-start.22 = (bf16[288,256]{1,0:T(8,128)(2,1)S(1)}, bf16[288,256]{1,0:T(8,128)(2,1)S(1)}, u32[]{:S(2)}, u32[]{:S(2)}) collective-permute-start(bf16[288,256]{1,0:T(8,128)(2,1)S(1)} %shard_map.97.refs_4_), channel_id=1, source_target_pairs={{0,10},{1,15},{2,8},{3,13},{4,14},{5,11},{6,12},{7,9},{8,18},{9,23... | collective-permute-start | bytes 442376 | tf_op jit(solution)/shard_map/ppermute | solution.py:37
  54.1 7.6 %collective-permute-start.21 = (bf16[288,256]{1,0:T(8,128)(2,1)S(1)}, bf16[288,256]{1,0:T(8,128)(2,1)S(1)}, u32[]{:S(2)}, u32[]{:S(2)}) collective-permute-start(bf16[288,256]{1,0:T(8,128)(2,1)S(1)} %collective-permute-done.20.refs_21_.refs_7_), channel_id=1, source_target_pairs={{0,1},{1,0},{2,3},{3,2},{4,5},{5,4},{6,7},{7,6},{8,9},{9,8},{10,11... | collective-permute-start | bytes 442376 | tf_op jit(solution)/shard_map/ppermute | solution.py:41
  58.3 3.4 %collective-permute-start.23 = (bf16[288,256]{1,0:T(8,128)(2,1)S(1)}, bf16[288,256]{1,0:T(8,128)(2,1)S(1)}, u32[]{:S(2)}, u32[]{:S(2)}) collective-permute-start(bf16[288,256]{1,0:T(8,128)(2,1)S(1)} %collective-permute-done.22.refs_23_.refs_9_), channel_id=1, source_target_pairs={{0,1},{1,0},{2,3},{3,2},{4,5},{5,4},{6,7},{7,6},{8,9},{9,8},{10,11... | collective-permute-start | bytes 442376 | tf_op jit(solution)/shard_map/ppermute | solution.py:41
  58.4 6.2 %collective-permute-start.24 = (bf16[288,256]{1,0:T(8,128)(2,1)S(1)}, bf16[288,256]{1,0:T(8,128)(2,1)S(1)}, u32[]{:S(2)}, u32[]{:S(2)}) collective-permute-start(bf16[288,256]{1,0:T(8,128)(2,1)S(1)} %shard_map.95.refs_0_), channel_id=1, source_target_pairs={{0,2},{1,5},{2,0},{3,7},{4,6},{5,1},{6,4},{7,3},{8,10},{9,13},{10,... | collective-permute-start | bytes 442376 | tf_op jit(solution)/shard_map/ppermute | solution.py:37
  59.0 9.5 %collective-permute-start.26 = (bf16[288,256]{1,0:T(8,128)(2,1)S(1)}, bf16[288,256]{1,0:T(8,128)(2,1)S(1)}, u32[]{:S(2)}, u32[]{:S(2)}) collective-permute-start(bf16[288,256]{1,0:T(8,128)(2,1)S(1)} %shard_map.95.refs_0_), channel_id=1, source_target_pairs={{0,6},{1,7},{2,4},{3,5},{4,2},{5,3},{6,0},{7,1},{8,14},{9,15},{10,... | collective-permute-start | bytes 442376 | tf_op jit(solution)/shard_map/ppermute | solution.py:37
  61.0 7.4 %collective-permute-start.27 = (bf16[288,256]{1,0:T(8,128)(2,1)S(1)}, bf16[288,256]{1,0:T(8,128)(2,1)S(1)}, u32[]{:S(2)}, u32[]{:S(2)}) collective-permute-start(bf16[288,256]{1,0:T(8,128)(2,1)S(1)} %shard_map.97.refs_4_), channel_id=1, source_target_pairs={{0,2},{1,5},{2,0},{3,7},{4,6},{5,1},{6,4},{7,3},{8,10},{9,13},{10,... | collective-permute-start | bytes 442376 | tf_op jit(solution)/shard_map/ppermute | solution.py:37
  63.2 8.3 %collective-permute-start.30 = (bf16[288,256]{1,0:T(8,128)(2,1)S(1)}, bf16[288,256]{1,0:T(8,128)(2,1)S(1)}, u32[]{:S(2)}, u32[]{:S(2)}) collective-permute-start(bf16[288,256]{1,0:T(8,128)(2,1)S(1)} %shard_map.99.refs_8_), channel_id=1, source_target_pairs={{0,2},{1,5},{2,0},{3,7},{4,6},{5,1},{6,4},{7,3},{8,10},{9,13},{10,... | collective-permute-start | bytes 442376 | tf_op jit(solution)/shard_map/ppermute | solution.py:37
  64.6 9.3 %collective-permute-start.25 = (bf16[288,256]{1,0:T(8,128)(2,1)S(1)}, bf16[288,256]{1,0:T(8,128)(2,1)S(1)}, u32[]{:S(2)}, u32[]{:S(2)}) collective-permute-start(bf16[288,256]{1,0:T(8,128)(2,1)S(1)} %collective-permute-done.24.refs_1_), channel_id=1, source_target_pairs={{0,1},{1,0},{2,3},{3,2},{4,5},{5,4},{6,7},{7,6},{8,9},{9,8},{10,11... | collective-permute-start | bytes 442376 | tf_op jit(solution)/shard_map/ppermute | solution.py:41
  64.6 10.1 %collective-permute-start.29 = (bf16[288,256]{1,0:T(8,128)(2,1)S(1)}, bf16[288,256]{1,0:T(8,128)(2,1)S(1)}, u32[]{:S(2)}, u32[]{:S(2)}) collective-permute-start(bf16[288,256]{1,0:T(8,128)(2,1)S(1)} %shard_map.97.refs_4_), channel_id=1, source_target_pairs={{0,6},{1,7},{2,4},{3,5},{4,2},{5,3},{6,0},{7,1},{8,14},{9,15},{10,... | collective-permute-start | bytes 442376 | tf_op jit(solution)/shard_map/ppermute | solution.py:37
  68.4 6.3 %collective-permute-start.28 = (bf16[288,256]{1,0:T(8,128)(2,1)S(1)}, bf16[288,256]{1,0:T(8,128)(2,1)S(1)}, u32[]{:S(2)}, u32[]{:S(2)}) collective-permute-start(bf16[288,256]{1,0:T(8,128)(2,1)S(1)} %collective-permute-done.27.refs_5_), channel_id=1, source_target_pairs={{0,1},{1,0},{2,3},{3,2},{4,5},{5,4},{6,7},{7,6},{8,9},{9,8},{10,11... | collective-permute-start | bytes 442376 | tf_op jit(solution)/shard_map/ppermute | solution.py:41
  68.4 8.3 %collective-permute-start.32 = (bf16[288,256]{1,0:T(8,128)(2,1)S(1)}, bf16[288,256]{1,0:T(8,128)(2,1)S(1)}, u32[]{:S(2)}, u32[]{:S(2)}) collective-permute-start(bf16[288,256]{1,0:T(8,128)(2,1)S(1)} %shard_map.99.refs_8_), channel_id=1, source_target_pairs={{0,6},{1,7},{2,4},{3,5},{4,2},{5,3},{6,0},{7,1},{8,14},{9,15},{10,... | collective-permute-start | bytes 442376 | tf_op jit(solution)/shard_map/ppermute | solution.py:37
  71.5 5.3 %collective-permute-start.31 = (bf16[288,256]{1,0:T(8,128)(2,1)S(1)}, bf16[288,256]{1,0:T(8,128)(2,1)S(1)}, u32[]{:S(2)}, u32[]{:S(2)}) collective-permute-start(bf16[288,256]{1,0:T(8,128)(2,1)S(1)} %collective-permute-done.30.refs_9_), channel_id=1, source_target_pairs={{0,1},{1,0},{2,3},{3,2},{4,5},{5,4},{6,7},{7,6},{8,9},{9,8},{10,11... | collective-permute-start | bytes 442376 | tf_op jit(solution)/shard_map/ppermute | solution.py:41

commit v2 on v1

v2 whole, which is shorter than its diff:
```python
import functools

import jax
import jax.numpy as jnp
from jax import lax
from jax.experimental import pallas as pl
from jax.experimental.pallas import tpu as pltpu
from jax.sharding import PartitionSpec as P

PW = 256
NOTE = 16
CORES = 2
WIDE = jnp.float32
NARROW = jnp.bfloat16


def partner(chip, offset, chips):
    if chips & (chips - 1) == 0:
        return chip ^ offset
    return (chip + offset) % chips


def multiply(matrix, vector):
    return jnp.dot(matrix, vector, preferred_element_type=WIDE)


def after(value, *others):
    return lax.optimization_barrier((value, *others))[0]


def hop(block, offset_of, step, ends):
    chips, chain = ends
    route = []
    for stage in range(chain - step):
        for chip in range(chips):
            for core in range(CORES):
                goal = partner(chip, offset_of(core), chips)
                source = (stage * chips + chip) * CORES + core
                target = ((stage + step) * chips + goal) * CORES + core
                route.append((source, target))
    return lax.ppermute(block, ("chain", "rows"), route)


def swap(block, rows):
    return lax.ppermute(block, "rows", [(i, i ^ 1) for i in range(rows)])


def place():
    me = lax.axis_index("rows")
    return me, lax.div(me, CORES), lax.rem(me, CORES)


def source_row(index, chips):
    _, chip, core = place()
    offset, side = divmod(index, CORES)
    other = partner(chip, (chips - offset) % chips if chips & (chips - 1) else offset, chips)
    return other * CORES + (core if side == 0 else 1 - core)


def lay_pairs(whole, columns, pieces, chips):
    height = pieces[0].shape[0] // CORES
    for offset, piece in enumerate(pieces):
        for side in range(CORES):
            row = source_row(offset * CORES + side, chips)
            rows = pl.ds(pl.multiple_of(row * height, height), height)
            whole[rows, columns] = piece[side * height : (side + 1) * height]


def is_live(order, count, slot):
    found = jnp.int32(0)
    for k in range(order.shape[1]):
        hit = jnp.logical_and(order[0, k] == slot, k < count[0])
        found = jnp.where(hit, jnp.int32(1), found)
    return found


def mark_kernel(slots, own_target, mate_target, order, count, notes, alive):
    me, _, core = place()
    for side, targets in enumerate((own_target, mate_target)):
        row = me if side == 0 else me + 1 - 2 * core
        for slot in range(slots):
            index = side * slots + slot
            rows = slice(index * NOTE, (index + 1) * NOTE)
            note = jnp.full((NOTE, notes.shape[1]), targets[0, slot], jnp.int32)
            notes[rows] = note.astype(WIDE).astype(NARROW)
            live = is_live(order, count, row * slots + slot)
            alive[index : index + 1] = jnp.full((1, notes.shape[1]), live).astype(WIDE)


def write_tiles(out, products, notes, alive, tile):
    for index in range(products.shape[0] // tile):
        base = index * (tile + NOTE)
        product = products[index * tile : (index + 1) * tile]
        kept = jnp.where(alive[index : index + 1] > 0, product, 0.0)
        out[base : base + tile] = kept.astype(NARROW)
        out[base + tile : base + tile + NOTE] = notes[index * NOTE : (index + 1) * NOTE]


def read_targets(sent, tile):
    found = []
    for index in range(sent.shape[0] // (tile + NOTE)):
        base = index * (tile + NOTE) + tile
        note = sent[base : base + NOTE, 0:128].astype(WIDE).astype(jnp.int32)
        found.append(note[0, 0])
    return found


def read_tiles(sent, tile):
    count = sent.shape[0] // (tile + NOTE)
    return jnp.concatenate(
        [sent[i * (tile + NOTE) : i * (tile + NOTE) + tile] for i in range(count)], axis=0
    )


def spread(matrices, sent, tile):
    targets = [t for one in sent for t in read_targets(one, tile)]
    picked = [
        jnp.concatenate(
            [m[:, pl.ds(pl.multiple_of(t * tile, tile), tile)] for t in targets], axis=1
        )
        for m in matrices
    ]
    tiles = jnp.concatenate([read_tiles(one, tile) for one in sent], axis=0)
    return multiply(jnp.concatenate(picked, axis=0), tiles)


def pair_kernel(panels, own, mate, out):
    half = out.shape[1] // panels
    height = own.shape[0] // panels
    for side, block in enumerate((own, mate)):
        rows = slice(side * height, (side + 1) * height)
        for panel in range(panels):
            columns = slice(panel * half, (panel + 1) * half)
            out[rows, columns] = block[panel * height : (panel + 1) * height]


def first_kernel(chips, tile, *refs):
    own, mate, notes, alive = refs[:4]
    pieces, out, whole = refs[4:-2], refs[-2], refs[-1]
    lay_pairs(whole, slice(0, whole.shape[1]), pieces, chips)
    tiles = jnp.concatenate([own[...], mate[...]], axis=0)
    products = multiply(tiles, whole[...])
    write_tiles(out, products, notes, alive, tile)


def ahead_kernel(chips, *refs):
    own, mate = refs[:2]
    pieces, out, whole = refs[2:-2], refs[-2], refs[-1]
    lay_pairs(whole, slice(0, whole.shape[1]), pieces, chips)
    tiles = jnp.concatenate([own[...], mate[...]], axis=0)
    out[...] = multiply(tiles, whole[...])


def next_kernel(chips, tick, tile, *refs):
    own, mate, notes, alive, ahead = refs[:5]
    sent, rest = refs[5 : 5 + chips], refs[5 + chips :]
    past, outs = rest[: len(rest) // 2], rest[len(rest) // 2 :]
    half = PW // CORES
    products = ahead[:, (tick - 1) * half : tick * half]
    products = products - spread((own, mate), sent, tile)
    out = outs[0]
    write_tiles(out, products, notes, alive, tile)
    for index, one in enumerate([*past, out] if past else []):
        history = outs[1]
        history[index * out.shape[0] : (index + 1) * out.shape[0]] = one[...]


def solve_kernel(chips, tile, ticks, *refs):
    inverse, mate = refs[:2]
    first, later = refs[2 : 2 + chips], refs[2 + chips : 2 + 2 * chips]
    sent, (out, other, whole) = refs[2 + 2 * chips : -3], refs[-3:]
    half = PW // CORES
    height = out.shape[0]
    lay_pairs(whole, slice(0, half), first, chips)
    lay_pairs(whole, slice(half, ticks * half), later, chips)
    matrix = jnp.concatenate([inverse[...], mate[...]], axis=0)
    solved = multiply(matrix, whole[...])
    for tick in range(ticks):
        columns = slice(tick * half, (tick + 1) * half)
        one_tick = solved[:, columns]
        if tick:
            here = sent[(tick - 1) * chips : tick * chips]
            one_tick = one_tick - spread((inverse, mate), here, tile)
        out[:, columns] = one_tick[:height]
        other[:, columns] = one_tick[height:].astype(other.dtype)


def update_kernel(tile, ticks, *refs):
    sent, (out, other, total) = refs[:-3], refs[-3:]
    half = PW // CORES
    height = out.shape[0]
    _, chip, core = place()
    size = total.shape[0]
    total[...] = jnp.zeros(total.shape, total.dtype)
    for one in sent:
        count = one.shape[0] // (tile + NOTE) // ticks
        for index, target in enumerate(read_targets(one, tile)):
            tick = index // count
            columns = slice(tick * half, (tick + 1) * half)
            base = index * (tile + NOTE)
            if size >= tile:
                held = size // tile
                spot = target - chip * held

                @pl.when(jnp.logical_and(spot >= 0, spot < held))
                def _(one=one, base=base, spot=spot, columns=columns):
                    rows = pl.ds(pl.multiple_of(spot * tile, tile), tile)
                    total[rows, columns] += one[base : base + tile].astype(WIDE)

            else:
                shares = tile // size
                start = base + lax.rem(chip, shares) * size

                @pl.when(target == lax.div(chip, shares))
                def _(one=one, start=start, columns=columns):
                    rows = pl.ds(pl.multiple_of(start, NOTE), size)
                    total[:, columns] += one[rows].astype(WIDE)

    out[...] = total[pl.ds(pl.multiple_of(core * height, height), height)]
    rest = total[pl.ds(pl.multiple_of((1 - core) * height, height), height)]
    other[...] = rest.astype(other.dtype)


def join_kernel(*refs):
    half = PW // CORES
    _, _, core = place()
    out, tick = refs[-1], 0
    for own, mate in zip(refs[0:-1:2], refs[1:-1:2]):
        for index in range(own.shape[1] // half):
            columns = slice(index * half, (index + 1) * half)
            for side, block in ((core, own), (1 - core, mate)):
                start = pl.multiple_of(tick * PW + side * half, half)
                out[:, pl.ds(start, half)] = block[:, columns].astype(out.dtype)
            tick += 1


def call(kernel, out_shape, args, scratch=()):
    in_specs = [
        pl.BlockSpec(memory_space=pltpu.SMEM if a.dtype == jnp.int32 else pltpu.VMEM)
        for a in args
    ]
    return pl.pallas_call(
        kernel,
        out_shape=out_shape,
        in_specs=in_specs,
        out_specs=jax.tree.map(lambda _: pl.BlockSpec(memory_space=pltpu.VMEM), out_shape),
        scratch_shapes=list(scratch),
        compiler_params=pltpu.CompilerParams(vmem_limit_bytes=40 * 1024 * 1024),
        cost_estimate=pl.CostEstimate(flops=1, bytes_accessed=1, transcendentals=0),
    )(*args)


def body(
    right_side,
    entering,
    first_updates,
    diag_inverse,
    tile_blocks,
    target_row_blocks,
    tile_usage_order,
    live_tile_count,
):
    rows, chain = lax.axis_size("rows"), lax.axis_size("chain")
    chips = rows // CORES
    slots, tile, separator = tile_blocks.shape[1:]
    height = right_side.shape[0]
    ticks = right_side.shape[1] // PW
    half = PW // CORES
    inverse = diag_inverse[0]
    own = tile_blocks[0].reshape(slots * tile, separator)
    ends = (chips, chain)

    def around(block):
        return [
            hop(block, lambda core, offset=offset: offset, 0, ends) for offset in range(1, chips)
        ]

    def shape(height, width, kind):
        return jax.ShapeDtypeStruct((height, width), kind)

    is_low = lax.rem(lax.axis_index("rows"), CORES) == 0
    is_first = (lax.axis_index("chain") == 0).astype(WIDE)

    def pair_up(panels, *others):
        count = len(panels)
        split = [(one[:, :half], one[:, half:]) for one in panels]
        mine = jnp.concatenate([jnp.where(is_low, a, b) for a, b in split], axis=0)
        other = jnp.concatenate([jnp.where(is_low, b, a) for a, b in split], axis=0)
        return call(
            functools.partial(pair_kernel, count),
            shape(CORES * height, count * half, NARROW),
            (after(mine, *others) if others else mine, swap(other, rows)),
        )

    def panel(tick):
        return right_side[:, tick * PW : (tick + 1) * PW].astype(WIDE)

    head = pair_up([(panel(0) - entering).astype(NARROW)])
    heads = [head, *around(head)]
    mate = swap(own, rows)
    mate_target = swap(target_row_blocks, rows)
    marks = call(
        functools.partial(mark_kernel, slots),
        (
            shape(CORES * slots * NOTE, half, NARROW),
            shape(CORES * slots, half, WIDE),
        ),
        (target_row_blocks, mate_target, tile_usage_order, live_tile_count),
    )
    rest = [
        (panel(t) - is_first * first_updates[:, (t - 1) * PW : t * PW]).astype(NARROW)
        for t in range(1, ticks)
    ]
    rest = after(pair_up(rest, mate, marks[1]), *heads[1:])
    laters = [rest, *around(rest)]

    block_rows = CORES * slots * (tile + NOTE)
    block = shape(block_rows, half, NARROW)
    tile_rows = CORES * slots * tile
    product = call(
        functools.partial(first_kernel, chips, tile),
        block,
        (own, mate, *marks, *heads),
        [pltpu.VMEM((separator, half), NARROW)],
    )
    ahead, came, past, shared = None, [], [], []
    for tick in range(1, ticks):
        past.append(product)
        arrived = hop(product, lambda core: 0, 1, ends)
        sent = [arrived, *around(arrived)]
        came += sent
        if ahead is None:
            ahead = call(
                functools.partial(ahead_kernel, chips),
                shape(tile_rows, (ticks - 1) * half, WIDE),
                (own, mate, *[after(one, arrived) for one in laters]),
                [pltpu.VMEM((separator, (ticks - 1) * half), NARROW)],
            )
        earlier = past if tick == ticks - 2 else []
        history = shape((tick + 1) * block_rows, half, NARROW)
        product, *history = call(
            functools.partial(next_kernel, chips, tick, tile),
            (block, history) if earlier else (block,),
            (own, mate, *marks, ahead, *sent, *earlier),
        )
        if tick == ticks - 2:
            shared = [history[0], *around(history[0])]
    last = [product, *around(product)]
    mate_inverse = swap(after(inverse, past[-1]), rows)
    mine, other = call(
        functools.partial(solve_kernel, chips, tile, ticks),
        (shape(height, ticks * half, WIDE), shape(height, ticks * half, NARROW)),
        (inverse, mate_inverse, *heads, *laters, *came[:-1], after(came[-1], product)),
        [pltpu.VMEM((separator, ticks * half), NARROW)],
    )
    out = shape(height, ticks * PW, WIDE)
    solved = call(join_kernel, out, (mine, swap(other, rows)))

    def add_up(count, blocks, kind):
        mine, other = call(
            functools.partial(update_kernel, tile, count),
            (shape(height, count * half, WIDE), shape(height, count * half, kind)),
            tuple(blocks),
            [pltpu.VMEM((CORES * height, count * half), WIDE)],
        )
        return mine, swap(other, rows)

    passed = (
        *add_up(ticks - 1, [after(shared[0], product), *shared[1:]], NARROW),
        *add_up(1, last, WIDE),
    )
    passed = call(join_kernel, out, passed[:-1] + (after(passed[-1], solved),))
    return solved, passed


def solution(mesh):
    placed = (
        P(("chain", "rows"), None),
        P(("chain", "rows"), None),
        P("rows", None),
        P("chain", "rows", None),
        P("chain", "rows", None, None),
        P("chain", "rows"),
        P("chain", None),
        P("chain"),
    )
    return jax.shard_map(
        body,
        mesh=mesh,
        in_specs=placed,
        out_specs=(P(("chain", "rows"), None), P(("chain", "rows"), None)),
        check_vma=False,
    )
```

time: 78.6 us -> 62.2 us (0.79)
  waiting for transfers between devices: 29.9 us -> 18.8 us
  starting transfers between devices: 34.8 us -> 31.7 us
  Pallas kernels: 9.28 us -> 7.33 us
  other arithmetic: 2.25 us -> 1.41 us
    ppermute x16 -> x20, waiting for transfers between devices: 28 us -> 17.7 us  [hop(): return lax.ppermute(block, ('chain', 'rows'), route)]
    ppermute x16 -> x20, starting transfers between devices: 32.1 us -> 29.8 us  [hop(): return lax.ppermute(block, ('chain', 'rows'), route)]
    pallas_call x6 -> x12, Pallas kernels: 9.28 us -> 7.33 us  [call(): pl.pallas_call(kernel, out_shape=out_shape, in_specs=in_specs, out_specs=...]
    convert_element_type x2 -> x1, other arithmetic: 2.25 us -> 1.35 us  [body(): (panel(t) - is_first * first_updates[:, (t - 1) * PW:t * PW]).astype(NARROW)]
    ppermute x17 -> x8, waiting for transfers between devices: 1.92 us -> 1.09 us  [swap(): return lax.ppermute(block, 'rows', [(i, i ^ 1) for i in range(rows)])]
    ppermute x17 -> x8, starting transfers between devices: 2.62 us -> 1.98 us  [swap(): return lax.ppermute(block, 'rows', [(i, i ^ 1) for i in range(rows)])]
  transfers between devices with their start and end apart: 33 -> 28, of which waited for: 13 -> 13; matrix products, arithmetic and copies ran while one was open for 2% -> 2% of each run, Pallas kernels for 8% -> 10%
where the time goes in v2:
time: 62.2 us; the launch traced here: 62 us
  starting transfers between devices  31.7 us (51%)
  waiting for transfers between devices  18.8 us (30%)
  Pallas kernels  7.33 us (12%)
  between operations  2.13 us (3%)
  other arithmetic  1.41 us (2%)
  local copies, waits for them, and re-layouts  0.64 us (1%)
    ppermute x20, starting transfers between devices, hop(): return lax.ppermute(block, ('chain', 'rows'), route)  29.8 us
    ppermute x20, waiting for transfers between devices, hop(): return lax.ppermute(block, ('chain', 'rows'), route)  17.7 us
    pallas_call x12, Pallas kernels, call(): pl.pallas_call(kernel, out_shape=out_shape, in_specs=in_specs, out_specs=...  7.33 us
    ppermute x8, starting transfers between devices, swap(): return lax.ppermute(block, 'rows', [(i, i ^ 1) for i in range(rows)])  1.98 us
    convert_element_type x1, other arithmetic, body(): (panel(t) - is_first * first_updates[:, (t - 1) * PW:t * PW]).astype(NARROW)  1.35 us
  transfers between devices with their start and end apart: 28, of which 13 were waited for; matrix products, arithmetic and copies ran while one was open for 2% of the time, Pallas kernels for 10%

profile of v2, /device:TPU:0, one launch (start us, length us, event | category | flops | bytes accessed | tf_op | source)
XLA Modules:
  0.0 62.0 jit_solution(9809266745873162850)
XLA Ops:
  0.6 0.5 collective-permute-start
  1.1 0.1 collective-permute-start.1
  1.2 1.3 %subtract_convert_fusion.2 = (bf16[256,256]{1,0:T(8,128)(2,1)S(1)}, bf16[256,256]{1,0:T(8,128)(2,1)S(1)}, bf16[256,256]{1,0:T(8,128)(2,1)S(1)}) fusion(f32[256,512]{1,0:T(8,128)} %param.10, f32[]{:T(128)S(6)} %convert_element_type.22, bf16[256,768]{1,0:T(8,128)(2,1)} %param.8, f32[256,256]{1,0:T(8,128)} %param.9), kind=kLoop, calls=%fused_computation.2 | loop fusion | flops 720896 | bytes 1572868 | tf_op jit(solution)/shard_map/convert_element_type | solution.py:311
  2.6 0.5 collective-permute-start.3
  3.1 0.1 collective-permute-start.2
  3.3 0.7 %collective-permute-done.3.mate = bf16[256,128]{1,0:T(8,128)(2,1)S(1)} collective-permute-done((bf16[256,128]{1,0:T(8,128)(2,1)S(1)}, bf16[256,128]{1,0:T(8,128)(2,1)S(1)}, u32[]{:S(2)}, u32[]{:S(2)}) %collective-permute-start.3) | collective-permute-done | bytes 65568 | tf_op jit(solution)/shard_map/ppermute | solution.py:45
  4.0 2.9 %collective-permute-start.4 = (bf16[512,128]{1,0:T(8,128)(2,1)S(1)}, bf16[512,128]{1,0:T(8,128)(2,1)S(1)}, u32[]{:S(2)}, u32[]{:S(2)}) collective-permute-start(bf16[512,128]{1,0:T(8,128)(2,1)S(1)} %shard_map.97.refs_4_.refs_2_), channel_id=1, source_target_pairs={{0,2},{1,3},{2,0},{3,1},{4,6},{5,7},{6,4},{7,5},{8,10},{9,11},{10,... | collective-permute-start | bytes 393224 | tf_op jit(solution)/shard_map/ppermute | solution.py:41
  6.9 1.5 %collective-permute-start.5 = (bf16[512,128]{1,0:T(8,128)(2,1)S(1)}, bf16[512,128]{1,0:T(8,128)(2,1)S(1)}, u32[]{:S(2)}, u32[]{:S(2)}) collective-permute-start(bf16[512,128]{1,0:T(8,128)(2,1)S(1)} %shard_map.97.refs_4_.refs_2_), channel_id=1, source_target_pairs={{0,4},{1,5},{2,6},{3,7},{4,0},{5,1},{6,2},{7,3},{8,12},{9,13},{10,... | collective-permute-start | bytes 393224 | tf_op jit(solution)/shard_map/ppermute | solution.py:41
  8.4 0.0 collective-permute-done.1.mate_target
  8.4 0.0 collective-permute-start.6
  9.8 0.0 copy-start.2
  9.8 0.6 %copy-done.2 = s32[1,8]{1,0:T(1,128)S(1)} copy-done((s32[1,8]{1,0:T(1,128)S(1)}, s32[1,8]{1,0:T(1,128)}, u32[]{:S(2)}) %copy-start.2) | copy-done | bytes 56
  10.4 1.1 %shard_map.95 = (bf16[32,128]{1,0:T(8,128)(2,1)S(1)}, f32[2,128]{1,0:T(2,128)S(1)}) custom-call(s32[1,1]{1,0:T(1,128)S(6)} %copy.10.own_target, s32[1,1]{1,0:T(1,128)} %collective-permute-done.1.mate_target, s32[1,8]{1,0:T(1,128)S(1)} %copy-done.2, s32[1]{0:T(128)S(6)} %copy.11.count), custom_call_target="tpu_custom_call" | custom-call | flops 1 | bytes 1 | tf_op jit(solution)/shard_map/pallas_call | solution.py:242
  11.6 0.0 collective-permute-done.refs_1_
  11.6 0.0 collective-permute-done.2.mate
  11.6 0.0 collective-permute-done.4.refs_5_.refs_3_
  11.6 3.4 %collective-permute-done.5.refs_6_.refs_4_ = bf16[512,128]{1,0:T(8,128)(2,1)S(1)} collective-permute-done((bf16[512,128]{1,0:T(8,128)(2,1)S(1)}, bf16[512,128]{1,0:T(8,128)(2,1)S(1)}, u32[]{:S(2)}, u32[]{:S(2)}) %collective-permute-start.5) | collective-permute-done | bytes 131104 | tf_op jit(solution)/shard_map/ppermute | solution.py:41
  15.0 0.0 collective-permute-done.6.refs_7_.refs_5_
  15.0 1.2 %collective-permute-start.8 = (bf16[512,256]{1,0:T(8,128)(2,1)S(1)}, bf16[512,256]{1,0:T(8,128)(2,1)S(1)}, u32[]{:S(2)}, u32[]{:S(2)}) collective-permute-start(bf16[512,256]{1,0:T(8,128)(2,1)S(1)} %shard_map.96.refs_2_.refs_6_), channel_id=1, source_target_pairs={{0,2},{1,3},{2,0},{3,1},{4,6},{5,7},{6,4},{7,5},{8,10},{9,11},{10,... | collective-permute-start | bytes 786440 | tf_op jit(solution)/shard_map/ppermute | solution.py:41
  16.2 0.8 %collective-permute-start.9 = (bf16[512,256]{1,0:T(8,128)(2,1)S(1)}, bf16[512,256]{1,0:T(8,128)(2,1)S(1)}, u32[]{:S(2)}, u32[]{:S(2)}) collective-permute-start(bf16[512,256]{1,0:T(8,128)(2,1)S(1)} %shard_map.96.refs_2_.refs_6_), channel_id=1, source_target_pairs={{0,4},{1,5},{2,6},{3,7},{4,0},{5,1},{6,2},{7,3},{8,12},{9,13},{10,... | collective-permute-start | bytes 786440 | tf_op jit(solution)/shard_map/ppermute | solution.py:41
  17.1 1.4 %collective-permute-start.10 = (bf16[512,256]{1,0:T(8,128)(2,1)S(1)}, bf16[512,256]{1,0:T(8,128)(2,1)S(1)}, u32[]{:S(2)}, u32[]{:S(2)}) collective-permute-start(bf16[512,256]{1,0:T(8,128)(2,1)S(1)} %shard_map.96.refs_2_.refs_6_), channel_id=1, source_target_pairs={{0,6},{1,7},{2,4},{3,5},{4,2},{5,3},{6,0},{7,1},{8,14},{9,15},{10,... | collective-permute-start | bytes 786440 | tf_op jit(solution)/shard_map/ppermute | solution.py:41
  18.5 0.5 shard_map.98.refs_9_
  19.0 3.5 %collective-permute-start.7 = (bf16[288,128]{1,0:T(8,128)(2,1)S(1)}, bf16[288,128]{1,0:T(8,128)(2,1)S(1)}, u32[]{:S(2)}, u32[]{:S(2)}) collective-permute-start(bf16[288,128]{1,0:T(8,128)(2,1)S(1)} %shard_map.98.refs_9_), channel_id=1, source_target_pairs={{0,8},{1,9},{2,10},{3,11},{4,12},{5,13},{6,14},{7,15},{8,16},{9,17... | collective-permute-start | bytes 221192 | tf_op jit(solution)/shard_map/ppermute | solution.py:41
  22.5 2.0 %collective-permute-done.7.refs_5_.refs_10_ = bf16[288,128]{1,0:T(8,128)(2,1)S(1)} collective-permute-done((bf16[288,128]{1,0:T(8,128)(2,1)S(1)}, bf16[288,128]{1,0:T(8,128)(2,1)S(1)}, u32[]{:S(2)}, u32[]{:S(2)}) %collective-permute-start.7) | collective-permute-done | bytes 73760 | tf_op jit(solution)/shard_map/ppermute | solution.py:41
  24.4 1.2 %collective-permute-start.11 = (bf16[288,128]{1,0:T(8,128)(2,1)S(1)}, bf16[288,128]{1,0:T(8,128)(2,1)S(1)}, u32[]{:S(2)}, u32[]{:S(2)}) collective-permute-start(bf16[288,128]{1,0:T(8,128)(2,1)S(1)} %collective-permute-done.7.refs_5_.refs_10_), channel_id=1, source_target_pairs={{0,2},{1,3},{2,0},{3,1},{4,6},{5,7},{6,4},{7,5},{8,10},{9,11},{10,... | collective-permute-start | bytes 221192 | tf_op jit(solution)/shard_map/ppermute | solution.py:41
  25.7 0.8 %collective-permute-start.12 = (bf16[288,128]{1,0:T(8,128)(2,1)S(1)}, bf16[288,128]{1,0:T(8,128)(2,1)S(1)}, u32[]{:S(2)}, u32[]{:S(2)}) collective-permute-start(bf16[288,128]{1,0:T(8,128)(2,1)S(1)} %collective-permute-done.7.refs_5_.refs_10_), channel_id=1, source_target_pairs={{0,4},{1,5},{2,6},{3,7},{4,0},{5,1},{6,2},{7,3},{8,12},{9,13},{10,... | collective-permute-start | bytes 221192 | tf_op jit(solution)/shard_map/ppermute | solution.py:41
  26.5 0.0 collective-permute-done.8.refs_3_.refs_7_
  26.5 1.4 %collective-permute-start.13 = (bf16[288,128]{1,0:T(8,128)(2,1)S(1)}, bf16[288,128]{1,0:T(8,128)(2,1)S(1)}, u32[]{:S(2)}, u32[]{:S(2)}) collective-permute-start(bf16[288,128]{1,0:T(8,128)(2,1)S(1)} %collective-permute-done.7.refs_5_.refs_10_), channel_id=1, source_target_pairs={{0,6},{1,7},{2,4},{3,5},{4,2},{5,3},{6,0},{7,1},{8,14},{9,15},{10,... | collective-permute-start | bytes 221192 | tf_op jit(solution)/shard_map/ppermute | solution.py:41
  27.9 0.0 collective-permute-done.9.refs_4_.refs_8_
  27.9 2.6 %collective-permute-done.10.refs_5_.refs_9_ = bf16[512,256]{1,0:T(8,128)(2,1)S(1)} collective-permute-done((bf16[512,256]{1,0:T(8,128)(2,1)S(1)}, bf16[512,256]{1,0:T(8,128)(2,1)S(1)}, u32[]{:S(2)}, u32[]{:S(2)}) %collective-permute-start.10) | collective-permute-done | bytes 262176 | tf_op jit(solution)/shard_map/ppermute | solution.py:41
  30.5 0.5 shard_map.99.refs_4_
  31.0 0.0 copy-start.1
  31.0 0.0 collective-permute-done.11.refs_6_.refs_11_
  31.0 1.2 %collective-permute-done.12.refs_7_.refs_12_ = bf16[288,128]{1,0:T(8,128)(2,1)S(1)} collective-permute-done((bf16[288,128]{1,0:T(8,128)(2,1)S(1)}, bf16[288,128]{1,0:T(8,128)(2,1)S(1)}, u32[]{:S(2)}, u32[]{:S(2)}) %collective-permute-start.12) | collective-permute-done | bytes 73760 | tf_op jit(solution)/shard_map/ppermute | solution.py:41
  32.3 0.0 collective-permute-done.13.refs_8_.refs_13_
  32.3 0.4 shard_map.100
  32.7 0.1 collective-permute-start.14
  32.7 3.7 %collective-permute-start.15 = (bf16[288,128]{1,0:T(8,128)(2,1)S(1)}, bf16[288,128]{1,0:T(8,128)(2,1)S(1)}, u32[]{:S(2)}, u32[]{:S(2)}) collective-permute-start(bf16[288,128]{1,0:T(8,128)(2,1)S(1)} %get-tuple-element.30), channel_id=1, source_target_pairs={{0,8},{1,9},{2,10},{3,11},{4,12},{5,13},{6,14},{7,15},{8,16},{9,17... | collective-permute-start | bytes 221192 | tf_op jit(solution)/shard_map/ppermute | solution.py:41
  36.5 2.2 %collective-permute-done.15.refs_5_.refs_14_ = bf16[288,128]{1,0:T(8,128)(2,1)S(1)} collective-permute-done((bf16[288,128]{1,0:T(8,128)(2,1)S(1)}, bf16[288,128]{1,0:T(8,128)(2,1)S(1)}, u32[]{:S(2)}, u32[]{:S(2)}) %collective-permute-start.15) | collective-permute-done | bytes 73760 | tf_op jit(solution)/shard_map/ppermute | solution.py:41
  38.6 1.5 %collective-permute-start.16 = (bf16[288,128]{1,0:T(8,128)(2,1)S(1)}, bf16[288,128]{1,0:T(8,128)(2,1)S(1)}, u32[]{:S(2)}, u32[]{:S(2)}) collective-permute-start(bf16[288,128]{1,0:T(8,128)(2,1)S(1)} %collective-permute-done.15.refs_5_.refs_14_), channel_id=1, source_target_pairs={{0,2},{1,3},{2,0},{3,1},{4,6},{5,7},{6,4},{7,5},{8,10},{9,11},{10,... | collective-permute-start | bytes 221192 | tf_op jit(solution)/shard_map/ppermute | solution.py:41
  40.1 0.5 collective-permute-start.17
  40.6 1.5 %collective-permute-start.18 = (bf16[288,128]{1,0:T(8,128)(2,1)S(1)}, bf16[288,128]{1,0:T(8,128)(2,1)S(1)}, u32[]{:S(2)}, u32[]{:S(2)}) collective-permute-start(bf16[288,128]{1,0:T(8,128)(2,1)S(1)} %collective-permute-done.15.refs_5_.refs_14_), channel_id=1, source_target_pairs={{0,6},{1,7},{2,4},{3,5},{4,2},{5,3},{6,0},{7,1},{8,14},{9,15},{10,... | collective-permute-start | bytes 221192 | tf_op jit(solution)/shard_map/ppermute | solution.py:41
  42.1 0.9 %collective-permute-done.16.refs_6_.refs_15_ = bf16[288,128]{1,0:T(8,128)(2,1)S(1)} collective-permute-done((bf16[288,128]{1,0:T(8,128)(2,1)S(1)}, bf16[288,128]{1,0:T(8,128)(2,1)S(1)}, u32[]{:S(2)}, u32[]{:S(2)}) %collective-permute-start.16) | collective-permute-done | bytes 73760 | tf_op jit(solution)/shard_map/ppermute | solution.py:41
  43.0 2.0 %collective-permute-done.17.refs_7_.refs_16_ = bf16[288,128]{1,0:T(8,128)(2,1)S(1)} collective-permute-done((bf16[288,128]{1,0:T(8,128)(2,1)S(1)}, bf16[288,128]{1,0:T(8,128)(2,1)S(1)}, u32[]{:S(2)}, u32[]{:S(2)}) %collective-permute-start.17) | collective-permute-done | bytes 73760 | tf_op jit(solution)/shard_map/ppermute | solution.py:41
  45.0 0.9 %collective-permute-done.18.refs_8_.refs_17_ = bf16[288,128]{1,0:T(8,128)(2,1)S(1)} collective-permute-done((bf16[288,128]{1,0:T(8,128)(2,1)S(1)}, bf16[288,128]{1,0:T(8,128)(2,1)S(1)}, u32[]{:S(2)}, u32[]{:S(2)}) %collective-permute-start.18) | collective-permute-done | bytes 73760 | tf_op jit(solution)/shard_map/ppermute | solution.py:41
  45.9 0.3 shard_map.101.refs_0_
  46.2 1.3 %collective-permute-start.24 = (bf16[288,128]{1,0:T(8,128)(2,1)S(1)}, bf16[288,128]{1,0:T(8,128)(2,1)S(1)}, u32[]{:S(2)}, u32[]{:S(2)}) collective-permute-start(bf16[288,128]{1,0:T(8,128)(2,1)S(1)} %shard_map.101.refs_0_), channel_id=1, source_target_pairs={{0,2},{1,3},{2,0},{3,1},{4,6},{5,7},{6,4},{7,5},{8,10},{9,11},{10,... | collective-permute-start | bytes 221192 | tf_op jit(solution)/shard_map/ppermute | solution.py:41
  47.5 0.8 %collective-permute-start.20 = (bf16[576,128]{1,0:T(8,128)(2,1)S(1)}, bf16[576,128]{1,0:T(8,128)(2,1)S(1)}, u32[]{:S(2)}, u32[]{:S(2)}) collective-permute-start(bf16[576,128]{1,0:T(8,128)(2,1)S(1)} %get-tuple-element.36.refs_0_), channel_id=1, source_target_pairs={{0,2},{1,3},{2,0},{3,1},{4,6},{5,7},{6,4},{7,5},{8,10},{9,11},{10,... | collective-permute-start | bytes 442376 | tf_op jit(solution)/shard_map/ppermute | solution.py:41
  48.3 1.5 %collective-permute-start.21 = (bf16[576,128]{1,0:T(8,128)(2,1)S(1)}, bf16[576,128]{1,0:T(8,128)(2,1)S(1)}, u32[]{:S(2)}, u32[]{:S(2)}) collective-permute-start(bf16[576,128]{1,0:T(8,128)(2,1)S(1)} %get-tuple-element.36.refs_0_), channel_id=1, source_target_pairs={{0,4},{1,5},{2,6},{3,7},{4,0},{5,1},{6,2},{7,3},{8,12},{9,13},{10,... | collective-permute-start | bytes 442376 | tf_op jit(solution)/shard_map/ppermute | solution.py:41
  49.8 1.2 %collective-permute-start.22 = (bf16[576,128]{1,0:T(8,128)(2,1)S(1)}, bf16[576,128]{1,0:T(8,128)(2,1)S(1)}, u32[]{:S(2)}, u32[]{:S(2)}) collective-permute-start(bf16[576,128]{1,0:T(8,128)(2,1)S(1)} %get-tuple-element.36.refs_0_), channel_id=1, source_target_pairs={{0,6},{1,7},{2,4},{3,5},{4,2},{5,3},{6,0},{7,1},{8,14},{9,15},{10,... | collective-permute-start | bytes 442376 | tf_op jit(solution)/shard_map/ppermute | solution.py:41
  51.0 0.3 collective-permute-done.24.refs_1_
  51.3 1.7 %collective-permute-start.25 = (bf16[288,128]{1,0:T(8,128)(2,1)S(1)}, bf16[288,128]{1,0:T(8,128)(2,1)S(1)}, u32[]{:S(2)}, u32[]{:S(2)}) collective-permute-start(bf16[288,128]{1,0:T(8,128)(2,1)S(1)} %shard_map.101.refs_0_), channel_id=1, source_target_pairs={{0,4},{1,5},{2,6},{3,7},{4,0},{5,1},{6,2},{7,3},{8,12},{9,13},{10,... | collective-permute-start | bytes 221192 | tf_op jit(solution)/shard_map/ppermute | solution.py:41
  52.9 1.2 %collective-permute-start.26 = (bf16[288,128]{1,0:T(8,128)(2,1)S(1)}, bf16[288,128]{1,0:T(8,128)(2,1)S(1)}, u32[]{:S(2)}, u32[]{:S(2)}) collective-permute-start(bf16[288,128]{1,0:T(8,128)(2,1)S(1)} %shard_map.101.refs_0_), channel_id=1, source_target_pairs={{0,6},{1,7},{2,4},{3,5},{4,2},{5,3},{6,0},{7,1},{8,14},{9,15},{10,... | collective-permute-start | bytes 221192 | tf_op jit(solution)/shard_map/ppermute | solution.py:41
  54.1 2.0 %shard_map.102 = (f32[256,384]{1,0:T(8,128)S(1)}, bf16[256,384]{1,0:T(8,128)(2,1)S(1)}) custom-call(bf16[256,2048]{1,0:T(8,128)(2,1)S(1)} %bitcast.8, bf16[256,2048]{1,0:T(8,128)(2,1)S(1)} %collective-permute-done.14.refs_1_, bf16[512,128]{1,0:T(8,128)(2,1)S(1)} %shard_map.97.refs_4_.refs_2_, bf16[512,128]{1,0:T(8,128)(2,1)S(1)} %collective-permute-done.4.refs_5_.refs_3_, ...), custom_call_target="tpu_custom_call" | custom-call | flops 1 | bytes 1 | tf_op jit(solution)/shard_map/pallas_call | solution.py:242
  56.1 2.3 %collective-permute-done.25.refs_2_ = bf16[288,128]{1,0:T(8,128)(2,1)S(1)} collective-permute-done((bf16[288,128]{1,0:T(8,128)(2,1)S(1)}, bf16[288,128]{1,0:T(8,128)(2,1)S(1)}, u32[]{:S(2)}, u32[]{:S(2)}) %collective-permute-start.25) | collective-permute-done | bytes 73760 | tf_op jit(solution)/shard_map/ppermute | solution.py:41
  58.5 0.0 collective-permute-done.26.refs_3_
  58.5 0.2 shard_map.105
  58.7 0.6 collective-permute-start.27
  59.3 0.3 shard_map.104
  59.7 0.1 collective-permute-start.23
  59.8 0.2 collective-permute-done.19.refs_1_
  59.9 0.9 %shard_map.103 = f32[256,768]{1,0:T(8,128)} custom-call(f32[256,384]{1,0:T(8,128)S(1)} %get-tuple-element.33.refs_0_, bf16[256,384]{1,0:T(8,128)(2,1)S(1)} %collective-permute-done.19.refs_1_), custom_call_target="tpu_custom_call" | custom-call | flops 1 | bytes 1 | tf_op jit(solution)/shard_map/pallas_call | solution.py:242
  60.9 0.2 collective-permute-done.23.refs_1_
  61.1 0.9 %shard_map.106 = f32[256,768]{1,0:T(8,128)} custom-call(f32[256,256]{1,0:T(8,128)S(1)} %get-tuple-element.37.refs_0_, bf16[256,256]{1,0:T(8,128)(2,1)S(1)} %collective-permute-done.23.refs_1_, f32[256,128]{1,0:T(8,128)S(1)} %get-tuple-element.39.refs_2_, f32[256,128]{1,0:T(8,128)S(1)} %collective-permute-done.27.refs_3_), custom_call_target="tpu_custom_call" | custom-call | flops 1 | bytes 1 | tf_op jit(solution)/shard_map/pallas_call | solution.py:242
  (15 shorter events, 0.1 us)
Async XLA Ops:
  0.6 10.9 %collective-permute-start = (bf16[128,2048]{1,0:T(8,128)(2,1)}, bf16[128,2048]{1,0:T(8,128)(2,1)S(1)}, u32[]{:S(2)}, u32[]{:S(2)}) collective-permute-start(bf16[128,2048]{1,0:T(8,128)(2,1)} %bitcast.2), channel_id=1, source_target_pairs={{0,1},{1,0},{2,3},{3,2},{4,5},{5,4},{6,7},{7,6},{8,9},{9,8},{10,11... | collective-permute-start | bytes 1572872 | tf_op jit(solution)/shard_map/ppermute | solution.py:45
  1.1 7.3 %collective-permute-start.1 = (s32[1,1]{1,0:T(1,128)}, s32[1,1]{1,0:T(1,128)}, u32[]{:S(2)}, u32[]{:S(2)}) collective-permute-start(s32[1,1]{1,0:T(1,128)} %param.13), channel_id=1, source_target_pairs={{0,1},{1,0},{2,3},{3,2},{4,5},{5,4},{6,7},{7,6},{8,9},{9,8},{10,11... | collective-permute-start | bytes 20 | tf_op jit(solution)/shard_map/ppermute | solution.py:45
  2.6 1.4 %collective-permute-start.3 = (bf16[256,128]{1,0:T(8,128)(2,1)S(1)}, bf16[256,128]{1,0:T(8,128)(2,1)S(1)}, u32[]{:S(2)}, u32[]{:S(2)}) collective-permute-start(bf16[256,128]{1,0:T(8,128)(2,1)S(1)} %get-tuple-element.45), channel_id=1, source_target_pairs={{0,1},{1,0},{2,3},{3,2},{4,5},{5,4},{6,7},{7,6},{8,9},{9,8},{10,11... | collective-permute-start | bytes 196616 | tf_op jit(solution)/shard_map/ppermute | solution.py:45
  3.1 8.4 %collective-permute-start.2 = (bf16[512,128]{1,0:T(8,128)(2,1)S(1)}, bf16[512,128]{1,0:T(8,128)(2,1)S(1)}, u32[]{:S(2)}, u32[]{:S(2)}) collective-permute-start(bf16[512,128]{1,0:T(8,128)(2,1)S(1)} %pad_maximum_fusion.1), channel_id=1, source_target_pairs={{0,1},{1,0},{2,3},{3,2},{4,5},{5,4},{6,7},{7,6},{8,9},{9,8},{10,11... | collective-permute-start | bytes 393224 | tf_op jit(solution)/shard_map/ppermute | solution.py:45
  4.0 14.5 %copy-start = (bf16[1,1,128,2048]{3,2,1,0:T(8,128)(2,1)S(1)}, bf16[1,1,128,2048]{3,2,1,0:T(8,128)(2,1)}, u32[]{:S(2)}) copy-start(bf16[1,1,128,2048]{3,2,1,0:T(8,128)(2,1)} %param.12) | copy-start | bytes 1572868
  4.0 7.6 %collective-permute-start.4 = (bf16[512,128]{1,0:T(8,128)(2,1)S(1)}, bf16[512,128]{1,0:T(8,128)(2,1)S(1)}, u32[]{:S(2)}, u32[]{:S(2)}) collective-permute-start(bf16[512,128]{1,0:T(8,128)(2,1)S(1)} %shard_map.97.refs_4_.refs_2_), channel_id=1, source_target_pairs={{0,2},{1,3},{2,0},{3,1},{4,6},{5,7},{6,4},{7,5},{8,10},{9,11},{10,... | collective-permute-start | bytes 393224 | tf_op jit(solution)/shard_map/ppermute | solution.py:41
  6.9 8.1 %collective-permute-start.5 = (bf16[512,128]{1,0:T(8,128)(2,1)S(1)}, bf16[512,128]{1,0:T(8,128)(2,1)S(1)}, u32[]{:S(2)}, u32[]{:S(2)}) collective-permute-start(bf16[512,128]{1,0:T(8,128)(2,1)S(1)} %shard_map.97.refs_4_.refs_2_), channel_id=1, source_target_pairs={{0,4},{1,5},{2,6},{3,7},{4,0},{5,1},{6,2},{7,3},{8,12},{9,13},{10,... | collective-permute-start | bytes 393224 | tf_op jit(solution)/shard_map/ppermute | solution.py:41
  8.4 6.6 %collective-permute-start.6 = (bf16[512,128]{1,0:T(8,128)(2,1)S(1)}, bf16[512,128]{1,0:T(8,128)(2,1)S(1)}, u32[]{:S(2)}, u32[]{:S(2)}) collective-permute-start(bf16[512,128]{1,0:T(8,128)(2,1)S(1)} %shard_map.97.refs_4_.refs_2_), channel_id=1, source_target_pairs={{0,6},{1,7},{2,4},{3,5},{4,2},{5,3},{6,0},{7,1},{8,14},{9,15},{10,... | collective-permute-start | bytes 393224 | tf_op jit(solution)/shard_map/ppermute | solution.py:41
  9.8 0.7 %copy-start.2 = (s32[1,8]{1,0:T(1,128)S(1)}, s32[1,8]{1,0:T(1,128)}, u32[]{:S(2)}) copy-start(s32[1,8]{1,0:T(1,128)} %order.1) | copy-start | bytes 100
  15.0 11.5 %collective-permute-start.8 = (bf16[512,256]{1,0:T(8,128)(2,1)S(1)}, bf16[512,256]{1,0:T(8,128)(2,1)S(1)}, u32[]{:S(2)}, u32[]{:S(2)}) collective-permute-start(bf16[512,256]{1,0:T(8,128)(2,1)S(1)} %shard_map.96.refs_2_.refs_6_), channel_id=1, source_target_pairs={{0,2},{1,3},{2,0},{3,1},{4,6},{5,7},{6,4},{7,5},{8,10},{9,11},{10,... | collective-permute-start | bytes 786440 | tf_op jit(solution)/shard_map/ppermute | solution.py:41
  16.2 11.7 %collective-permute-start.9 = (bf16[512,256]{1,0:T(8,128)(2,1)S(1)}, bf16[512,256]{1,0:T(8,128)(2,1)S(1)}, u32[]{:S(2)}, u32[]{:S(2)}) collective-permute-start(bf16[512,256]{1,0:T(8,128)(2,1)S(1)} %shard_map.96.refs_2_.refs_6_), channel_id=1, source_target_pairs={{0,4},{1,5},{2,6},{3,7},{4,0},{5,1},{6,2},{7,3},{8,12},{9,13},{10,... | collective-permute-start | bytes 786440 | tf_op jit(solution)/shard_map/ppermute | solution.py:41
  17.1 13.4 %collective-permute-start.10 = (bf16[512,256]{1,0:T(8,128)(2,1)S(1)}, bf16[512,256]{1,0:T(8,128)(2,1)S(1)}, u32[]{:S(2)}, u32[]{:S(2)}) collective-permute-start(bf16[512,256]{1,0:T(8,128)(2,1)S(1)} %shard_map.96.refs_2_.refs_6_), channel_id=1, source_target_pairs={{0,6},{1,7},{2,4},{3,5},{4,2},{5,3},{6,0},{7,1},{8,14},{9,15},{10,... | collective-permute-start | bytes 786440 | tf_op jit(solution)/shard_map/ppermute | solution.py:41
  19.0 5.5 %collective-permute-start.7 = (bf16[288,128]{1,0:T(8,128)(2,1)S(1)}, bf16[288,128]{1,0:T(8,128)(2,1)S(1)}, u32[]{:S(2)}, u32[]{:S(2)}) collective-permute-start(bf16[288,128]{1,0:T(8,128)(2,1)S(1)} %shard_map.98.refs_9_), channel_id=1, source_target_pairs={{0,8},{1,9},{2,10},{3,11},{4,12},{5,13},{6,14},{7,15},{8,16},{9,17... | collective-permute-start | bytes 221192 | tf_op jit(solution)/shard_map/ppermute | solution.py:41
  24.4 6.6 %collective-permute-start.11 = (bf16[288,128]{1,0:T(8,128)(2,1)S(1)}, bf16[288,128]{1,0:T(8,128)(2,1)S(1)}, u32[]{:S(2)}, u32[]{:S(2)}) collective-permute-start(bf16[288,128]{1,0:T(8,128)(2,1)S(1)} %collective-permute-done.7.refs_5_.refs_10_), channel_id=1, source_target_pairs={{0,2},{1,3},{2,0},{3,1},{4,6},{5,7},{6,4},{7,5},{8,10},{9,11},{10,... | collective-permute-start | bytes 221192 | tf_op jit(solution)/shard_map/ppermute | solution.py:41
  25.7 6.6 %collective-permute-start.12 = (bf16[288,128]{1,0:T(8,128)(2,1)S(1)}, bf16[288,128]{1,0:T(8,128)(2,1)S(1)}, u32[]{:S(2)}, u32[]{:S(2)}) collective-permute-start(bf16[288,128]{1,0:T(8,128)(2,1)S(1)} %collective-permute-done.7.refs_5_.refs_10_), channel_id=1, source_target_pairs={{0,4},{1,5},{2,6},{3,7},{4,0},{5,1},{6,2},{7,3},{8,12},{9,13},{10,... | collective-permute-start | bytes 221192 | tf_op jit(solution)/shard_map/ppermute | solution.py:41
  26.5 5.8 %collective-permute-start.13 = (bf16[288,128]{1,0:T(8,128)(2,1)S(1)}, bf16[288,128]{1,0:T(8,128)(2,1)S(1)}, u32[]{:S(2)}, u32[]{:S(2)}) collective-permute-start(bf16[288,128]{1,0:T(8,128)(2,1)S(1)} %collective-permute-done.7.refs_5_.refs_10_), channel_id=1, source_target_pairs={{0,6},{1,7},{2,4},{3,5},{4,2},{5,3},{6,0},{7,1},{8,14},{9,15},{10,... | collective-permute-start | bytes 221192 | tf_op jit(solution)/shard_map/ppermute | solution.py:41
  31.0 1.6 %copy-start.1 = (bf16[1,256,2048]{2,1,0:T(8,128)(2,1)S(1)}, bf16[1,256,2048]{2,1,0:T(8,128)(2,1)}, u32[]{:S(2)}) copy-start(bf16[1,256,2048]{2,1,0:T(8,128)(2,1)} %param.11) | copy-start | bytes 3145732
  32.7 20.3 %collective-permute-start.14 = (bf16[256,2048]{1,0:T(8,128)(2,1)S(1)}, bf16[256,2048]{1,0:T(8,128)(2,1)S(1)}, u32[]{:S(2)}, u32[]{:S(2)}) collective-permute-start(bf16[256,2048]{1,0:T(8,128)(2,1)S(1)} %bitcast.7), channel_id=1, source_target_pairs={{0,1},{1,0},{2,3},{3,2},{4,5},{5,4},{6,7},{7,6},{8,9},{9,8},{10,11... | collective-permute-start | bytes 3145736 | tf_op jit(solution)/shard_map/ppermute | solution.py:45
  32.7 5.9 %collective-permute-start.15 = (bf16[288,128]{1,0:T(8,128)(2,1)S(1)}, bf16[288,128]{1,0:T(8,128)(2,1)S(1)}, u32[]{:S(2)}, u32[]{:S(2)}) collective-permute-start(bf16[288,128]{1,0:T(8,128)(2,1)S(1)} %get-tuple-element.30), channel_id=1, source_target_pairs={{0,8},{1,9},{2,10},{3,11},{4,12},{5,13},{6,14},{7,15},{8,16},{9,17... | collective-permute-start | bytes 221192 | tf_op jit(solution)/shard_map/ppermute | solution.py:41
  38.6 4.4 %collective-permute-start.16 = (bf16[288,128]{1,0:T(8,128)(2,1)S(1)}, bf16[288,128]{1,0:T(8,128)(2,1)S(1)}, u32[]{:S(2)}, u32[]{:S(2)}) collective-permute-start(bf16[288,128]{1,0:T(8,128)(2,1)S(1)} %collective-permute-done.15.refs_5_.refs_14_), channel_id=1, source_target_pairs={{0,2},{1,3},{2,0},{3,1},{4,6},{5,7},{6,4},{7,5},{8,10},{9,11},{10,... | collective-permute-start | bytes 221192 | tf_op jit(solution)/shard_map/ppermute | solution.py:41
  40.1 4.9 %collective-permute-start.17 = (bf16[288,128]{1,0:T(8,128)(2,1)S(1)}, bf16[288,128]{1,0:T(8,128)(2,1)S(1)}, u32[]{:S(2)}, u32[]{:S(2)}) collective-permute-start(bf16[288,128]{1,0:T(8,128)(2,1)S(1)} %collective-permute-done.15.refs_5_.refs_14_), channel_id=1, source_target_pairs={{0,4},{1,5},{2,6},{3,7},{4,0},{5,1},{6,2},{7,3},{8,12},{9,13},{10,... | collective-permute-start | bytes 221192 | tf_op jit(solution)/shard_map/ppermute | solution.py:41
  40.6 5.3 %collective-permute-start.18 = (bf16[288,128]{1,0:T(8,128)(2,1)S(1)}, bf16[288,128]{1,0:T(8,128)(2,1)S(1)}, u32[]{:S(2)}, u32[]{:S(2)}) collective-permute-start(bf16[288,128]{1,0:T(8,128)(2,1)S(1)} %collective-permute-done.15.refs_5_.refs_14_), channel_id=1, source_target_pairs={{0,6},{1,7},{2,4},{3,5},{4,2},{5,3},{6,0},{7,1},{8,14},{9,15},{10,... | collective-permute-start | bytes 221192 | tf_op jit(solution)/shard_map/ppermute | solution.py:41
  46.2 5.1 %collective-permute-start.24 = (bf16[288,128]{1,0:T(8,128)(2,1)S(1)}, bf16[288,128]{1,0:T(8,128)(2,1)S(1)}, u32[]{:S(2)}, u32[]{:S(2)}) collective-permute-start(bf16[288,128]{1,0:T(8,128)(2,1)S(1)} %shard_map.101.refs_0_), channel_id=1, source_target_pairs={{0,2},{1,3},{2,0},{3,1},{4,6},{5,7},{6,4},{7,5},{8,10},{9,11},{10,... | collective-permute-start | bytes 221192 | tf_op jit(solution)/shard_map/ppermute | solution.py:41
  47.5 11.8 %collective-permute-start.20 = (bf16[576,128]{1,0:T(8,128)(2,1)S(1)}, bf16[576,128]{1,0:T(8,128)(2,1)S(1)}, u32[]{:S(2)}, u32[]{:S(2)}) collective-permute-start(bf16[576,128]{1,0:T(8,128)(2,1)S(1)} %get-tuple-element.36.refs_0_), channel_id=1, source_target_pairs={{0,2},{1,3},{2,0},{3,1},{4,6},{5,7},{6,4},{7,5},{8,10},{9,11},{10,... | collective-permute-start | bytes 442376 | tf_op jit(solution)/shard_map/ppermute | solution.py:41
  48.3 11.0 %collective-permute-start.21 = (bf16[576,128]{1,0:T(8,128)(2,1)S(1)}, bf16[576,128]{1,0:T(8,128)(2,1)S(1)}, u32[]{:S(2)}, u32[]{:S(2)}) collective-permute-start(bf16[576,128]{1,0:T(8,128)(2,1)S(1)} %get-tuple-element.36.refs_0_), channel_id=1, source_target_pairs={{0,4},{1,5},{2,6},{3,7},{4,0},{5,1},{6,2},{7,3},{8,12},{9,13},{10,... | collective-permute-start | bytes 442376 | tf_op jit(solution)/shard_map/ppermute | solution.py:41
  49.8 9.5 %collective-permute-start.22 = (bf16[576,128]{1,0:T(8,128)(2,1)S(1)}, bf16[576,128]{1,0:T(8,128)(2,1)S(1)}, u32[]{:S(2)}, u32[]{:S(2)}) collective-permute-start(bf16[576,128]{1,0:T(8,128)(2,1)S(1)} %get-tuple-element.36.refs_0_), channel_id=1, source_target_pairs={{0,6},{1,7},{2,4},{3,5},{4,2},{5,3},{6,0},{7,1},{8,14},{9,15},{10,... | collective-permute-start | bytes 442376 | tf_op jit(solution)/shard_map/ppermute | solution.py:41
  51.3 7.2 %collective-permute-start.25 = (bf16[288,128]{1,0:T(8,128)(2,1)S(1)}, bf16[288,128]{1,0:T(8,128)(2,1)S(1)}, u32[]{:S(2)}, u32[]{:S(2)}) collective-permute-start(bf16[288,128]{1,0:T(8,128)(2,1)S(1)} %shard_map.101.refs_0_), channel_id=1, source_target_pairs={{0,4},{1,5},{2,6},{3,7},{4,0},{5,1},{6,2},{7,3},{8,12},{9,13},{10,... | collective-permute-start | bytes 221192 | tf_op jit(solution)/shard_map/ppermute | solution.py:41
  52.9 5.5 %collective-permute-start.26 = (bf16[288,128]{1,0:T(8,128)(2,1)S(1)}, bf16[288,128]{1,0:T(8,128)(2,1)S(1)}, u32[]{:S(2)}, u32[]{:S(2)}) collective-permute-start(bf16[288,128]{1,0:T(8,128)(2,1)S(1)} %shard_map.101.refs_0_), channel_id=1, source_target_pairs={{0,6},{1,7},{2,4},{3,5},{4,2},{5,3},{6,0},{7,1},{8,14},{9,15},{10,... | collective-permute-start | bytes 221192 | tf_op jit(solution)/shard_map/ppermute | solution.py:41
  58.5 1.4 %collective-permute-start.19 = (bf16[256,384]{1,0:T(8,128)(2,1)S(1)}, bf16[256,384]{1,0:T(8,128)(2,1)S(1)}, u32[]{:S(2)}, u32[]{:S(2)}) collective-permute-start(bf16[256,384]{1,0:T(8,128)(2,1)S(1)} %get-tuple-element.34), channel_id=1, source_target_pairs={{0,1},{1,0},{2,3},{3,2},{4,5},{5,4},{6,7},{7,6},{8,9},{9,8},{10,11... | collective-permute-start | bytes 589832 | tf_op jit(solution)/shard_map/ppermute | solution.py:45
  58.7 2.1 %collective-permute-start.27 = (f32[256,128]{1,0:T(8,128)S(1)}, f32[256,128]{1,0:T(8,128)S(1)}, u32[]{:S(2)}, u32[]{:S(2)}) collective-permute-start(f32[256,128]{1,0:T(8,128)S(1)} %get-tuple-element.40), channel_id=1, source_target_pairs={{0,1},{1,0},{2,3},{3,2},{4,5},{5,4},{6,7},{7,6},{8,9},{9,8},{10,11... | collective-permute-start | bytes 393224 | tf_op jit(solution)/shard_map/ppermute | solution.py:45
  59.7 1.4 %collective-permute-start.23 = (bf16[256,256]{1,0:T(8,128)(2,1)S(1)}, bf16[256,256]{1,0:T(8,128)(2,1)S(1)}, u32[]{:S(2)}, u32[]{:S(2)}) collective-permute-start(bf16[256,256]{1,0:T(8,128)(2,1)S(1)} %get-tuple-element.38), channel_id=1, source_target_pairs={{0,1},{1,0},{2,3},{3,2},{4,5},{5,4},{6,7},{7,6},{8,9},{9,8},{10,11... | collective-permute-start | bytes 393224 | tf_op jit(solution)/shard_map/ppermute | solution.py:45

commit v3 on v2

--- a/solution.py
+++ b/solution.py
@@ -88,39 +88,33 @@
 
 
 def write_tiles(out, products, notes, alive, tile):
-    for index in range(products.shape[0] // tile):
-        base = index * (tile + NOTE)
-        product = products[index * tile : (index + 1) * tile]
-        kept = jnp.where(alive[index : index + 1] > 0, product, 0.0)
-        out[base : base + tile] = kept.astype(NARROW)
-        out[base + tile : base + tile + NOTE] = notes[index * NOTE : (index + 1) * NOTE]
-
-
-def read_targets(sent, tile):
+    rows = products.shape[0]
+    for index in range(rows // tile):
+        here = slice(index * tile, (index + 1) * tile)
+        kept = jnp.where(alive[index : index + 1] > 0, products[here], 0.0)
+        out[here] = kept.astype(NARROW)
+    out[rows:] = notes[...]
+
+
+def read_targets(sent, count):
+    first = sent.shape[0] - count * NOTE
     found = []
-    for index in range(sent.shape[0] // (tile + NOTE)):
-        base = index * (tile + NOTE) + tile
-        note = sent[base : base + NOTE, 0:128].astype(WIDE).astype(jnp.int32)
-        found.append(note[0, 0])
+    for index in range(count):
+        note = sent[first + index * NOTE : first + (index + 1) * NOTE, 0:128]
+        found.append(note.astype(WIDE).astype(jnp.int32)[0, 0])
     return found
 
 
-def read_tiles(sent, tile):
-    count = sent.shape[0] // (tile + NOTE)
-    return jnp.concatenate(
-        [sent[i * (tile + NOTE) : i * (tile + NOTE) + tile] for i in range(count)], axis=0
-    )
-
-
 def spread(matrices, sent, tile):
-    targets = [t for one in sent for t in read_targets(one, tile)]
+    count = sent[0].shape[0] // (tile + NOTE)
+    targets = [t for one in sent for t in read_targets(one, count)]
     picked = [
         jnp.concatenate(
             [m[:, pl.ds(pl.multiple_of(t * tile, tile), tile)] for t in targets], axis=1
         )
         for m in matrices
     ]
-    tiles = jnp.concatenate([read_tiles(one, tile) for one in sent], axis=0)
+    tiles = jnp.concatenate([one[: count * tile] for one in sent], axis=0)
     return multiply(jnp.concatenate(picked, axis=0), tiles)
 
 
@@ -160,9 +154,11 @@
     products = products - spread((own, mate), sent, tile)
     out = outs[0]
     write_tiles(out, products, notes, alive, tile)
+    rows = products.shape[0]
     for index, one in enumerate([*past, out] if past else []):
-        history = outs[1]
-        history[index * out.shape[0] : (index + 1) * out.shape[0]] = one[...]
+        outs[1][index * rows : (index + 1) * rows] = one[:rows]
+    if past:
+        outs[1][(len(past) + 1) * rows :] = notes[...]
 
 
 def solve_kernel(chips, tile, ticks, *refs):
@@ -185,7 +181,7 @@
         other[:, columns] = one_tick[height:].astype(other.dtype)
 
 
-def update_kernel(tile, ticks, *refs):
+def update_kernel(tile, ticks, count, *refs):
     sent, (out, other, total) = refs[:-3], refs[-3:]
     half = PW // CORES
     height = out.shape[0]
@@ -193,11 +189,11 @@
     size = total.shape[0]
     total[...] = jnp.zeros(total.shape, total.dtype)
     for one in sent:
-        count = one.shape[0] // (tile + NOTE) // ticks
-        for index, target in enumerate(read_targets(one, tile)):
-            tick = index // count
+        targets = read_targets(one, count)
+        for index in range(ticks * count):
+            tick, target = index // count, targets[index % count]
             columns = slice(tick * half, (tick + 1) * half)
-            base = index * (tile + NOTE)
+            base = index * tile
             if size >= tile:
                 held = size // tile
                 spot = target - chip * held
@@ -234,7 +230,7 @@
             tick += 1
 
 
-def call(kernel, out_shape, args, scratch=()):
+def call(kernel, out_shape, args, scratch=(), moved=1):
     in_specs = [
         pl.BlockSpec(memory_space=pltpu.SMEM if a.dtype == jnp.int32 else pltpu.VMEM)
         for a in args
@@ -246,7 +242,7 @@
         out_specs=jax.tree.map(lambda _: pl.BlockSpec(memory_space=pltpu.VMEM), out_shape),
         scratch_shapes=list(scratch),
         compiler_params=pltpu.CompilerParams(vmem_limit_bytes=40 * 1024 * 1024),
-        cost_estimate=pl.CostEstimate(flops=1, bytes_accessed=1, transcendentals=0),
+        cost_estimate=pl.CostEstimate(flops=1, bytes_accessed=moved, transcendentals=0),
     )(*args)
 
 
@@ -299,6 +295,7 @@
     heads = [head, *around(head)]
     mate = swap(own, rows)
     mate_target = swap(target_row_blocks, rows)
+    mate_inverse = swap(inverse, rows)
     marks = call(
         functools.partial(mark_kernel, slots),
         (
@@ -311,7 +308,7 @@
         (panel(t) - is_first * first_updates[:, (t - 1) * PW : t * PW]).astype(NARROW)
         for t in range(1, ticks)
     ]
-    rest = after(pair_up(rest, mate, marks[1]), *heads[1:])
+    rest = after(pair_up(rest, mate, mate_inverse, marks[1]), *heads[1:])
     laters = [rest, *around(rest)]
 
     block_rows = CORES * slots * (tile + NOTE)
@@ -337,16 +334,15 @@
                 [pltpu.VMEM((separator, (ticks - 1) * half), NARROW)],
             )
         earlier = past if tick == ticks - 2 else []
-        history = shape((tick + 1) * block_rows, half, NARROW)
+        history = shape(block_rows + tick * tile_rows, half, NARROW)
         product, *history = call(
             functools.partial(next_kernel, chips, tick, tile),
             (block, history) if earlier else (block,),
-            (own, mate, *marks, ahead, *sent, *earlier),
+            (own, mate, *marks, after(ahead, *shared[1:]) if shared else ahead, *sent, *earlier),
         )
         if tick == ticks - 2:
             shared = [history[0], *around(history[0])]
     last = [product, *around(product)]
-    mate_inverse = swap(after(inverse, past[-1]), rows)
     mine, other = call(
         functools.partial(solve_kernel, chips, tile, ticks),
         (shape(height, ticks * half, WIDE), shape(height, ticks * half, NARROW)),
@@ -356,12 +352,13 @@
     out = shape(height, ticks * PW, WIDE)
     solved = call(join_kernel, out, (mine, swap(other, rows)))
 
-    def add_up(count, blocks, kind):
+    def add_up(count, blocks, kind, moved=1):
         mine, other = call(
-            functools.partial(update_kernel, tile, count),
+            functools.partial(update_kernel, tile, count, CORES * slots),
             (shape(height, count * half, WIDE), shape(height, count * half, kind)),
             tuple(blocks),
             [pltpu.VMEM((CORES * height, count * half), WIDE)],
+            moved,
         )
         return mine, swap(other, rows)
 

time: 62.2 us -> 58.2 us (0.936)
  waiting for transfers between devices: 18.8 us -> 15 us
    ppermute x20, waiting for transfers between devices: 17.7 us -> 14.3 us  [hop(): return lax.ppermute(block, ('chain', 'rows'), route)]
    ppermute x20, starting transfers between devices: 29.8 us -> 29.1 us  [hop(): return lax.ppermute(block, ('chain', 'rows'), route)]
  transfers between devices with their start and end apart: 28 -> 28, of which waited for: 13 -> 17; matrix products, arithmetic and copies ran while one was open for 2% -> 2% of each run, Pallas kernels for 10% -> 10%
where the time goes in v3:
time: 58.2 us; the launch traced here: 57.9 us
  starting transfers between devices  31.4 us (54%)
  waiting for transfers between devices  15 us (26%)
  Pallas kernels  7.32 us (13%)
  between operations  2.12 us (4%)
  other arithmetic  1.41 us (2%)
  local copies, waits for them, and re-layouts  0.64 us (1%)
    ppermute x20, starting transfers between devices, hop(): return lax.ppermute(block, ('chain', 'rows'), route)  29.1 us
    ppermute x20, waiting for transfers between devices, hop(): return lax.ppermute(block, ('chain', 'rows'), route)  14.3 us
    pallas_call x12, Pallas kernels, call(): pl.pallas_call(kernel, out_shape=out_shape, in_specs=in_specs, out_specs=...  7.32 us
    ppermute x8, starting transfers between devices, swap(): return lax.ppermute(block, 'rows', [(i, i ^ 1) for i in range(rows)])  2.37 us
    convert_element_type x1, other arithmetic, body(): (panel(t) - is_first * first_updates[:, (t - 1) * PW:t * PW]).astype(NARROW)  1.35 us
  transfers between devices with their start and end apart: 28, of which 17 were waited for; matrix products, arithmetic and copies ran while one was open for 2% of the time, Pallas kernels for 10%

profile of v3, /device:TPU:0, one launch (start us, length us, event | category | flops | bytes accessed | tf_op | source)
XLA Modules:
  0.0 57.9 jit_solution(17277886456376062671)
XLA Ops:
  0.6 0.5 collective-permute-start
  1.1 0.1 collective-permute-start.6
  1.2 0.4 collective-permute-start.5
  1.7 1.3 %subtract_convert_fusion.1 = (bf16[256,256]{1,0:T(8,128)(2,1)S(1)}, bf16[256,256]{1,0:T(8,128)(2,1)S(1)}, bf16[256,256]{1,0:T(8,128)(2,1)S(1)}) fusion(f32[256,512]{1,0:T(8,128)} %param.10, f32[]{:T(128)S(6)} %convert_element_type.24, bf16[256,768]{1,0:T(8,128)(2,1)} %param.8, f32[256,256]{1,0:T(8,128)} %param.9), kind=kLoop, calls=%fused_computation.1 | loop fusion | flops 720896 | bytes 1572868 | tf_op jit(solution)/shard_map/convert_element_type | solution.py:308
  3.0 0.1 collective-permute-start.1
  3.2 0.5 collective-permute-start.7
  3.7 0.6 %collective-permute-done.1.mate = bf16[256,128]{1,0:T(8,128)(2,1)S(1)} collective-permute-done((bf16[256,128]{1,0:T(8,128)(2,1)S(1)}, bf16[256,128]{1,0:T(8,128)(2,1)S(1)}, u32[]{:S(2)}, u32[]{:S(2)}) %collective-permute-start.1) | collective-permute-done | bytes 65568 | tf_op jit(solution)/shard_map/ppermute | solution.py:45
  4.4 3.8 %collective-permute-start.4 = (bf16[512,128]{1,0:T(8,128)(2,1)S(1)}, bf16[512,128]{1,0:T(8,128)(2,1)S(1)}, u32[]{:S(2)}, u32[]{:S(2)}) collective-permute-start(bf16[512,128]{1,0:T(8,128)(2,1)S(1)} %shard_map.95.refs_4_.refs_2_), channel_id=1, source_target_pairs={{0,6},{1,7},{2,4},{3,5},{4,2},{5,3},{6,0},{7,1},{8,14},{9,15},{10,... | collective-permute-start | bytes 393224 | tf_op jit(solution)/shard_map/ppermute | solution.py:41
  8.2 0.0 collective-permute-done.6.mate_target
  8.2 0.5 collective-permute-start.3
  8.7 0.1 collective-permute-start.2
  10.1 0.0 copy-start.2
  10.2 0.6 %copy-done.2 = s32[1,8]{1,0:T(1,128)S(1)} copy-done((s32[1,8]{1,0:T(1,128)S(1)}, s32[1,8]{1,0:T(1,128)}, u32[]{:S(2)}) %copy-start.2) | copy-done | bytes 56
  10.8 1.1 %shard_map.96 = (bf16[32,128]{1,0:T(8,128)(2,1)S(1)}, f32[2,128]{1,0:T(2,128)S(1)}) custom-call(s32[1,1]{1,0:T(1,128)S(6)} %copy.10.own_target, s32[1,1]{1,0:T(1,128)} %collective-permute-done.6.mate_target, s32[1,8]{1,0:T(1,128)S(1)} %copy-done.2, s32[1]{0:T(128)S(6)} %copy.11.count), custom_call_target="tpu_custom_call" | custom-call | flops 1 | bytes 1 | tf_op jit(solution)/shard_map/pallas_call | solution.py:238
  11.9 0.0 collective-permute-done.refs_1_
  12.0 0.1 collective-permute-done.4.refs_7_.refs_5_
  12.2 2.7 %collective-permute-done.3.refs_6_.refs_4_ = bf16[512,128]{1,0:T(8,128)(2,1)S(1)} collective-permute-done((bf16[512,128]{1,0:T(8,128)(2,1)S(1)}, bf16[512,128]{1,0:T(8,128)(2,1)S(1)}, u32[]{:S(2)}, u32[]{:S(2)}) %collective-permute-start.3) | collective-permute-done | bytes 131104 | tf_op jit(solution)/shard_map/ppermute | solution.py:41
  14.9 0.3 collective-permute-done.2.refs_5_.refs_3_
  15.1 1.5 %collective-permute-start.10 = (bf16[512,256]{1,0:T(8,128)(2,1)S(1)}, bf16[512,256]{1,0:T(8,128)(2,1)S(1)}, u32[]{:S(2)}, u32[]{:S(2)}) collective-permute-start(bf16[512,256]{1,0:T(8,128)(2,1)S(1)} %shard_map.97.refs_2_.refs_6_), channel_id=1, source_target_pairs={{0,6},{1,7},{2,4},{3,5},{4,2},{5,3},{6,0},{7,1},{8,14},{9,15},{10,... | collective-permute-start | bytes 786440 | tf_op jit(solution)/shard_map/ppermute | solution.py:41
  16.7 1.4 %collective-permute-start.9 = (bf16[512,256]{1,0:T(8,128)(2,1)S(1)}, bf16[512,256]{1,0:T(8,128)(2,1)S(1)}, u32[]{:S(2)}, u32[]{:S(2)}) collective-permute-start(bf16[512,256]{1,0:T(8,128)(2,1)S(1)} %shard_map.97.refs_2_.refs_6_), channel_id=1, source_target_pairs={{0,4},{1,5},{2,6},{3,7},{4,0},{5,1},{6,2},{7,3},{8,12},{9,13},{10,... | collective-permute-start | bytes 786440 | tf_op jit(solution)/shard_map/ppermute | solution.py:41
  18.1 0.5 collective-permute-start.8
  18.6 0.5 shard_map.98.refs_9_
  19.1 3.5 %collective-permute-start.11 = (bf16[288,128]{1,0:T(8,128)(2,1)S(1)}, bf16[288,128]{1,0:T(8,128)(2,1)S(1)}, u32[]{:S(2)}, u32[]{:S(2)}) collective-permute-start(bf16[288,128]{1,0:T(8,128)(2,1)S(1)} %shard_map.98.refs_9_), channel_id=1, source_target_pairs={{0,8},{1,9},{2,10},{3,11},{4,12},{5,13},{6,14},{7,15},{8,16},{9,17... | collective-permute-start | bytes 221192 | tf_op jit(solution)/shard_map/ppermute | solution.py:41
  22.6 2.0 %collective-permute-done.11.refs_5_.refs_10_ = bf16[288,128]{1,0:T(8,128)(2,1)S(1)} collective-permute-done((bf16[288,128]{1,0:T(8,128)(2,1)S(1)}, bf16[288,128]{1,0:T(8,128)(2,1)S(1)}, u32[]{:S(2)}, u32[]{:S(2)}) %collective-permute-start.11) | collective-permute-done | bytes 73760 | tf_op jit(solution)/shard_map/ppermute | solution.py:41
  24.6 1.7 %collective-permute-start.14 = (bf16[288,128]{1,0:T(8,128)(2,1)S(1)}, bf16[288,128]{1,0:T(8,128)(2,1)S(1)}, u32[]{:S(2)}, u32[]{:S(2)}) collective-permute-start(bf16[288,128]{1,0:T(8,128)(2,1)S(1)} %collective-permute-done.11.refs_5_.refs_10_), channel_id=1, source_target_pairs={{0,6},{1,7},{2,4},{3,5},{4,2},{5,3},{6,0},{7,1},{8,14},{9,15},{10,... | collective-permute-start | bytes 221192 | tf_op jit(solution)/shard_map/ppermute | solution.py:41
  26.2 1.3 %collective-permute-start.13 = (bf16[288,128]{1,0:T(8,128)(2,1)S(1)}, bf16[288,128]{1,0:T(8,128)(2,1)S(1)}, u32[]{:S(2)}, u32[]{:S(2)}) collective-permute-start(bf16[288,128]{1,0:T(8,128)(2,1)S(1)} %collective-permute-done.11.refs_5_.refs_10_), channel_id=1, source_target_pairs={{0,4},{1,5},{2,6},{3,7},{4,0},{5,1},{6,2},{7,3},{8,12},{9,13},{10,... | collective-permute-start | bytes 221192 | tf_op jit(solution)/shard_map/ppermute | solution.py:41
  27.5 0.0 collective-permute-done.10.refs_5_.refs_9_
  27.5 0.5 collective-permute-start.12
  28.1 2.4 %collective-permute-done.9.refs_4_.refs_8_ = bf16[512,256]{1,0:T(8,128)(2,1)S(1)} collective-permute-done((bf16[512,256]{1,0:T(8,128)(2,1)S(1)}, bf16[512,256]{1,0:T(8,128)(2,1)S(1)}, u32[]{:S(2)}, u32[]{:S(2)}) %collective-permute-start.9) | collective-permute-done | bytes 262176 | tf_op jit(solution)/shard_map/ppermute | solution.py:41
  30.5 0.3 collective-permute-done.8.refs_3_.refs_7_
  30.8 0.5 shard_map.99.refs_4_
  31.4 0.8 %collective-permute-done.14.refs_8_.refs_13_ = bf16[288,128]{1,0:T(8,128)(2,1)S(1)} collective-permute-done((bf16[288,128]{1,0:T(8,128)(2,1)S(1)}, bf16[288,128]{1,0:T(8,128)(2,1)S(1)}, u32[]{:S(2)}, u32[]{:S(2)}) %collective-permute-start.14) | collective-permute-done | bytes 73760 | tf_op jit(solution)/shard_map/ppermute | solution.py:41
  32.1 0.6 %collective-permute-done.13.refs_7_.refs_12_ = bf16[288,128]{1,0:T(8,128)(2,1)S(1)} collective-permute-done((bf16[288,128]{1,0:T(8,128)(2,1)S(1)}, bf16[288,128]{1,0:T(8,128)(2,1)S(1)}, u32[]{:S(2)}, u32[]{:S(2)}) %collective-permute-start.13) | collective-permute-done | bytes 73760 | tf_op jit(solution)/shard_map/ppermute | solution.py:41
  32.8 0.3 collective-permute-done.12.refs_6_.refs_11_
  33.1 0.4 shard_map.100
  33.4 1.5 %collective-permute-start.21 = (bf16[544,128]{1,0:T(8,128)(2,1)S(1)}, bf16[544,128]{1,0:T(8,128)(2,1)S(1)}, u32[]{:S(2)}, u32[]{:S(2)}) collective-permute-start(bf16[544,128]{1,0:T(8,128)(2,1)S(1)} %get-tuple-element.36.refs_0_), channel_id=1, source_target_pairs={{0,6},{1,7},{2,4},{3,5},{4,2},{5,3},{6,0},{7,1},{8,14},{9,15},{10,... | collective-permute-start | bytes 417800 | tf_op jit(solution)/shard_map/ppermute | solution.py:41
  34.9 3.5 %collective-permute-start.15 = (bf16[288,128]{1,0:T(8,128)(2,1)S(1)}, bf16[288,128]{1,0:T(8,128)(2,1)S(1)}, u32[]{:S(2)}, u32[]{:S(2)}) collective-permute-start(bf16[288,128]{1,0:T(8,128)(2,1)S(1)} %get-tuple-element.30), channel_id=1, source_target_pairs={{0,8},{1,9},{2,10},{3,11},{4,12},{5,13},{6,14},{7,15},{8,16},{9,17... | collective-permute-start | bytes 221192 | tf_op jit(solution)/shard_map/ppermute | solution.py:41
  38.4 1.5 %collective-permute-start.20 = (bf16[544,128]{1,0:T(8,128)(2,1)S(1)}, bf16[544,128]{1,0:T(8,128)(2,1)S(1)}, u32[]{:S(2)}, u32[]{:S(2)}) collective-permute-start(bf16[544,128]{1,0:T(8,128)(2,1)S(1)} %get-tuple-element.36.refs_0_), channel_id=1, source_target_pairs={{0,4},{1,5},{2,6},{3,7},{4,0},{5,1},{6,2},{7,3},{8,12},{9,13},{10,... | collective-permute-start | bytes 417800 | tf_op jit(solution)/shard_map/ppermute | solution.py:41
  39.9 0.6 %collective-permute-start.19 = (bf16[544,128]{1,0:T(8,128)(2,1)S(1)}, bf16[544,128]{1,0:T(8,128)(2,1)S(1)}, u32[]{:S(2)}, u32[]{:S(2)}) collective-permute-start(bf16[544,128]{1,0:T(8,128)(2,1)S(1)} %get-tuple-element.36.refs_0_), channel_id=1, source_target_pairs={{0,2},{1,3},{2,0},{3,1},{4,6},{5,7},{6,4},{7,5},{8,10},{9,11},{10,... | collective-permute-start | bytes 417800 | tf_op jit(solution)/shard_map/ppermute | solution.py:41
  40.5 0.0 collective-permute-done.15.refs_5_.refs_14_
  40.5 1.4 %collective-permute-start.18 = (bf16[288,128]{1,0:T(8,128)(2,1)S(1)}, bf16[288,128]{1,0:T(8,128)(2,1)S(1)}, u32[]{:S(2)}, u32[]{:S(2)}) collective-permute-start(bf16[288,128]{1,0:T(8,128)(2,1)S(1)} %collective-permute-done.15.refs_5_.refs_14_), channel_id=1, source_target_pairs={{0,6},{1,7},{2,4},{3,5},{4,2},{5,3},{6,0},{7,1},{8,14},{9,15},{10,... | collective-permute-start | bytes 221192 | tf_op jit(solution)/shard_map/ppermute | solution.py:41
  42.0 1.4 %collective-permute-start.17 = (bf16[288,128]{1,0:T(8,128)(2,1)S(1)}, bf16[288,128]{1,0:T(8,128)(2,1)S(1)}, u32[]{:S(2)}, u32[]{:S(2)}) collective-permute-start(bf16[288,128]{1,0:T(8,128)(2,1)S(1)} %collective-permute-done.15.refs_5_.refs_14_), channel_id=1, source_target_pairs={{0,4},{1,5},{2,6},{3,7},{4,0},{5,1},{6,2},{7,3},{8,12},{9,13},{10,... | collective-permute-start | bytes 221192 | tf_op jit(solution)/shard_map/ppermute | solution.py:41
  43.4 0.0 collective-permute-done.21.refs_3_
  43.4 0.6 %collective-permute-start.16 = (bf16[288,128]{1,0:T(8,128)(2,1)S(1)}, bf16[288,128]{1,0:T(8,128)(2,1)S(1)}, u32[]{:S(2)}, u32[]{:S(2)}) collective-permute-start(bf16[288,128]{1,0:T(8,128)(2,1)S(1)} %collective-permute-done.15.refs_5_.refs_14_), channel_id=1, source_target_pairs={{0,2},{1,3},{2,0},{3,1},{4,6},{5,7},{6,4},{7,5},{8,10},{9,11},{10,... | collective-permute-start | bytes 221192 | tf_op jit(solution)/shard_map/ppermute | solution.py:41
  44.0 0.9 %collective-permute-done.20.refs_2_ = bf16[544,128]{1,0:T(8,128)(2,1)S(1)} collective-permute-done((bf16[544,128]{1,0:T(8,128)(2,1)S(1)}, bf16[544,128]{1,0:T(8,128)(2,1)S(1)}, u32[]{:S(2)}, u32[]{:S(2)}) %collective-permute-start.20) | collective-permute-done | bytes 139296 | tf_op jit(solution)/shard_map/ppermute | solution.py:41
  44.9 1.3 %collective-permute-done.19.refs_1_ = bf16[544,128]{1,0:T(8,128)(2,1)S(1)} collective-permute-done((bf16[544,128]{1,0:T(8,128)(2,1)S(1)}, bf16[544,128]{1,0:T(8,128)(2,1)S(1)}, u32[]{:S(2)}, u32[]{:S(2)}) %collective-permute-start.19) | collective-permute-done | bytes 139296 | tf_op jit(solution)/shard_map/ppermute | solution.py:41
  46.2 0.7 %collective-permute-done.18.refs_8_.refs_17_ = bf16[288,128]{1,0:T(8,128)(2,1)S(1)} collective-permute-done((bf16[288,128]{1,0:T(8,128)(2,1)S(1)}, bf16[288,128]{1,0:T(8,128)(2,1)S(1)}, u32[]{:S(2)}, u32[]{:S(2)}) %collective-permute-start.18) | collective-permute-done | bytes 73760 | tf_op jit(solution)/shard_map/ppermute | solution.py:41
  46.9 0.2 collective-permute-done.17.refs_7_.refs_16_
  47.1 0.7 %collective-permute-done.16.refs_6_.refs_15_ = bf16[288,128]{1,0:T(8,128)(2,1)S(1)} collective-permute-done((bf16[288,128]{1,0:T(8,128)(2,1)S(1)}, bf16[288,128]{1,0:T(8,128)(2,1)S(1)}, u32[]{:S(2)}, u32[]{:S(2)}) %collective-permute-start.16) | collective-permute-done | bytes 73760 | tf_op jit(solution)/shard_map/ppermute | solution.py:41
  47.8 0.3 shard_map.101.refs_0_
  48.2 1.5 %collective-permute-start.26 = (bf16[288,128]{1,0:T(8,128)(2,1)S(1)}, bf16[288,128]{1,0:T(8,128)(2,1)S(1)}, u32[]{:S(2)}, u32[]{:S(2)}) collective-permute-start(bf16[288,128]{1,0:T(8,128)(2,1)S(1)} %shard_map.101.refs_0_), channel_id=1, source_target_pairs={{0,6},{1,7},{2,4},{3,5},{4,2},{5,3},{6,0},{7,1},{8,14},{9,15},{10,... | collective-permute-start | bytes 221192 | tf_op jit(solution)/shard_map/ppermute | solution.py:41
  49.7 0.7 %collective-permute-start.25 = (bf16[288,128]{1,0:T(8,128)(2,1)S(1)}, bf16[288,128]{1,0:T(8,128)(2,1)S(1)}, u32[]{:S(2)}, u32[]{:S(2)}) collective-permute-start(bf16[288,128]{1,0:T(8,128)(2,1)S(1)} %shard_map.101.refs_0_), channel_id=1, source_target_pairs={{0,4},{1,5},{2,6},{3,7},{4,0},{5,1},{6,2},{7,3},{8,12},{9,13},{10,... | collective-permute-start | bytes 221192 | tf_op jit(solution)/shard_map/ppermute | solution.py:41
  50.4 1.3 %collective-permute-start.24 = (bf16[288,128]{1,0:T(8,128)(2,1)S(1)}, bf16[288,128]{1,0:T(8,128)(2,1)S(1)}, u32[]{:S(2)}, u32[]{:S(2)}) collective-permute-start(bf16[288,128]{1,0:T(8,128)(2,1)S(1)} %shard_map.101.refs_0_), channel_id=1, source_target_pairs={{0,2},{1,3},{2,0},{3,1},{4,6},{5,7},{6,4},{7,5},{8,10},{9,11},{10,... | collective-permute-start | bytes 221192 | tf_op jit(solution)/shard_map/ppermute | solution.py:41
  51.7 2.0 %shard_map.102 = (f32[256,384]{1,0:T(8,128)S(1)}, bf16[256,384]{1,0:T(8,128)(2,1)S(1)}) custom-call(bf16[256,2048]{1,0:T(8,128)(2,1)S(1)} %bitcast.8, bf16[256,2048]{1,0:T(8,128)(2,1)S(1)} %collective-permute-done.refs_1_, bf16[512,128]{1,0:T(8,128)(2,1)S(1)} %shard_map.95.refs_4_.refs_2_, bf16[512,128]{1,0:T(8,128)(2,1)S(1)} %collective-permute-done.2.refs_5_.refs_3_, ...), custom_call_target="tpu_custom_call" | custom-call | flops 1 | bytes 1 | tf_op jit(solution)/shard_map/pallas_call | solution.py:238
  53.7 0.1 collective-permute-start.22
  53.8 0.4 collective-permute-done.25.refs_2_
  54.3 0.5 collective-permute-done.24.refs_1_
  54.8 0.2 shard_map.105
  55.0 0.1 collective-permute-start.27
  55.1 0.3 shard_map.104
  55.4 0.6 collective-permute-start.23
  56.0 0.9 %shard_map.103 = f32[256,768]{1,0:T(8,128)} custom-call(f32[256,384]{1,0:T(8,128)S(1)} %get-tuple-element.34.refs_0_, bf16[256,384]{1,0:T(8,128)(2,1)S(1)} %collective-permute-done.22.refs_1_), custom_call_target="tpu_custom_call" | custom-call | flops 1 | bytes 1 | tf_op jit(solution)/shard_map/pallas_call | solution.py:238
  57.0 0.0 collective-permute-done.23.refs_1_
  57.0 0.9 %shard_map.106 = f32[256,768]{1,0:T(8,128)} custom-call(f32[256,256]{1,0:T(8,128)S(1)} %get-tuple-element.37.refs_0_, bf16[256,256]{1,0:T(8,128)(2,1)S(1)} %collective-permute-done.23.refs_1_, f32[256,128]{1,0:T(8,128)S(1)} %get-tuple-element.39.refs_2_, f32[256,128]{1,0:T(8,128)S(1)} %collective-permute-done.27.refs_3_), custom_call_target="tpu_custom_call" | custom-call | flops 1 | bytes 1 | tf_op jit(solution)/shard_map/pallas_call | solution.py:238
  (15 shorter events, 0.1 us)
Async XLA Ops:
  0.6 11.3 %collective-permute-start = (bf16[256,2048]{1,0:T(8,128)(2,1)}, bf16[256,2048]{1,0:T(8,128)(2,1)S(1)}, u32[]{:S(2)}, u32[]{:S(2)}) collective-permute-start(bf16[256,2048]{1,0:T(8,128)(2,1)} %bitcast.7), channel_id=1, source_target_pairs={{0,1},{1,0},{2,3},{3,2},{4,5},{5,4},{6,7},{7,6},{8,9},{9,8},{10,11... | collective-permute-start | bytes 3145736 | tf_op jit(solution)/shard_map/ppermute | solution.py:45
  1.1 7.0 %collective-permute-start.6 = (s32[1,1]{1,0:T(1,128)}, s32[1,1]{1,0:T(1,128)}, u32[]{:S(2)}, u32[]{:S(2)}) collective-permute-start(s32[1,1]{1,0:T(1,128)} %param.13), channel_id=1, source_target_pairs={{0,1},{1,0},{2,3},{3,2},{4,5},{5,4},{6,7},{7,6},{8,9},{9,8},{10,11... | collective-permute-start | bytes 20 | tf_op jit(solution)/shard_map/ppermute | solution.py:45
  1.2 7.5 %collective-permute-start.5 = (bf16[128,2048]{1,0:T(8,128)(2,1)}, bf16[128,2048]{1,0:T(8,128)(2,1)S(1)}, u32[]{:S(2)}, u32[]{:S(2)}) collective-permute-start(bf16[128,2048]{1,0:T(8,128)(2,1)} %bitcast.2), channel_id=1, source_target_pairs={{0,1},{1,0},{2,3},{3,2},{4,5},{5,4},{6,7},{7,6},{8,9},{9,8},{10,11... | collective-permute-start | bytes 1572872 | tf_op jit(solution)/shard_map/ppermute | solution.py:45
  3.0 1.3 %collective-permute-start.1 = (bf16[256,128]{1,0:T(8,128)(2,1)S(1)}, bf16[256,128]{1,0:T(8,128)(2,1)S(1)}, u32[]{:S(2)}, u32[]{:S(2)}) collective-permute-start(bf16[256,128]{1,0:T(8,128)(2,1)S(1)} %get-tuple-element.49), channel_id=1, source_target_pairs={{0,1},{1,0},{2,3},{3,2},{4,5},{5,4},{6,7},{7,6},{8,9},{9,8},{10,11... | collective-permute-start | bytes 196616 | tf_op jit(solution)/shard_map/ppermute | solution.py:45
  3.2 8.7 %collective-permute-start.7 = (bf16[512,128]{1,0:T(8,128)(2,1)S(1)}, bf16[512,128]{1,0:T(8,128)(2,1)S(1)}, u32[]{:S(2)}, u32[]{:S(2)}) collective-permute-start(bf16[512,128]{1,0:T(8,128)(2,1)S(1)} %pad_maximum_fusion.1), channel_id=1, source_target_pairs={{0,1},{1,0},{2,3},{3,2},{4,5},{5,4},{6,7},{7,6},{8,9},{9,8},{10,11... | collective-permute-start | bytes 393224 | tf_op jit(solution)/shard_map/ppermute | solution.py:45
  4.4 14.3 %copy-start = (bf16[1,1,128,2048]{3,2,1,0:T(8,128)(2,1)S(1)}, bf16[1,1,128,2048]{3,2,1,0:T(8,128)(2,1)}, u32[]{:S(2)}) copy-start(bf16[1,1,128,2048]{3,2,1,0:T(8,128)(2,1)} %param.12) | copy-start | bytes 1572868
  4.4 7.8 %collective-permute-start.4 = (bf16[512,128]{1,0:T(8,128)(2,1)S(1)}, bf16[512,128]{1,0:T(8,128)(2,1)S(1)}, u32[]{:S(2)}, u32[]{:S(2)}) collective-permute-start(bf16[512,128]{1,0:T(8,128)(2,1)S(1)} %shard_map.95.refs_4_.refs_2_), channel_id=1, source_target_pairs={{0,6},{1,7},{2,4},{3,5},{4,2},{5,3},{6,0},{7,1},{8,14},{9,15},{10,... | collective-permute-start | bytes 393224 | tf_op jit(solution)/shard_map/ppermute | solution.py:41
  8.2 6.7 %collective-permute-start.3 = (bf16[512,128]{1,0:T(8,128)(2,1)S(1)}, bf16[512,128]{1,0:T(8,128)(2,1)S(1)}, u32[]{:S(2)}, u32[]{:S(2)}) collective-permute-start(bf16[512,128]{1,0:T(8,128)(2,1)S(1)} %shard_map.95.refs_4_.refs_2_), channel_id=1, source_target_pairs={{0,4},{1,5},{2,6},{3,7},{4,0},{5,1},{6,2},{7,3},{8,12},{9,13},{10,... | collective-permute-start | bytes 393224 | tf_op jit(solution)/shard_map/ppermute | solution.py:41
  8.7 6.5 %collective-permute-start.2 = (bf16[512,128]{1,0:T(8,128)(2,1)S(1)}, bf16[512,128]{1,0:T(8,128)(2,1)S(1)}, u32[]{:S(2)}, u32[]{:S(2)}) collective-permute-start(bf16[512,128]{1,0:T(8,128)(2,1)S(1)} %shard_map.95.refs_4_.refs_2_), channel_id=1, source_target_pairs={{0,2},{1,3},{2,0},{3,1},{4,6},{5,7},{6,4},{7,5},{8,10},{9,11},{10,... | collective-permute-start | bytes 393224 | tf_op jit(solution)/shard_map/ppermute | solution.py:41
  10.1 0.7 %copy-start.2 = (s32[1,8]{1,0:T(1,128)S(1)}, s32[1,8]{1,0:T(1,128)}, u32[]{:S(2)}) copy-start(s32[1,8]{1,0:T(1,128)} %order.1) | copy-start | bytes 100
  15.1 12.4 %collective-permute-start.10 = (bf16[512,256]{1,0:T(8,128)(2,1)S(1)}, bf16[512,256]{1,0:T(8,128)(2,1)S(1)}, u32[]{:S(2)}, u32[]{:S(2)}) collective-permute-start(bf16[512,256]{1,0:T(8,128)(2,1)S(1)} %shard_map.97.refs_2_.refs_6_), channel_id=1, source_target_pairs={{0,6},{1,7},{2,4},{3,5},{4,2},{5,3},{6,0},{7,1},{8,14},{9,15},{10,... | collective-permute-start | bytes 786440 | tf_op jit(solution)/shard_map/ppermute | solution.py:41
  16.7 13.8 %collective-permute-start.9 = (bf16[512,256]{1,0:T(8,128)(2,1)S(1)}, bf16[512,256]{1,0:T(8,128)(2,1)S(1)}, u32[]{:S(2)}, u32[]{:S(2)}) collective-permute-start(bf16[512,256]{1,0:T(8,128)(2,1)S(1)} %shard_map.97.refs_2_.refs_6_), channel_id=1, source_target_pairs={{0,4},{1,5},{2,6},{3,7},{4,0},{5,1},{6,2},{7,3},{8,12},{9,13},{10,... | collective-permute-start | bytes 786440 | tf_op jit(solution)/shard_map/ppermute | solution.py:41
  18.1 12.7 %collective-permute-start.8 = (bf16[512,256]{1,0:T(8,128)(2,1)S(1)}, bf16[512,256]{1,0:T(8,128)(2,1)S(1)}, u32[]{:S(2)}, u32[]{:S(2)}) collective-permute-start(bf16[512,256]{1,0:T(8,128)(2,1)S(1)} %shard_map.97.refs_2_.refs_6_), channel_id=1, source_target_pairs={{0,2},{1,3},{2,0},{3,1},{4,6},{5,7},{6,4},{7,5},{8,10},{9,11},{10,... | collective-permute-start | bytes 786440 | tf_op jit(solution)/shard_map/ppermute | solution.py:41
  19.1 5.5 %collective-permute-start.11 = (bf16[288,128]{1,0:T(8,128)(2,1)S(1)}, bf16[288,128]{1,0:T(8,128)(2,1)S(1)}, u32[]{:S(2)}, u32[]{:S(2)}) collective-permute-start(bf16[288,128]{1,0:T(8,128)(2,1)S(1)} %shard_map.98.refs_9_), channel_id=1, source_target_pairs={{0,8},{1,9},{2,10},{3,11},{4,12},{5,13},{6,14},{7,15},{8,16},{9,17... | collective-permute-start | bytes 221192 | tf_op jit(solution)/shard_map/ppermute | solution.py:41
  24.6 7.6 %collective-permute-start.14 = (bf16[288,128]{1,0:T(8,128)(2,1)S(1)}, bf16[288,128]{1,0:T(8,128)(2,1)S(1)}, u32[]{:S(2)}, u32[]{:S(2)}) collective-permute-start(bf16[288,128]{1,0:T(8,128)(2,1)S(1)} %collective-permute-done.11.refs_5_.refs_10_), channel_id=1, source_target_pairs={{0,6},{1,7},{2,4},{3,5},{4,2},{5,3},{6,0},{7,1},{8,14},{9,15},{10,... | collective-permute-start | bytes 221192 | tf_op jit(solution)/shard_map/ppermute | solution.py:41
  26.2 6.5 %collective-permute-start.13 = (bf16[288,128]{1,0:T(8,128)(2,1)S(1)}, bf16[288,128]{1,0:T(8,128)(2,1)S(1)}, u32[]{:S(2)}, u32[]{:S(2)}) collective-permute-start(bf16[288,128]{1,0:T(8,128)(2,1)S(1)} %collective-permute-done.11.refs_5_.refs_10_), channel_id=1, source_target_pairs={{0,4},{1,5},{2,6},{3,7},{4,0},{5,1},{6,2},{7,3},{8,12},{9,13},{10,... | collective-permute-start | bytes 221192 | tf_op jit(solution)/shard_map/ppermute | solution.py:41
  27.5 5.5 %collective-permute-start.12 = (bf16[288,128]{1,0:T(8,128)(2,1)S(1)}, bf16[288,128]{1,0:T(8,128)(2,1)S(1)}, u32[]{:S(2)}, u32[]{:S(2)}) collective-permute-start(bf16[288,128]{1,0:T(8,128)(2,1)S(1)} %collective-permute-done.11.refs_5_.refs_10_), channel_id=1, source_target_pairs={{0,2},{1,3},{2,0},{3,1},{4,6},{5,7},{6,4},{7,5},{8,10},{9,11},{10,... | collective-permute-start | bytes 221192 | tf_op jit(solution)/shard_map/ppermute | solution.py:41
  33.4 18.3 %copy-start.1 = (bf16[1,256,2048]{2,1,0:T(8,128)(2,1)S(1)}, bf16[1,256,2048]{2,1,0:T(8,128)(2,1)}, u32[]{:S(2)}) copy-start(bf16[1,256,2048]{2,1,0:T(8,128)(2,1)} %param.11) | copy-start | bytes 3145732
  33.4 10.0 %collective-permute-start.21 = (bf16[544,128]{1,0:T(8,128)(2,1)S(1)}, bf16[544,128]{1,0:T(8,128)(2,1)S(1)}, u32[]{:S(2)}, u32[]{:S(2)}) collective-permute-start(bf16[544,128]{1,0:T(8,128)(2,1)S(1)} %get-tuple-element.36.refs_0_), channel_id=1, source_target_pairs={{0,6},{1,7},{2,4},{3,5},{4,2},{5,3},{6,0},{7,1},{8,14},{9,15},{10,... | collective-permute-start | bytes 417800 | tf_op jit(solution)/shard_map/ppermute | solution.py:41
  34.9 5.6 %collective-permute-start.15 = (bf16[288,128]{1,0:T(8,128)(2,1)S(1)}, bf16[288,128]{1,0:T(8,128)(2,1)S(1)}, u32[]{:S(2)}, u32[]{:S(2)}) collective-permute-start(bf16[288,128]{1,0:T(8,128)(2,1)S(1)} %get-tuple-element.30), channel_id=1, source_target_pairs={{0,8},{1,9},{2,10},{3,11},{4,12},{5,13},{6,14},{7,15},{8,16},{9,17... | collective-permute-start | bytes 221192 | tf_op jit(solution)/shard_map/ppermute | solution.py:41
  38.4 6.5 %collective-permute-start.20 = (bf16[544,128]{1,0:T(8,128)(2,1)S(1)}, bf16[544,128]{1,0:T(8,128)(2,1)S(1)}, u32[]{:S(2)}, u32[]{:S(2)}) collective-permute-start(bf16[544,128]{1,0:T(8,128)(2,1)S(1)} %get-tuple-element.36.refs_0_), channel_id=1, source_target_pairs={{0,4},{1,5},{2,6},{3,7},{4,0},{5,1},{6,2},{7,3},{8,12},{9,13},{10,... | collective-permute-start | bytes 417800 | tf_op jit(solution)/shard_map/ppermute | solution.py:41
  39.9 6.3 %collective-permute-start.19 = (bf16[544,128]{1,0:T(8,128)(2,1)S(1)}, bf16[544,128]{1,0:T(8,128)(2,1)S(1)}, u32[]{:S(2)}, u32[]{:S(2)}) collective-permute-start(bf16[544,128]{1,0:T(8,128)(2,1)S(1)} %get-tuple-element.36.refs_0_), channel_id=1, source_target_pairs={{0,2},{1,3},{2,0},{3,1},{4,6},{5,7},{6,4},{7,5},{8,10},{9,11},{10,... | collective-permute-start | bytes 417800 | tf_op jit(solution)/shard_map/ppermute | solution.py:41
  40.5 6.4 %collective-permute-start.18 = (bf16[288,128]{1,0:T(8,128)(2,1)S(1)}, bf16[288,128]{1,0:T(8,128)(2,1)S(1)}, u32[]{:S(2)}, u32[]{:S(2)}) collective-permute-start(bf16[288,128]{1,0:T(8,128)(2,1)S(1)} %collective-permute-done.15.refs_5_.refs_14_), channel_id=1, source_target_pairs={{0,6},{1,7},{2,4},{3,5},{4,2},{5,3},{6,0},{7,1},{8,14},{9,15},{10,... | collective-permute-start | bytes 221192 | tf_op jit(solution)/shard_map/ppermute | solution.py:41
  42.0 5.1 %collective-permute-start.17 = (bf16[288,128]{1,0:T(8,128)(2,1)S(1)}, bf16[288,128]{1,0:T(8,128)(2,1)S(1)}, u32[]{:S(2)}, u32[]{:S(2)}) collective-permute-start(bf16[288,128]{1,0:T(8,128)(2,1)S(1)} %collective-permute-done.15.refs_5_.refs_14_), channel_id=1, source_target_pairs={{0,4},{1,5},{2,6},{3,7},{4,0},{5,1},{6,2},{7,3},{8,12},{9,13},{10,... | collective-permute-start | bytes 221192 | tf_op jit(solution)/shard_map/ppermute | solution.py:41
  43.4 4.4 %collective-permute-start.16 = (bf16[288,128]{1,0:T(8,128)(2,1)S(1)}, bf16[288,128]{1,0:T(8,128)(2,1)S(1)}, u32[]{:S(2)}, u32[]{:S(2)}) collective-permute-start(bf16[288,128]{1,0:T(8,128)(2,1)S(1)} %collective-permute-done.15.refs_5_.refs_14_), channel_id=1, source_target_pairs={{0,2},{1,3},{2,0},{3,1},{4,6},{5,7},{6,4},{7,5},{8,10},{9,11},{10,... | collective-permute-start | bytes 221192 | tf_op jit(solution)/shard_map/ppermute | solution.py:41
  48.2 5.7 %collective-permute-start.26 = (bf16[288,128]{1,0:T(8,128)(2,1)S(1)}, bf16[288,128]{1,0:T(8,128)(2,1)S(1)}, u32[]{:S(2)}, u32[]{:S(2)}) collective-permute-start(bf16[288,128]{1,0:T(8,128)(2,1)S(1)} %shard_map.101.refs_0_), channel_id=1, source_target_pairs={{0,6},{1,7},{2,4},{3,5},{4,2},{5,3},{6,0},{7,1},{8,14},{9,15},{10,... | collective-permute-start | bytes 221192 | tf_op jit(solution)/shard_map/ppermute | solution.py:41
  49.7 4.6 %collective-permute-start.25 = (bf16[288,128]{1,0:T(8,128)(2,1)S(1)}, bf16[288,128]{1,0:T(8,128)(2,1)S(1)}, u32[]{:S(2)}, u32[]{:S(2)}) collective-permute-start(bf16[288,128]{1,0:T(8,128)(2,1)S(1)} %shard_map.101.refs_0_), channel_id=1, source_target_pairs={{0,4},{1,5},{2,6},{3,7},{4,0},{5,1},{6,2},{7,3},{8,12},{9,13},{10,... | collective-permute-start | bytes 221192 | tf_op jit(solution)/shard_map/ppermute | solution.py:41
  50.4 4.4 %collective-permute-start.24 = (bf16[288,128]{1,0:T(8,128)(2,1)S(1)}, bf16[288,128]{1,0:T(8,128)(2,1)S(1)}, u32[]{:S(2)}, u32[]{:S(2)}) collective-permute-start(bf16[288,128]{1,0:T(8,128)(2,1)S(1)} %shard_map.101.refs_0_), channel_id=1, source_target_pairs={{0,2},{1,3},{2,0},{3,1},{4,6},{5,7},{6,4},{7,5},{8,10},{9,11},{10,... | collective-permute-start | bytes 221192 | tf_op jit(solution)/shard_map/ppermute | solution.py:41
  53.7 2.3 %collective-permute-start.22 = (bf16[256,384]{1,0:T(8,128)(2,1)S(1)}, bf16[256,384]{1,0:T(8,128)(2,1)S(1)}, u32[]{:S(2)}, u32[]{:S(2)}) collective-permute-start(bf16[256,384]{1,0:T(8,128)(2,1)S(1)} %get-tuple-element.35), channel_id=1, source_target_pairs={{0,1},{1,0},{2,3},{3,2},{4,5},{5,4},{6,7},{7,6},{8,9},{9,8},{10,11... | collective-permute-start | bytes 589832 | tf_op jit(solution)/shard_map/ppermute | solution.py:45
  55.0 1.9 %collective-permute-start.27 = (f32[256,128]{1,0:T(8,128)S(1)}, f32[256,128]{1,0:T(8,128)S(1)}, u32[]{:S(2)}, u32[]{:S(2)}) collective-permute-start(f32[256,128]{1,0:T(8,128)S(1)} %get-tuple-element.40), channel_id=1, source_target_pairs={{0,1},{1,0},{2,3},{3,2},{4,5},{5,4},{6,7},{7,6},{8,9},{9,8},{10,11... | collective-permute-start | bytes 393224 | tf_op jit(solution)/shard_map/ppermute | solution.py:45
  55.4 1.5 %collective-permute-start.23 = (bf16[256,256]{1,0:T(8,128)(2,1)S(1)}, bf16[256,256]{1,0:T(8,128)(2,1)S(1)}, u32[]{:S(2)}, u32[]{:S(2)}) collective-permute-start(bf16[256,256]{1,0:T(8,128)(2,1)S(1)} %get-tuple-element.38), channel_id=1, source_target_pairs={{0,1},{1,0},{2,3},{3,2},{4,5},{5,4},{6,7},{7,6},{8,9},{9,8},{10,11... | collective-permute-start | bytes 393224 | tf_op jit(solution)/shard_map/ppermute | solution.py:45

commit v4 on v3

--- a/solution.py
+++ b/solution.py
@@ -50,20 +50,40 @@
     return me, lax.div(me, CORES), lax.rem(me, CORES)
 
 
-def source_row(index, chips):
+def source_row(offsets, side, chips):
     _, chip, core = place()
-    offset, side = divmod(index, CORES)
-    other = partner(chip, (chips - offset) % chips if chips & (chips - 1) else offset, chips)
+    if chips & (chips - 1):
+        other = lax.rem(chip + chips - offsets[0], chips)
+    else:
+        other = chip ^ jnp.where(core == 0, offsets[0], offsets[1])
     return other * CORES + (core if side == 0 else 1 - core)
 
 
-def lay_pairs(whole, columns, pieces, chips):
-    height = pieces[0].shape[0] // CORES
-    for offset, piece in enumerate(pieces):
-        for side in range(CORES):
-            row = source_row(offset * CORES + side, chips)
-            rows = pl.ds(pl.multiple_of(row * height, height), height)
-            whole[rows, columns] = piece[side * height : (side + 1) * height]
+def straight(chips):
+    return [[(offset, offset)] for offset in range(chips)]
+
+
+def doubling(chips):
+    bits = chips.bit_length() - 1
+    known, pieces, phases = [(0, 0)], [[(0, 0)]], []
+    for phase in range(bits):
+        step = (1 << phase, 1 << (phase + 1) % bits)
+        phases.append(step)
+        pieces.append([(a ^ step[0], b ^ step[1]) for a, b in known])
+        known = known + pieces[-1]
+    return pieces, phases
+
+
+def lay_pairs(whole, columns, pieces, origins, chips, start=0):
+    height = whole.shape[0] // chips // CORES
+    for piece, sources in zip(pieces, origins):
+        stride = piece.shape[0] // len(sources)
+        for index, offsets in enumerate(sources):
+            for side in range(CORES):
+                row = source_row(offsets, side, chips)
+                rows = pl.ds(pl.multiple_of(row * height, height), height)
+                first = index * stride + start + side * height
+                whole[rows, columns] = piece[first : first + height]
 
 
 def is_live(order, count, slot):
@@ -119,38 +139,44 @@
 
 
 def pair_kernel(panels, own, mate, out):
-    half = out.shape[1] // panels
     height = own.shape[0] // panels
-    for side, block in enumerate((own, mate)):
-        rows = slice(side * height, (side + 1) * height)
-        for panel in range(panels):
-            columns = slice(panel * half, (panel + 1) * half)
-            out[rows, columns] = block[panel * height : (panel + 1) * height]
+    for panel in range(panels):
+        rows = slice(panel * height, (panel + 1) * height)
+        first = panel * CORES * height
+        out[first : first + height] = own[rows]
+        out[first + height : first + CORES * height] = mate[rows]
+
+
+def stack_kernel(parts, *refs):
+    out, first = refs[-1], 0
+    for (start, size), ref in zip(parts, refs[:-1]):
+        out[first : first + size] = ref[start : start + size]
+        first += size
 
 
 def first_kernel(chips, tile, *refs):
     own, mate, notes, alive = refs[:4]
     pieces, out, whole = refs[4:-2], refs[-2], refs[-1]
-    lay_pairs(whole, slice(0, whole.shape[1]), pieces, chips)
+    lay_pairs(whole, slice(0, whole.shape[1]), pieces, straight(chips), chips)
     tiles = jnp.concatenate([own[...], mate[...]], axis=0)
     products = multiply(tiles, whole[...])
     write_tiles(out, products, notes, alive, tile)
 
 
-def ahead_kernel(chips, *refs):
+def ahead_kernel(chips, origins, starts, *refs):
     own, mate = refs[:2]
     pieces, out, whole = refs[2:-2], refs[-2], refs[-1]
-    lay_pairs(whole, slice(0, whole.shape[1]), pieces, chips)
+    for piece, sources, start in zip(pieces, origins, starts):
+        lay_pairs(whole, slice(0, whole.shape[1]), [piece], [sources], chips, start)
     tiles = jnp.concatenate([own[...], mate[...]], axis=0)
     out[...] = multiply(tiles, whole[...])
 
 
-def next_kernel(chips, tick, tile, *refs):
+def next_kernel(chips, tile, *refs):
     own, mate, notes, alive, ahead = refs[:5]
     sent, rest = refs[5 : 5 + chips], refs[5 + chips :]
     past, outs = rest[: len(rest) // 2], rest[len(rest) // 2 :]
-    half = PW // CORES
-    products = ahead[:, (tick - 1) * half : tick * half]
+    products = ahead[...]
     products = products - spread((own, mate), sent, tile)
     out = outs[0]
     write_tiles(out, products, notes, alive, tile)
@@ -161,14 +187,15 @@
         outs[1][(len(past) + 1) * rows :] = notes[...]
 
 
-def solve_kernel(chips, tile, ticks, *refs):
+def solve_kernel(chips, tile, ticks, origins, starts, *refs):
     inverse, mate = refs[:2]
-    first, later = refs[2 : 2 + chips], refs[2 + chips : 2 + 2 * chips]
-    sent, (out, other, whole) = refs[2 + 2 * chips : -3], refs[-3:]
+    heads, (out, other, whole) = refs[2 : 2 + len(origins)], refs[-3:]
+    sent = refs[2 + len(origins) : -3]
     half = PW // CORES
     height = out.shape[0]
-    lay_pairs(whole, slice(0, half), first, chips)
-    lay_pairs(whole, slice(half, ticks * half), later, chips)
+    for piece, (tick, sources), start in zip(heads, origins, starts):
+        columns = slice(tick * half, (tick + 1) * half)
+        lay_pairs(whole, columns, [piece], [sources], chips, start)
     matrix = jnp.concatenate([inverse[...], mate[...]], axis=0)
     solved = multiply(matrix, whole[...])
     for tick in range(ticks):
@@ -188,7 +215,13 @@
     _, chip, core = place()
     size = total.shape[0]
     total[...] = jnp.zeros(total.shape, total.dtype)
-    for one in sent:
+    block_rows = count * (ticks * tile + NOTE)
+    blocks = [
+        one.at[first : first + block_rows]
+        for one in sent
+        for first in range(0, one.shape[0], block_rows)
+    ]
+    for one in blocks:
         targets = read_targets(one, count)
         for index in range(ticks * count):
             tick, target = index // count, targets[index % count]
@@ -242,7 +275,7 @@
         out_specs=jax.tree.map(lambda _: pl.BlockSpec(memory_space=pltpu.VMEM), out_shape),
         scratch_shapes=list(scratch),
         compiler_params=pltpu.CompilerParams(vmem_limit_bytes=40 * 1024 * 1024),
-        cost_estimate=pl.CostEstimate(flops=1, bytes_accessed=moved, transcendentals=0),
+        cost_estimate=pl.CostEstimate(flops=moved * 1000, bytes_accessed=moved, transcendentals=0),
     )(*args)
 
 
@@ -284,7 +317,7 @@
         other = jnp.concatenate([jnp.where(is_low, b, a) for a, b in split], axis=0)
         return call(
             functools.partial(pair_kernel, count),
-            shape(CORES * height, count * half, NARROW),
+            shape(count * CORES * height, half, NARROW),
             (after(mine, *others) if others else mine, swap(other, rows)),
         )
 
@@ -309,7 +342,41 @@
         for t in range(1, ticks)
     ]
     rest = after(pair_up(rest, mate, mate_inverse, marks[1]), *heads[1:])
-    laters = [rest, *around(rest)]
+    pair_rows = CORES * height
+    origins, phases = doubling(chips)
+
+    def phase(block, index):
+        return hop(block, lambda core: phases[index][core], 0, ends)
+
+    def stacked(parts, args, moved=1):
+        rows_in_all = sum(size for _, size in parts)
+        kernel = functools.partial(stack_kernel, parts)
+        return call(kernel, shape(rows_in_all, half, NARROW), args, (), moved)
+
+    begun = phase(rest, 0)
+
+    def go_on(panel, gate):
+        start = panel * pair_rows
+        pieces, starts = [rest, begun], [start, start]
+        if len(phases) > 1:
+            held = stacked([(start, pair_rows)] * 2, (rest, after(begun, gate)))
+        for index in range(1, len(phases)):
+            pieces.append(phase(held, index))
+            starts.append(0)
+            if index + 1 < len(phases):
+                size = held.shape[0]
+                held = stacked([(0, size)] * 2, (held, pieces[-1]))
+        return pieces, starts
+
+    def gather(block, gate):
+        held, pieces = block, [block]
+        for index in range(len(phases)):
+            came = phase(held, index)
+            pieces.append(came)
+            if index + 1 < len(phases):
+                size = held.shape[0]
+                held = stacked([(0, size)] * 2, (held, after(came, *gate)))
+        return pieces
 
     block_rows = CORES * slots * (tile + NOTE)
     block = shape(block_rows, half, NARROW)
@@ -319,35 +386,49 @@
         block,
         (own, mate, *marks, *heads),
         [pltpu.VMEM((separator, half), NARROW)],
+        1,
     )
-    ahead, came, past, shared = None, [], [], []
+    came, past, shared, laters = [], [], [], []
     for tick in range(1, ticks):
         past.append(product)
         arrived = hop(product, lambda core: 0, 1, ends)
         sent = [arrived, *around(arrived)]
         came += sent
-        if ahead is None:
-            ahead = call(
-                functools.partial(ahead_kernel, chips),
-                shape(tile_rows, (ticks - 1) * half, WIDE),
-                (own, mate, *[after(one, arrived) for one in laters]),
-                [pltpu.VMEM((separator, (ticks - 1) * half), NARROW)],
-            )
+        if shared:
+            shared = gather(shared[0], (arrived,))
+        if tick == 1:
+            laters.append(go_on(0, arrived))
+            laters += [go_on(panel, sent[-1]) for panel in range(1, ticks - 1)]
+        pieces, starts = laters[tick - 1]
+        ahead = call(
+            functools.partial(ahead_kernel, chips, origins, starts),
+            shape(tile_rows, half, WIDE),
+            (own, mate, *pieces),
+            [pltpu.VMEM((separator, half), NARROW)],
+        )
         earlier = past if tick == ticks - 2 else []
         history = shape(block_rows + tick * tile_rows, half, NARROW)
         product, *history = call(
-            functools.partial(next_kernel, chips, tick, tile),
+            functools.partial(next_kernel, chips, tile),
             (block, history) if earlier else (block,),
-            (own, mate, *marks, after(ahead, *shared[1:]) if shared else ahead, *sent, *earlier),
+            (own, mate, *marks, ahead, *sent, *earlier),
+            (),
+            1048576 if tick == 1 else 4194304,
         )
         if tick == ticks - 2:
-            shared = [history[0], *around(history[0])]
+            shared = history
     last = [product, *around(product)]
+    columns_of, sources, offsets = list(heads), [(0, one) for one in straight(chips)], [0] * chips
+    for tick, (pieces, starts) in enumerate(laters):
+        columns_of += pieces
+        sources += [(tick + 1, one) for one in origins]
+        offsets += starts
     mine, other = call(
-        functools.partial(solve_kernel, chips, tile, ticks),
+        functools.partial(solve_kernel, chips, tile, ticks, sources, offsets),
         (shape(height, ticks * half, WIDE), shape(height, ticks * half, NARROW)),
-        (inverse, mate_inverse, *heads, *laters, *came[:-1], after(came[-1], product)),
+        (inverse, mate_inverse, *columns_of, *came[:-1], after(came[-1], product)),
         [pltpu.VMEM((separator, ticks * half), NARROW)],
+        1,
     )
     out = shape(height, ticks * PW, WIDE)
     solved = call(join_kernel, out, (mine, swap(other, rows)))
@@ -362,10 +443,8 @@
         )
         return mine, swap(other, rows)
 
-    passed = (
-        *add_up(ticks - 1, [after(shared[0], product), *shared[1:]], NARROW),
-        *add_up(1, last, WIDE),
-    )
+    early = add_up(ticks - 1, [after(shared[0], product), *shared[1:]], NARROW)
+    passed = (*early, *add_up(1, [after(product, early[0]), *last[1:]], WIDE, 1))
     passed = call(join_kernel, out, passed[:-1] + (after(passed[-1], solved),))
     return solved, passed
 

time: 58.2 us -> 56.1 us (0.964)
  waiting for transfers between devices: 15 us -> 12.2 us
  Pallas kernels: 7.32 us -> 7.96 us
    ppermute x20 -> x19, waiting for transfers between devices: 14.3 us -> 11.5 us  [hop(): return lax.ppermute(block, ('chain', 'rows'), route)]
    pallas_call x12 -> x16, Pallas kernels: 7.32 us -> 7.96 us  [call(): pl.pallas_call(kernel, out_shape=out_shape, in_specs=in_specs, out_specs=...]
    ppermute x20 -> x19, starting transfers between devices: 29.1 us -> 29.2 us  [hop(): return lax.ppermute(block, ('chain', 'rows'), route)]
  transfers between devices with their start and end apart: 28 -> 27, of which waited for: 17 -> 14; matrix products, arithmetic and copies ran while one was open for 2% -> 3% of each run, Pallas kernels for 10% -> 13%
where the time goes in v4:
time: 56.1 us; the launch traced here: 55.9 us
  starting transfers between devices  31.5 us (56%)
  waiting for transfers between devices  12.2 us (22%)
  Pallas kernels  7.96 us (14%)
  between operations  2.14 us (4%)
  other arithmetic  1.41 us (3%)
  local copies, waits for them, and re-layouts  0.64 us (1%)
    ppermute x19, starting transfers between devices, hop(): return lax.ppermute(block, ('chain', 'rows'), route)  29.2 us
    ppermute x19, waiting for transfers between devices, hop(): return lax.ppermute(block, ('chain', 'rows'), route)  11.5 us
    pallas_call x16, Pallas kernels, call(): pl.pallas_call(kernel, out_shape=out_shape, in_specs=in_specs, out_specs=...  7.96 us
    ppermute x8, starting transfers between devices, swap(): return lax.ppermute(block, 'rows', [(i, i ^ 1) for i in range(rows)])  2.31 us
    convert_element_type x1, other arithmetic, body(): (panel(t) - is_first * first_updates[:, (t - 1) * PW:t * PW]).astype(NARROW)  1.35 us
  transfers between devices with their start and end apart: 27, of which 14 were waited for; matrix products, arithmetic and copies ran while one was open for 3% of the time, Pallas kernels for 13%

profile of v4, /device:TPU:0, one launch (start us, length us, event | category | flops | bytes accessed | tf_op | source)
XLA Modules:
  0.0 55.9 jit_solution(8111909408482729410)
XLA Ops:
  0.6 0.5 collective-permute-start
  1.1 0.1 collective-permute-start.6
  1.2 0.4 collective-permute-start.5
  1.7 1.3 %subtract_convert_fusion.1 = (bf16[256,256]{1,0:T(8,128)(2,1)S(1)}, bf16[256,256]{1,0:T(8,128)(2,1)S(1)}, bf16[256,256]{1,0:T(8,128)(2,1)S(1)}) fusion(f32[256,512]{1,0:T(8,128)} %param.10, f32[]{:T(128)S(6)} %convert_element_type.24, bf16[256,768]{1,0:T(8,128)(2,1)} %param.8, f32[256,256]{1,0:T(8,128)} %param.9), kind=kLoop, calls=%fused_computation.1 | loop fusion | flops 720896 | bytes 1572868 | tf_op jit(solution)/shard_map/convert_element_type | solution.py:341
  3.0 0.1 collective-permute-start.1
  3.2 0.5 collective-permute-start.7
  3.7 0.6 %collective-permute-done.1.mate = bf16[256,128]{1,0:T(8,128)(2,1)S(1)} collective-permute-done((bf16[256,128]{1,0:T(8,128)(2,1)S(1)}, bf16[256,128]{1,0:T(8,128)(2,1)S(1)}, u32[]{:S(2)}, u32[]{:S(2)}) %collective-permute-start.1) | collective-permute-done | bytes 65568 | tf_op jit(solution)/shard_map/ppermute | solution.py:45
  4.4 3.8 %collective-permute-start.4 = (bf16[512,128]{1,0:T(8,128)(2,1)S(1)}, bf16[512,128]{1,0:T(8,128)(2,1)S(1)}, u32[]{:S(2)}, u32[]{:S(2)}) collective-permute-start(bf16[512,128]{1,0:T(8,128)(2,1)S(1)} %shard_map.95.refs_4_.refs_2_), channel_id=1, source_target_pairs={{0,6},{1,7},{2,4},{3,5},{4,2},{5,3},{6,0},{7,1},{8,14},{9,15},{10,... | collective-permute-start | bytes 393224 | tf_op jit(solution)/shard_map/ppermute | solution.py:41
  8.2 0.0 collective-permute-done.6.mate_target
  8.2 0.5 collective-permute-start.3
  8.7 0.0 collective-permute-done.5.refs_1_
  8.7 0.1 collective-permute-start.2
  10.1 0.0 copy-start.2
  10.2 0.6 %copy-done.2 = s32[1,8]{1,0:T(1,128)S(1)} copy-done((s32[1,8]{1,0:T(1,128)S(1)}, s32[1,8]{1,0:T(1,128)}, u32[]{:S(2)}) %copy-start.2) | copy-done | bytes 56
  10.8 1.2 %shard_map.96 = (bf16[32,128]{1,0:T(8,128)(2,1)S(1)}, f32[2,128]{1,0:T(2,128)S(1)}) custom-call(s32[1,1]{1,0:T(1,128)S(6)} %copy.10.own_target, s32[1,1]{1,0:T(1,128)} %collective-permute-done.6.mate_target, s32[1,8]{1,0:T(1,128)S(1)} %copy-done.2, s32[1]{0:T(128)S(6)} %copy.11.count), custom_call_target="tpu_custom_call" | custom-call | flops 1000 | bytes 1 | tf_op jit(solution)/shard_map/pallas_call | solution.py:271
  12.0 0.0 collective-permute-done.refs_1_
  12.1 0.0 collective-permute-done.7.mate
  12.1 0.1 collective-permute-done.4.refs_7_.refs_5_
  12.2 2.7 %collective-permute-done.3.refs_6_.refs_4_ = bf16[512,128]{1,0:T(8,128)(2,1)S(1)} collective-permute-done((bf16[512,128]{1,0:T(8,128)(2,1)S(1)}, bf16[512,128]{1,0:T(8,128)(2,1)S(1)}, u32[]{:S(2)}, u32[]{:S(2)}) %collective-permute-start.3) | collective-permute-done | bytes 131104 | tf_op jit(solution)/shard_map/ppermute | solution.py:41
  14.9 0.3 collective-permute-done.2.refs_5_.refs_3_
  15.1 1.5 %collective-permute-start.8 = (bf16[1024,128]{1,0:T(8,128)(2,1)S(1)}, bf16[1024,128]{1,0:T(8,128)(2,1)S(1)}, u32[]{:S(2)}, u32[]{:S(2)}) collective-permute-start(bf16[1024,128]{1,0:T(8,128)(2,1)S(1)} %shard_map.97.refs_0_.refs_2_.refs_6_.refs_9_), channel_id=1, source_target_pairs={{0,2},{1,5},{2,0},{3,7},{4,6},{5,1},{6,4},{7,3},{8,10},{9,13},{10,... | collective-permute-start | bytes 786440 | tf_op jit(solution)/shard_map/ppermute | solution.py:41
  16.6 0.5 shard_map.98.refs_9_
  17.1 3.5 %collective-permute-start.9 = (bf16[288,128]{1,0:T(8,128)(2,1)S(1)}, bf16[288,128]{1,0:T(8,128)(2,1)S(1)}, u32[]{:S(2)}, u32[]{:S(2)}) collective-permute-start(bf16[288,128]{1,0:T(8,128)(2,1)S(1)} %shard_map.98.refs_9_), channel_id=1, source_target_pairs={{0,8},{1,9},{2,10},{3,11},{4,12},{5,13},{6,14},{7,15},{8,16},{9,17... | collective-permute-start | bytes 221192 | tf_op jit(solution)/shard_map/ppermute | solution.py:41
  20.6 2.0 %collective-permute-done.9.refs_5_.refs_12_ = bf16[288,128]{1,0:T(8,128)(2,1)S(1)} collective-permute-done((bf16[288,128]{1,0:T(8,128)(2,1)S(1)}, bf16[288,128]{1,0:T(8,128)(2,1)S(1)}, u32[]{:S(2)}, u32[]{:S(2)}) %collective-permute-start.9) | collective-permute-done | bytes 73760 | tf_op jit(solution)/shard_map/ppermute | solution.py:41
  22.6 0.0 collective-permute-done.8.refs_1_.refs_3_.refs_7_.refs_10_
  22.6 0.8 %collective-permute-start.10 = (bf16[1024,128]{1,0:T(8,128)(2,1)S(1)}, bf16[1024,128]{1,0:T(8,128)(2,1)S(1)}, u32[]{:S(2)}, u32[]{:S(2)}) collective-permute-start(bf16[1024,128]{1,0:T(8,128)(2,1)S(1)} %shard_map.99), channel_id=1, source_target_pairs={{0,4},{1,3},{2,6},{3,1},{4,0},{5,7},{6,2},{7,5},{8,12},{9,11},{10,... | collective-permute-start | bytes 786440 | tf_op jit(solution)/shard_map/ppermute | solution.py:41
  23.4 1.3 %collective-permute-start.11 = (bf16[288,128]{1,0:T(8,128)(2,1)S(1)}, bf16[288,128]{1,0:T(8,128)(2,1)S(1)}, u32[]{:S(2)}, u32[]{:S(2)}) collective-permute-start(bf16[288,128]{1,0:T(8,128)(2,1)S(1)} %collective-permute-done.9.refs_5_.refs_12_), channel_id=1, source_target_pairs={{0,6},{1,7},{2,4},{3,5},{4,2},{5,3},{6,0},{7,1},{8,14},{9,15},{10,... | collective-permute-start | bytes 221192 | tf_op jit(solution)/shard_map/ppermute | solution.py:41
  24.6 1.4 %collective-permute-start.14 = (bf16[288,128]{1,0:T(8,128)(2,1)S(1)}, bf16[288,128]{1,0:T(8,128)(2,1)S(1)}, u32[]{:S(2)}, u32[]{:S(2)}) collective-permute-start(bf16[288,128]{1,0:T(8,128)(2,1)S(1)} %collective-permute-done.9.refs_5_.refs_12_), channel_id=1, source_target_pairs={{0,4},{1,5},{2,6},{3,7},{4,0},{5,1},{6,2},{7,3},{8,12},{9,13},{10,... | collective-permute-start | bytes 221192 | tf_op jit(solution)/shard_map/ppermute | solution.py:41
  26.1 0.8 %collective-permute-start.13 = (bf16[288,128]{1,0:T(8,128)(2,1)S(1)}, bf16[288,128]{1,0:T(8,128)(2,1)S(1)}, u32[]{:S(2)}, u32[]{:S(2)}) collective-permute-start(bf16[288,128]{1,0:T(8,128)(2,1)S(1)} %collective-permute-done.9.refs_5_.refs_12_), channel_id=1, source_target_pairs={{0,2},{1,3},{2,0},{3,1},{4,6},{5,7},{6,4},{7,5},{8,10},{9,11},{10,... | collective-permute-start | bytes 221192 | tf_op jit(solution)/shard_map/ppermute | solution.py:41
  26.9 2.5 %collective-permute-done.11.refs_8_.refs_15_ = bf16[288,128]{1,0:T(8,128)(2,1)S(1)} collective-permute-done((bf16[288,128]{1,0:T(8,128)(2,1)S(1)}, bf16[288,128]{1,0:T(8,128)(2,1)S(1)}, u32[]{:S(2)}, u32[]{:S(2)}) %collective-permute-start.11) | collective-permute-done | bytes 73760 | tf_op jit(solution)/shard_map/ppermute | solution.py:41
  29.4 1.4 %collective-permute-start.12 = (bf16[1024,128]{1,0:T(8,128)(2,1)S(1)}, bf16[1024,128]{1,0:T(8,128)(2,1)S(1)}, u32[]{:S(2)}, u32[]{:S(2)}) collective-permute-start(bf16[1024,128]{1,0:T(8,128)(2,1)S(1)} %shard_map.100), channel_id=1, source_target_pairs={{0,4},{1,3},{2,6},{3,1},{4,0},{5,7},{6,2},{7,5},{8,12},{9,11},{10,... | collective-permute-start | bytes 786440 | tf_op jit(solution)/shard_map/ppermute | solution.py:41
  30.8 0.1 collective-permute-done.10.refs_4_.refs_8_
  30.9 0.5 shard_map.101.refs_4_
  31.4 0.3 collective-permute-done.14.refs_7_.refs_14_
  31.7 0.0 collective-permute-done.13.refs_6_.refs_13_
  31.7 0.4 shard_map.102
  32.0 4.0 %collective-permute-start.15 = (bf16[288,128]{1,0:T(8,128)(2,1)S(1)}, bf16[288,128]{1,0:T(8,128)(2,1)S(1)}, u32[]{:S(2)}, u32[]{:S(2)}) collective-permute-start(bf16[288,128]{1,0:T(8,128)(2,1)S(1)} %get-tuple-element.27), channel_id=1, source_target_pairs={{0,8},{1,9},{2,10},{3,11},{4,12},{5,13},{6,14},{7,15},{8,16},{9,17... | collective-permute-start | bytes 221192 | tf_op jit(solution)/shard_map/ppermute | solution.py:41
  36.1 1.3 %collective-permute-start.20 = (bf16[544,128]{1,0:T(8,128)(2,1)S(1)}, bf16[544,128]{1,0:T(8,128)(2,1)S(1)}, u32[]{:S(2)}, u32[]{:S(2)}) collective-permute-start(bf16[544,128]{1,0:T(8,128)(2,1)S(1)} %get-tuple-element.32.refs_0_), channel_id=1, source_target_pairs={{0,2},{1,5},{2,0},{3,7},{4,6},{5,1},{6,4},{7,3},{8,10},{9,13},{10,... | collective-permute-start | bytes 417800 | tf_op jit(solution)/shard_map/ppermute | solution.py:41
  37.4 0.7 %collective-permute-done.15.refs_5_.refs_16_ = bf16[288,128]{1,0:T(8,128)(2,1)S(1)} collective-permute-done((bf16[288,128]{1,0:T(8,128)(2,1)S(1)}, bf16[288,128]{1,0:T(8,128)(2,1)S(1)}, u32[]{:S(2)}, u32[]{:S(2)}) %collective-permute-start.15) | collective-permute-done | bytes 73760 | tf_op jit(solution)/shard_map/ppermute | solution.py:41
  38.0 1.4 %collective-permute-start.18 = (bf16[288,128]{1,0:T(8,128)(2,1)S(1)}, bf16[288,128]{1,0:T(8,128)(2,1)S(1)}, u32[]{:S(2)}, u32[]{:S(2)}) collective-permute-start(bf16[288,128]{1,0:T(8,128)(2,1)S(1)} %collective-permute-done.15.refs_5_.refs_16_), channel_id=1, source_target_pairs={{0,6},{1,7},{2,4},{3,5},{4,2},{5,3},{6,0},{7,1},{8,14},{9,15},{10,... | collective-permute-start | bytes 221192 | tf_op jit(solution)/shard_map/ppermute | solution.py:41
  39.4 1.3 %collective-permute-start.17 = (bf16[288,128]{1,0:T(8,128)(2,1)S(1)}, bf16[288,128]{1,0:T(8,128)(2,1)S(1)}, u32[]{:S(2)}, u32[]{:S(2)}) collective-permute-start(bf16[288,128]{1,0:T(8,128)(2,1)S(1)} %collective-permute-done.15.refs_5_.refs_16_), channel_id=1, source_target_pairs={{0,4},{1,5},{2,6},{3,7},{4,0},{5,1},{6,2},{7,3},{8,12},{9,13},{10,... | collective-permute-start | bytes 221192 | tf_op jit(solution)/shard_map/ppermute | solution.py:41
  40.7 0.8 %collective-permute-start.16 = (bf16[288,128]{1,0:T(8,128)(2,1)S(1)}, bf16[288,128]{1,0:T(8,128)(2,1)S(1)}, u32[]{:S(2)}, u32[]{:S(2)}) collective-permute-start(bf16[288,128]{1,0:T(8,128)(2,1)S(1)} %collective-permute-done.15.refs_5_.refs_16_), channel_id=1, source_target_pairs={{0,2},{1,3},{2,0},{3,1},{4,6},{5,7},{6,4},{7,5},{8,10},{9,11},{10,... | collective-permute-start | bytes 221192 | tf_op jit(solution)/shard_map/ppermute | solution.py:41
  41.5 0.0 collective-permute-done.12.refs_4_.refs_11_
  41.5 0.5 shard_map.103.refs_4_
  42.0 0.2 collective-permute-done.20.refs_1_
  42.2 0.0 copy-start.1
  42.2 1.8 %collective-permute-start.21 = (bf16[1088,128]{1,0:T(8,128)(2,1)S(1)}, bf16[1088,128]{1,0:T(8,128)(2,1)S(1)}, u32[]{:S(2)}, u32[]{:S(2)}) collective-permute-start(bf16[1088,128]{1,0:T(8,128)(2,1)S(1)} %shard_map.107), channel_id=1, source_target_pairs={{0,4},{1,3},{2,6},{3,1},{4,0},{5,7},{6,2},{7,5},{8,12},{9,11},{10,... | collective-permute-start | bytes 835592 | tf_op jit(solution)/shard_map/ppermute | solution.py:41
  44.0 0.9 %collective-permute-done.18.refs_8_.refs_19_ = bf16[288,128]{1,0:T(8,128)(2,1)S(1)} collective-permute-done((bf16[288,128]{1,0:T(8,128)(2,1)S(1)}, bf16[288,128]{1,0:T(8,128)(2,1)S(1)}, u32[]{:S(2)}, u32[]{:S(2)}) %collective-permute-start.18) | collective-permute-done | bytes 73760 | tf_op jit(solution)/shard_map/ppermute | solution.py:41
  44.9 1.0 %collective-permute-done.16.refs_6_.refs_17_ = bf16[288,128]{1,0:T(8,128)(2,1)S(1)} collective-permute-done((bf16[288,128]{1,0:T(8,128)(2,1)S(1)}, bf16[288,128]{1,0:T(8,128)(2,1)S(1)}, u32[]{:S(2)}, u32[]{:S(2)}) %collective-permute-start.16) | collective-permute-done | bytes 73760 | tf_op jit(solution)/shard_map/ppermute | solution.py:41
  45.9 0.3 shard_map.104.refs_0_
  46.2 1.6 %collective-permute-start.25 = (bf16[288,128]{1,0:T(8,128)(2,1)S(1)}, bf16[288,128]{1,0:T(8,128)(2,1)S(1)}, u32[]{:S(2)}, u32[]{:S(2)}) collective-permute-start(bf16[288,128]{1,0:T(8,128)(2,1)S(1)} %shard_map.104.refs_0_), channel_id=1, source_target_pairs={{0,6},{1,7},{2,4},{3,5},{4,2},{5,3},{6,0},{7,1},{8,14},{9,15},{10,... | collective-permute-start | bytes 221192 | tf_op jit(solution)/shard_map/ppermute | solution.py:41
  47.8 1.0 %collective-permute-start.24 = (bf16[288,128]{1,0:T(8,128)(2,1)S(1)}, bf16[288,128]{1,0:T(8,128)(2,1)S(1)}, u32[]{:S(2)}, u32[]{:S(2)}) collective-permute-start(bf16[288,128]{1,0:T(8,128)(2,1)S(1)} %shard_map.104.refs_0_), channel_id=1, source_target_pairs={{0,4},{1,5},{2,6},{3,7},{4,0},{5,1},{6,2},{7,3},{8,12},{9,13},{10,... | collective-permute-start | bytes 221192 | tf_op jit(solution)/shard_map/ppermute | solution.py:41
  48.8 1.0 %collective-permute-start.23 = (bf16[288,128]{1,0:T(8,128)(2,1)S(1)}, bf16[288,128]{1,0:T(8,128)(2,1)S(1)}, u32[]{:S(2)}, u32[]{:S(2)}) collective-permute-start(bf16[288,128]{1,0:T(8,128)(2,1)S(1)} %shard_map.104.refs_0_), channel_id=1, source_target_pairs={{0,2},{1,3},{2,0},{3,1},{4,6},{5,7},{6,4},{7,5},{8,10},{9,11},{10,... | collective-permute-start | bytes 221192 | tf_op jit(solution)/shard_map/ppermute | solution.py:41
  49.8 2.1 %shard_map.105 = (f32[256,384]{1,0:T(8,128)S(1)}, bf16[256,384]{1,0:T(8,128)(2,1)S(1)}) custom-call(bf16[256,2048]{1,0:T(8,128)(2,1)S(1)} %bitcast.9, bf16[256,2048]{1,0:T(8,128)(2,1)S(1)} %collective-permute-done.refs_1_, bf16[512,128]{1,0:T(8,128)(2,1)S(1)} %shard_map.95.refs_4_.refs_2_, bf16[512,128]{1,0:T(8,128)(2,1)S(1)} %collective-permute-done.2.refs_5_.refs_3_, ...), custom_call_target="tpu_custom_call" | custom-call | flops 1000 | bytes 1 | tf_op jit(solution)/shard_map/pallas_call | solution.py:271
  51.9 0.1 collective-permute-start.19
  52.0 0.3 shard_map.108
  52.4 0.0 collective-permute-done.24.refs_2_
  52.4 0.8 %collective-permute-done.23.refs_1_ = bf16[288,128]{1,0:T(8,128)(2,1)S(1)} collective-permute-done((bf16[288,128]{1,0:T(8,128)(2,1)S(1)}, bf16[288,128]{1,0:T(8,128)(2,1)S(1)}, u32[]{:S(2)}, u32[]{:S(2)}) %collective-permute-start.23) | collective-permute-done | bytes 73760 | tf_op jit(solution)/shard_map/ppermute | solution.py:41
  53.1 0.2 shard_map.109
  53.4 0.1 collective-permute-start.26
  53.4 0.5 collective-permute-start.22
  53.9 0.9 %shard_map.106 = f32[256,768]{1,0:T(8,128)} custom-call(f32[256,384]{1,0:T(8,128)S(1)} %get-tuple-element.29.refs_0_, bf16[256,384]{1,0:T(8,128)(2,1)S(1)} %collective-permute-done.19.refs_1_), custom_call_target="tpu_custom_call" | custom-call | flops 1000 | bytes 1 | tf_op jit(solution)/shard_map/pallas_call | solution.py:271
  54.9 0.1 collective-permute-done.22.refs_1_
  55.0 0.9 %shard_map.110 = f32[256,768]{1,0:T(8,128)} custom-call(f32[256,256]{1,0:T(8,128)S(1)} %get-tuple-element.34.refs_0_, bf16[256,256]{1,0:T(8,128)(2,1)S(1)} %collective-permute-done.22.refs_1_, f32[256,128]{1,0:T(8,128)S(1)} %get-tuple-element.37.refs_2_, f32[256,128]{1,0:T(8,128)S(1)} %collective-permute-done.26.refs_3_), custom_call_target="tpu_custom_call" | custom-call | flops 1000 | bytes 1 | tf_op jit(solution)/shard_map/pallas_call | solution.py:271
  (17 shorter events, 0.2 us)
Async XLA Ops:
  0.6 11.4 %collective-permute-start = (bf16[256,2048]{1,0:T(8,128)(2,1)}, bf16[256,2048]{1,0:T(8,128)(2,1)S(1)}, u32[]{:S(2)}, u32[]{:S(2)}) collective-permute-start(bf16[256,2048]{1,0:T(8,128)(2,1)} %bitcast.8), channel_id=1, source_target_pairs={{0,1},{1,0},{2,3},{3,2},{4,5},{5,4},{6,7},{7,6},{8,9},{9,8},{10,11... | collective-permute-start | bytes 3145736 | tf_op jit(solution)/shard_map/ppermute | solution.py:45
  1.1 7.0 %collective-permute-start.6 = (s32[1,1]{1,0:T(1,128)}, s32[1,1]{1,0:T(1,128)}, u32[]{:S(2)}, u32[]{:S(2)}) collective-permute-start(s32[1,1]{1,0:T(1,128)} %param.13), channel_id=1, source_target_pairs={{0,1},{1,0},{2,3},{3,2},{4,5},{5,4},{6,7},{7,6},{8,9},{9,8},{10,11... | collective-permute-start | bytes 20 | tf_op jit(solution)/shard_map/ppermute | solution.py:45
  1.2 7.5 %collective-permute-start.5 = (bf16[128,2048]{1,0:T(8,128)(2,1)}, bf16[128,2048]{1,0:T(8,128)(2,1)S(1)}, u32[]{:S(2)}, u32[]{:S(2)}) collective-permute-start(bf16[128,2048]{1,0:T(8,128)(2,1)} %bitcast.2), channel_id=1, source_target_pairs={{0,1},{1,0},{2,3},{3,2},{4,5},{5,4},{6,7},{7,6},{8,9},{9,8},{10,11... | collective-permute-start | bytes 1572872 | tf_op jit(solution)/shard_map/ppermute | solution.py:45
  3.0 1.3 %collective-permute-start.1 = (bf16[256,128]{1,0:T(8,128)(2,1)S(1)}, bf16[256,128]{1,0:T(8,128)(2,1)S(1)}, u32[]{:S(2)}, u32[]{:S(2)}) collective-permute-start(bf16[256,128]{1,0:T(8,128)(2,1)S(1)} %get-tuple-element.47), channel_id=1, source_target_pairs={{0,1},{1,0},{2,3},{3,2},{4,5},{5,4},{6,7},{7,6},{8,9},{9,8},{10,11... | collective-permute-start | bytes 196616 | tf_op jit(solution)/shard_map/ppermute | solution.py:45
  3.2 8.8 %collective-permute-start.7 = (bf16[512,128]{1,0:T(8,128)(2,1)S(1)}, bf16[512,128]{1,0:T(8,128)(2,1)S(1)}, u32[]{:S(2)}, u32[]{:S(2)}) collective-permute-start(bf16[512,128]{1,0:T(8,128)(2,1)S(1)} %pad_maximum_fusion.1), channel_id=1, source_target_pairs={{0,1},{1,0},{2,3},{3,2},{4,5},{5,4},{6,7},{7,6},{8,9},{9,8},{10,11... | collective-permute-start | bytes 393224 | tf_op jit(solution)/shard_map/ppermute | solution.py:45
  4.4 12.3 %copy-start = (bf16[1,1,128,2048]{3,2,1,0:T(8,128)(2,1)S(1)}, bf16[1,1,128,2048]{3,2,1,0:T(8,128)(2,1)}, u32[]{:S(2)}) copy-start(bf16[1,1,128,2048]{3,2,1,0:T(8,128)(2,1)} %param.12) | copy-start | bytes 1572868
  4.4 7.8 %collective-permute-start.4 = (bf16[512,128]{1,0:T(8,128)(2,1)S(1)}, bf16[512,128]{1,0:T(8,128)(2,1)S(1)}, u32[]{:S(2)}, u32[]{:S(2)}) collective-permute-start(bf16[512,128]{1,0:T(8,128)(2,1)S(1)} %shard_map.95.refs_4_.refs_2_), channel_id=1, source_target_pairs={{0,6},{1,7},{2,4},{3,5},{4,2},{5,3},{6,0},{7,1},{8,14},{9,15},{10,... | collective-permute-start | bytes 393224 | tf_op jit(solution)/shard_map/ppermute | solution.py:41
  8.2 6.7 %collective-permute-start.3 = (bf16[512,128]{1,0:T(8,128)(2,1)S(1)}, bf16[512,128]{1,0:T(8,128)(2,1)S(1)}, u32[]{:S(2)}, u32[]{:S(2)}) collective-permute-start(bf16[512,128]{1,0:T(8,128)(2,1)S(1)} %shard_map.95.refs_4_.refs_2_), channel_id=1, source_target_pairs={{0,4},{1,5},{2,6},{3,7},{4,0},{5,1},{6,2},{7,3},{8,12},{9,13},{10,... | collective-permute-start | bytes 393224 | tf_op jit(solution)/shard_map/ppermute | solution.py:41
  8.7 6.5 %collective-permute-start.2 = (bf16[512,128]{1,0:T(8,128)(2,1)S(1)}, bf16[512,128]{1,0:T(8,128)(2,1)S(1)}, u32[]{:S(2)}, u32[]{:S(2)}) collective-permute-start(bf16[512,128]{1,0:T(8,128)(2,1)S(1)} %shard_map.95.refs_4_.refs_2_), channel_id=1, source_target_pairs={{0,2},{1,3},{2,0},{3,1},{4,6},{5,7},{6,4},{7,5},{8,10},{9,11},{10,... | collective-permute-start | bytes 393224 | tf_op jit(solution)/shard_map/ppermute | solution.py:41
  10.1 0.7 %copy-start.2 = (s32[1,8]{1,0:T(1,128)S(1)}, s32[1,8]{1,0:T(1,128)}, u32[]{:S(2)}) copy-start(s32[1,8]{1,0:T(1,128)} %order.1) | copy-start | bytes 100
  15.1 7.4 %collective-permute-start.8 = (bf16[1024,128]{1,0:T(8,128)(2,1)S(1)}, bf16[1024,128]{1,0:T(8,128)(2,1)S(1)}, u32[]{:S(2)}, u32[]{:S(2)}) collective-permute-start(bf16[1024,128]{1,0:T(8,128)(2,1)S(1)} %shard_map.97.refs_0_.refs_2_.refs_6_.refs_9_), channel_id=1, source_target_pairs={{0,2},{1,5},{2,0},{3,7},{4,6},{5,1},{6,4},{7,3},{8,10},{9,13},{10,... | collective-permute-start | bytes 786440 | tf_op jit(solution)/shard_map/ppermute | solution.py:41
  17.1 5.5 %collective-permute-start.9 = (bf16[288,128]{1,0:T(8,128)(2,1)S(1)}, bf16[288,128]{1,0:T(8,128)(2,1)S(1)}, u32[]{:S(2)}, u32[]{:S(2)}) collective-permute-start(bf16[288,128]{1,0:T(8,128)(2,1)S(1)} %shard_map.98.refs_9_), channel_id=1, source_target_pairs={{0,8},{1,9},{2,10},{3,11},{4,12},{5,13},{6,14},{7,15},{8,16},{9,17... | collective-permute-start | bytes 221192 | tf_op jit(solution)/shard_map/ppermute | solution.py:41
  22.6 8.3 %collective-permute-start.10 = (bf16[1024,128]{1,0:T(8,128)(2,1)S(1)}, bf16[1024,128]{1,0:T(8,128)(2,1)S(1)}, u32[]{:S(2)}, u32[]{:S(2)}) collective-permute-start(bf16[1024,128]{1,0:T(8,128)(2,1)S(1)} %shard_map.99), channel_id=1, source_target_pairs={{0,4},{1,3},{2,6},{3,1},{4,0},{5,7},{6,2},{7,5},{8,12},{9,11},{10,... | collective-permute-start | bytes 786440 | tf_op jit(solution)/shard_map/ppermute | solution.py:41
  23.4 6.0 %collective-permute-start.11 = (bf16[288,128]{1,0:T(8,128)(2,1)S(1)}, bf16[288,128]{1,0:T(8,128)(2,1)S(1)}, u32[]{:S(2)}, u32[]{:S(2)}) collective-permute-start(bf16[288,128]{1,0:T(8,128)(2,1)S(1)} %collective-permute-done.9.refs_5_.refs_12_), channel_id=1, source_target_pairs={{0,6},{1,7},{2,4},{3,5},{4,2},{5,3},{6,0},{7,1},{8,14},{9,15},{10,... | collective-permute-start | bytes 221192 | tf_op jit(solution)/shard_map/ppermute | solution.py:41
  24.6 7.0 %collective-permute-start.14 = (bf16[288,128]{1,0:T(8,128)(2,1)S(1)}, bf16[288,128]{1,0:T(8,128)(2,1)S(1)}, u32[]{:S(2)}, u32[]{:S(2)}) collective-permute-start(bf16[288,128]{1,0:T(8,128)(2,1)S(1)} %collective-permute-done.9.refs_5_.refs_12_), channel_id=1, source_target_pairs={{0,4},{1,5},{2,6},{3,7},{4,0},{5,1},{6,2},{7,3},{8,12},{9,13},{10,... | collective-permute-start | bytes 221192 | tf_op jit(solution)/shard_map/ppermute | solution.py:41
  26.1 5.6 %collective-permute-start.13 = (bf16[288,128]{1,0:T(8,128)(2,1)S(1)}, bf16[288,128]{1,0:T(8,128)(2,1)S(1)}, u32[]{:S(2)}, u32[]{:S(2)}) collective-permute-start(bf16[288,128]{1,0:T(8,128)(2,1)S(1)} %collective-permute-done.9.refs_5_.refs_12_), channel_id=1, source_target_pairs={{0,2},{1,3},{2,0},{3,1},{4,6},{5,7},{6,4},{7,5},{8,10},{9,11},{10,... | collective-permute-start | bytes 221192 | tf_op jit(solution)/shard_map/ppermute | solution.py:41
  29.4 12.1 %collective-permute-start.12 = (bf16[1024,128]{1,0:T(8,128)(2,1)S(1)}, bf16[1024,128]{1,0:T(8,128)(2,1)S(1)}, u32[]{:S(2)}, u32[]{:S(2)}) collective-permute-start(bf16[1024,128]{1,0:T(8,128)(2,1)S(1)} %shard_map.100), channel_id=1, source_target_pairs={{0,4},{1,3},{2,6},{3,1},{4,0},{5,7},{6,2},{7,5},{8,12},{9,11},{10,... | collective-permute-start | bytes 786440 | tf_op jit(solution)/shard_map/ppermute | solution.py:41
  32.0 6.0 %collective-permute-start.15 = (bf16[288,128]{1,0:T(8,128)(2,1)S(1)}, bf16[288,128]{1,0:T(8,128)(2,1)S(1)}, u32[]{:S(2)}, u32[]{:S(2)}) collective-permute-start(bf16[288,128]{1,0:T(8,128)(2,1)S(1)} %get-tuple-element.27), channel_id=1, source_target_pairs={{0,8},{1,9},{2,10},{3,11},{4,12},{5,13},{6,14},{7,15},{8,16},{9,17... | collective-permute-start | bytes 221192 | tf_op jit(solution)/shard_map/ppermute | solution.py:41
  36.1 6.1 %collective-permute-start.20 = (bf16[544,128]{1,0:T(8,128)(2,1)S(1)}, bf16[544,128]{1,0:T(8,128)(2,1)S(1)}, u32[]{:S(2)}, u32[]{:S(2)}) collective-permute-start(bf16[544,128]{1,0:T(8,128)(2,1)S(1)} %get-tuple-element.32.refs_0_), channel_id=1, source_target_pairs={{0,2},{1,5},{2,0},{3,7},{4,6},{5,1},{6,4},{7,3},{8,10},{9,13},{10,... | collective-permute-start | bytes 417800 | tf_op jit(solution)/shard_map/ppermute | solution.py:41
  38.0 6.9 %collective-permute-start.18 = (bf16[288,128]{1,0:T(8,128)(2,1)S(1)}, bf16[288,128]{1,0:T(8,128)(2,1)S(1)}, u32[]{:S(2)}, u32[]{:S(2)}) collective-permute-start(bf16[288,128]{1,0:T(8,128)(2,1)S(1)} %collective-permute-done.15.refs_5_.refs_16_), channel_id=1, source_target_pairs={{0,6},{1,7},{2,4},{3,5},{4,2},{5,3},{6,0},{7,1},{8,14},{9,15},{10,... | collective-permute-start | bytes 221192 | tf_op jit(solution)/shard_map/ppermute | solution.py:41
  39.4 5.5 %collective-permute-start.17 = (bf16[288,128]{1,0:T(8,128)(2,1)S(1)}, bf16[288,128]{1,0:T(8,128)(2,1)S(1)}, u32[]{:S(2)}, u32[]{:S(2)}) collective-permute-start(bf16[288,128]{1,0:T(8,128)(2,1)S(1)} %collective-permute-done.15.refs_5_.refs_16_), channel_id=1, source_target_pairs={{0,4},{1,5},{2,6},{3,7},{4,0},{5,1},{6,2},{7,3},{8,12},{9,13},{10,... | collective-permute-start | bytes 221192 | tf_op jit(solution)/shard_map/ppermute | solution.py:41
  40.7 5.2 %collective-permute-start.16 = (bf16[288,128]{1,0:T(8,128)(2,1)S(1)}, bf16[288,128]{1,0:T(8,128)(2,1)S(1)}, u32[]{:S(2)}, u32[]{:S(2)}) collective-permute-start(bf16[288,128]{1,0:T(8,128)(2,1)S(1)} %collective-permute-done.15.refs_5_.refs_16_), channel_id=1, source_target_pairs={{0,2},{1,3},{2,0},{3,1},{4,6},{5,7},{6,4},{7,5},{8,10},{9,11},{10,... | collective-permute-start | bytes 221192 | tf_op jit(solution)/shard_map/ppermute | solution.py:41
  42.2 7.6 %copy-start.1 = (bf16[1,256,2048]{2,1,0:T(8,128)(2,1)S(1)}, bf16[1,256,2048]{2,1,0:T(8,128)(2,1)}, u32[]{:S(2)}) copy-start(bf16[1,256,2048]{2,1,0:T(8,128)(2,1)} %param.11) | copy-start | bytes 3145732
  42.2 9.8 %collective-permute-start.21 = (bf16[1088,128]{1,0:T(8,128)(2,1)S(1)}, bf16[1088,128]{1,0:T(8,128)(2,1)S(1)}, u32[]{:S(2)}, u32[]{:S(2)}) collective-permute-start(bf16[1088,128]{1,0:T(8,128)(2,1)S(1)} %shard_map.107), channel_id=1, source_target_pairs={{0,4},{1,3},{2,6},{3,1},{4,0},{5,7},{6,2},{7,5},{8,12},{9,11},{10,... | collective-permute-start | bytes 835592 | tf_op jit(solution)/shard_map/ppermute | solution.py:41
  46.2 6.1 %collective-permute-start.25 = (bf16[288,128]{1,0:T(8,128)(2,1)S(1)}, bf16[288,128]{1,0:T(8,128)(2,1)S(1)}, u32[]{:S(2)}, u32[]{:S(2)}) collective-permute-start(bf16[288,128]{1,0:T(8,128)(2,1)S(1)} %shard_map.104.refs_0_), channel_id=1, source_target_pairs={{0,6},{1,7},{2,4},{3,5},{4,2},{5,3},{6,0},{7,1},{8,14},{9,15},{10,... | collective-permute-start | bytes 221192 | tf_op jit(solution)/shard_map/ppermute | solution.py:41
  47.8 4.6 %collective-permute-start.24 = (bf16[288,128]{1,0:T(8,128)(2,1)S(1)}, bf16[288,128]{1,0:T(8,128)(2,1)S(1)}, u32[]{:S(2)}, u32[]{:S(2)}) collective-permute-start(bf16[288,128]{1,0:T(8,128)(2,1)S(1)} %shard_map.104.refs_0_), channel_id=1, source_target_pairs={{0,4},{1,5},{2,6},{3,7},{4,0},{5,1},{6,2},{7,3},{8,12},{9,13},{10,... | collective-permute-start | bytes 221192 | tf_op jit(solution)/shard_map/ppermute | solution.py:41
  48.8 4.4 %collective-permute-start.23 = (bf16[288,128]{1,0:T(8,128)(2,1)S(1)}, bf16[288,128]{1,0:T(8,128)(2,1)S(1)}, u32[]{:S(2)}, u32[]{:S(2)}) collective-permute-start(bf16[288,128]{1,0:T(8,128)(2,1)S(1)} %shard_map.104.refs_0_), channel_id=1, source_target_pairs={{0,2},{1,3},{2,0},{3,1},{4,6},{5,7},{6,4},{7,5},{8,10},{9,11},{10,... | collective-permute-start | bytes 221192 | tf_op jit(solution)/shard_map/ppermute | solution.py:41
  51.9 2.0 %collective-permute-start.19 = (bf16[256,384]{1,0:T(8,128)(2,1)S(1)}, bf16[256,384]{1,0:T(8,128)(2,1)S(1)}, u32[]{:S(2)}, u32[]{:S(2)}) collective-permute-start(bf16[256,384]{1,0:T(8,128)(2,1)S(1)} %get-tuple-element.30), channel_id=1, source_target_pairs={{0,1},{1,0},{2,3},{3,2},{4,5},{5,4},{6,7},{7,6},{8,9},{9,8},{10,11... | collective-permute-start | bytes 589832 | tf_op jit(solution)/shard_map/ppermute | solution.py:45
  53.4 1.5 %collective-permute-start.26 = (f32[256,128]{1,0:T(8,128)S(1)}, f32[256,128]{1,0:T(8,128)S(1)}, u32[]{:S(2)}, u32[]{:S(2)}) collective-permute-start(f32[256,128]{1,0:T(8,128)S(1)} %get-tuple-element.38), channel_id=1, source_target_pairs={{0,1},{1,0},{2,3},{3,2},{4,5},{5,4},{6,7},{7,6},{8,9},{9,8},{10,11... | collective-permute-start | bytes 393224 | tf_op jit(solution)/shard_map/ppermute | solution.py:45
  53.4 1.5 %collective-permute-start.22 = (bf16[256,256]{1,0:T(8,128)(2,1)S(1)}, bf16[256,256]{1,0:T(8,128)(2,1)S(1)}, u32[]{:S(2)}, u32[]{:S(2)}) collective-permute-start(bf16[256,256]{1,0:T(8,128)(2,1)S(1)} %get-tuple-element.35), channel_id=1, source_target_pairs={{0,1},{1,0},{2,3},{3,2},{4,5},{5,4},{6,7},{7,6},{8,9},{9,8},{10,11... | collective-permute-start | bytes 393224 | tf_op jit(solution)/shard_map/ppermute | solution.py:45

commit v5 on v4

--- a/solution.py
+++ b/solution.py
@@ -336,12 +336,14 @@
             shape(CORES * slots, half, WIDE),
         ),
         (target_row_blocks, mate_target, tile_usage_order, live_tile_count),
+        (),
+        1,
     )
     rest = [
         (panel(t) - is_first * first_updates[:, (t - 1) * PW : t * PW]).astype(NARROW)
         for t in range(1, ticks)
     ]
-    rest = after(pair_up(rest, mate, mate_inverse, marks[1]), *heads[1:])
+    rest = after(pair_up(rest, mate, mate_inverse, marks[1]), *heads[3:])
     pair_rows = CORES * height
     origins, phases = doubling(chips)
 
@@ -386,18 +388,20 @@
         block,
         (own, mate, *marks, *heads),
         [pltpu.VMEM((separator, half), NARROW)],
-        1,
+        8388608,
     )
     came, past, shared, laters = [], [], [], []
     for tick in range(1, ticks):
         past.append(product)
         arrived = hop(product, lambda core: 0, 1, ends)
+        if tick == 1:
+            arrived = stacked([(0, block_rows)], (arrived,), 8388608)
         sent = [arrived, *around(arrived)]
         came += sent
         if shared:
             shared = gather(shared[0], (arrived,))
         if tick == 1:
-            laters.append(go_on(0, arrived))
+            laters.append(go_on(0, product))
             laters += [go_on(panel, sent[-1]) for panel in range(1, ticks - 1)]
         pieces, starts = laters[tick - 1]
         ahead = call(

time: 56.1 us -> 53.8 us (0.959)
  waiting for transfers between devices: 12.2 us -> 9.08 us
  starting transfers between devices: 31.5 us -> 32.3 us
    ppermute x19, waiting for transfers between devices: 11.5 us -> 6.77 us  [hop(): return lax.ppermute(block, ('chain', 'rows'), route)]
    ppermute x8, waiting for transfers between devices: 0.72 us -> 2.31 us  [swap(): return lax.ppermute(block, 'rows', [(i, i ^ 1) for i in range(rows)])]
    ppermute x19, starting transfers between devices: 29.2 us -> 30.4 us  [hop(): return lax.ppermute(block, ('chain', 'rows'), route)]
    pallas_call x16 -> x17, Pallas kernels: 7.96 us -> 7.98 us  [call(): pl.pallas_call(kernel, out_shape=out_shape, in_specs=in_specs, out_specs=...]
  transfers between devices with their start and end apart: 27 -> 27, of which waited for: 14 -> 12; matrix products, arithmetic and copies ran while one was open for 3% -> 3% of each run, Pallas kernels for 13% -> 13%
where the time goes in v5:
time: 53.8 us; the launch traced here: 53.5 us
  starting transfers between devices  32.3 us (60%)
  waiting for transfers between devices  9.08 us (17%)
  Pallas kernels  7.98 us (15%)
  between operations  2.16 us (4%)
  other arithmetic  1.41 us (3%)
  local copies, waits for them, and re-layouts  0.64 us (1%)
    ppermute x19, starting transfers between devices, hop(): return lax.ppermute(block, ('chain', 'rows'), route)  30.4 us
    pallas_call x17, Pallas kernels, call(): pl.pallas_call(kernel, out_shape=out_shape, in_specs=in_specs, out_specs=...  7.98 us
    ppermute x19, waiting for transfers between devices, hop(): return lax.ppermute(block, ('chain', 'rows'), route)  6.77 us
    ppermute x8, waiting for transfers between devices, swap(): return lax.ppermute(block, 'rows', [(i, i ^ 1) for i in range(rows)])  2.31 us
    ppermute x8, starting transfers between devices, swap(): return lax.ppermute(block, 'rows', [(i, i ^ 1) for i in range(rows)])  1.88 us
    convert_element_type x1, other arithmetic, body(): (panel(t) - is_first * first_updates[:, (t - 1) * PW:t * PW]).astype(NARROW)  1.35 us
  transfers between devices with their start and end apart: 27, of which 12 were waited for; matrix products, arithmetic and copies ran while one was open for 3% of the time, Pallas kernels for 13%

profile of v5, /device:TPU:0, one launch (start us, length us, event | category | flops | bytes accessed | tf_op | source)
XLA Modules:
  0.0 53.5 jit_solution(17247183215239116388)
XLA Ops:
  0.6 0.5 collective-permute-start
  1.1 0.1 collective-permute-start.5
  1.2 1.3 %subtract_convert_fusion.1 = (bf16[256,256]{1,0:T(8,128)(2,1)S(1)}, bf16[256,256]{1,0:T(8,128)(2,1)S(1)}, bf16[256,256]{1,0:T(8,128)(2,1)S(1)}) fusion(f32[256,512]{1,0:T(8,128)} %param.10, f32[]{:T(128)S(6)} %convert_element_type.24, bf16[256,768]{1,0:T(8,128)(2,1)} %param.8, f32[256,256]{1,0:T(8,128)} %param.9), kind=kLoop, calls=%fused_computation.1 | loop fusion | flops 720896 | bytes 1572868 | tf_op jit(solution)/shard_map/convert_element_type | solution.py:343
  2.6 0.5 collective-permute-start.1
  3.1 0.1 collective-permute-start.7
  3.3 1.0 %collective-permute-done.1.mate = bf16[256,128]{1,0:T(8,128)(2,1)S(1)} collective-permute-done((bf16[256,128]{1,0:T(8,128)(2,1)S(1)}, bf16[256,128]{1,0:T(8,128)(2,1)S(1)}, u32[]{:S(2)}, u32[]{:S(2)}) %collective-permute-start.1) | collective-permute-done | bytes 65568 | tf_op jit(solution)/shard_map/ppermute | solution.py:45
  4.3 3.9 %collective-permute-start.4 = (bf16[512,128]{1,0:T(8,128)(2,1)S(1)}, bf16[512,128]{1,0:T(8,128)(2,1)S(1)}, u32[]{:S(2)}, u32[]{:S(2)}) collective-permute-start(bf16[512,128]{1,0:T(8,128)(2,1)S(1)} %shard_map.95.refs_4_.refs_2_), channel_id=1, source_target_pairs={{0,6},{1,7},{2,4},{3,5},{4,2},{5,3},{6,0},{7,1},{8,14},{9,15},{10,... | collective-permute-start | bytes 393224 | tf_op jit(solution)/shard_map/ppermute | solution.py:41
  8.2 1.2 %collective-permute-done.6.mate_target = s32[1,1]{1,0:T(1,128)} collective-permute-done((s32[1,1]{1,0:T(1,128)}, s32[1,1]{1,0:T(1,128)}, u32[]{:S(2)}, u32[]{:S(2)}) %collective-permute-start.6) | collective-permute-done | bytes 36 | tf_op jit(solution)/shard_map/ppermute | solution.py:45
  9.4 0.5 collective-permute-start.3
  9.9 0.1 collective-permute-start.2
  11.4 0.0 copy-start.2
  11.4 0.6 %copy-done.2 = s32[1,8]{1,0:T(1,128)S(1)} copy-done((s32[1,8]{1,0:T(1,128)S(1)}, s32[1,8]{1,0:T(1,128)}, u32[]{:S(2)}) %copy-start.2) | copy-done | bytes 56
  12.0 1.2 %shard_map.96 = (bf16[32,128]{1,0:T(8,128)(2,1)S(1)}, f32[2,128]{1,0:T(2,128)S(1)}) custom-call(s32[1,1]{1,0:T(1,128)S(6)} %copy.10.own_target, s32[1,1]{1,0:T(1,128)} %collective-permute-done.6.mate_target, s32[1,8]{1,0:T(1,128)S(1)} %copy-done.2, s32[1]{0:T(128)S(6)} %copy.11.count), custom_call_target="tpu_custom_call" | custom-call | flops 1000 | bytes 1 | tf_op jit(solution)/shard_map/pallas_call | solution.py:271
  13.3 0.0 collective-permute-done.refs_1_
  13.3 0.0 collective-permute-done.4.refs_7_.refs_5_
  13.3 2.0 %collective-permute-start.8 = (bf16[1024,128]{1,0:T(8,128)(2,1)S(1)}, bf16[1024,128]{1,0:T(8,128)(2,1)S(1)}, u32[]{:S(2)}, u32[]{:S(2)}) collective-permute-start(bf16[1024,128]{1,0:T(8,128)(2,1)S(1)} %shard_map.97.refs_0_.refs_2_.refs_6_.refs_9_), channel_id=1, source_target_pairs={{0,2},{1,5},{2,0},{3,7},{4,6},{5,1},{6,4},{7,3},{8,10},{9,13},{10,... | collective-permute-start | bytes 786440 | tf_op jit(solution)/shard_map/ppermute | solution.py:41
  15.3 0.0 collective-permute-done.3.refs_6_.refs_4_
  15.3 0.0 collective-permute-done.2.refs_5_.refs_3_
  15.3 0.5 shard_map.98.refs_9_
  15.8 3.5 %collective-permute-start.10 = (bf16[288,128]{1,0:T(8,128)(2,1)S(1)}, bf16[288,128]{1,0:T(8,128)(2,1)S(1)}, u32[]{:S(2)}, u32[]{:S(2)}) collective-permute-start(bf16[288,128]{1,0:T(8,128)(2,1)S(1)} %shard_map.98.refs_9_), channel_id=1, source_target_pairs={{0,8},{1,9},{2,10},{3,11},{4,12},{5,13},{6,14},{7,15},{8,16},{9,17... | collective-permute-start | bytes 221192 | tf_op jit(solution)/shard_map/ppermute | solution.py:41
  19.3 0.5 collective-permute-done.8.refs_1_.refs_3_.refs_7_.refs_10_
  19.8 2.0 %collective-permute-start.9 = (bf16[1024,128]{1,0:T(8,128)(2,1)S(1)}, bf16[1024,128]{1,0:T(8,128)(2,1)S(1)}, u32[]{:S(2)}, u32[]{:S(2)}) collective-permute-start(bf16[1024,128]{1,0:T(8,128)(2,1)S(1)} %shard_map.99), channel_id=1, source_target_pairs={{0,4},{1,3},{2,6},{3,1},{4,0},{5,7},{6,2},{7,5},{8,12},{9,11},{10,... | collective-permute-start | bytes 786440 | tf_op jit(solution)/shard_map/ppermute | solution.py:41
  21.8 0.0 collective-permute-done.10.refs_0_
  21.8 1.6 %collective-permute-start.11 = (bf16[288,128]{1,0:T(8,128)(2,1)S(1)}, bf16[288,128]{1,0:T(8,128)(2,1)S(1)}, u32[]{:S(2)}, u32[]{:S(2)}) collective-permute-start(bf16[288,128]{1,0:T(8,128)(2,1)S(1)} %shard_map.100.refs_5_.refs_12_), channel_id=1, source_target_pairs={{0,6},{1,7},{2,4},{3,5},{4,2},{5,3},{6,0},{7,1},{8,14},{9,15},{10,... | collective-permute-start | bytes 221192 | tf_op jit(solution)/shard_map/ppermute | solution.py:41
  23.4 1.4 %collective-permute-start.14 = (bf16[288,128]{1,0:T(8,128)(2,1)S(1)}, bf16[288,128]{1,0:T(8,128)(2,1)S(1)}, u32[]{:S(2)}, u32[]{:S(2)}) collective-permute-start(bf16[288,128]{1,0:T(8,128)(2,1)S(1)} %shard_map.100.refs_5_.refs_12_), channel_id=1, source_target_pairs={{0,4},{1,5},{2,6},{3,7},{4,0},{5,1},{6,2},{7,3},{8,12},{9,13},{10,... | collective-permute-start | bytes 221192 | tf_op jit(solution)/shard_map/ppermute | solution.py:41
  24.8 0.5 %collective-permute-start.13 = (bf16[288,128]{1,0:T(8,128)(2,1)S(1)}, bf16[288,128]{1,0:T(8,128)(2,1)S(1)}, u32[]{:S(2)}, u32[]{:S(2)}) collective-permute-start(bf16[288,128]{1,0:T(8,128)(2,1)S(1)} %shard_map.100.refs_5_.refs_12_), channel_id=1, source_target_pairs={{0,2},{1,3},{2,0},{3,1},{4,6},{5,7},{6,4},{7,5},{8,10},{9,11},{10,... | collective-permute-start | bytes 221192 | tf_op jit(solution)/shard_map/ppermute | solution.py:41
  25.3 2.5 %collective-permute-done.11.refs_8_.refs_15_ = bf16[288,128]{1,0:T(8,128)(2,1)S(1)} collective-permute-done((bf16[288,128]{1,0:T(8,128)(2,1)S(1)}, bf16[288,128]{1,0:T(8,128)(2,1)S(1)}, u32[]{:S(2)}, u32[]{:S(2)}) %collective-permute-start.11) | collective-permute-done | bytes 73760 | tf_op jit(solution)/shard_map/ppermute | solution.py:41
  27.8 0.4 collective-permute-start.12
  28.3 0.3 collective-permute-done.9.refs_4_.refs_8_
  28.6 0.5 shard_map.102.refs_4_
  29.1 0.3 collective-permute-done.14.refs_7_.refs_14_
  29.4 0.2 collective-permute-done.13.refs_6_.refs_13_
  29.6 0.4 shard_map.103
  29.9 3.7 %collective-permute-start.15 = (bf16[288,128]{1,0:T(8,128)(2,1)S(1)}, bf16[288,128]{1,0:T(8,128)(2,1)S(1)}, u32[]{:S(2)}, u32[]{:S(2)}) collective-permute-start(bf16[288,128]{1,0:T(8,128)(2,1)S(1)} %get-tuple-element.27), channel_id=1, source_target_pairs={{0,8},{1,9},{2,10},{3,11},{4,12},{5,13},{6,14},{7,15},{8,16},{9,17... | collective-permute-start | bytes 221192 | tf_op jit(solution)/shard_map/ppermute | solution.py:41
  33.6 1.6 %collective-permute-start.20 = (bf16[544,128]{1,0:T(8,128)(2,1)S(1)}, bf16[544,128]{1,0:T(8,128)(2,1)S(1)}, u32[]{:S(2)}, u32[]{:S(2)}) collective-permute-start(bf16[544,128]{1,0:T(8,128)(2,1)S(1)} %get-tuple-element.32.refs_0_), channel_id=1, source_target_pairs={{0,2},{1,5},{2,0},{3,7},{4,6},{5,1},{6,4},{7,3},{8,10},{9,13},{10,... | collective-permute-start | bytes 417800 | tf_op jit(solution)/shard_map/ppermute | solution.py:41
  35.2 0.4 collective-permute-done.15.refs_5_.refs_16_
  35.6 1.9 %collective-permute-start.18 = (bf16[288,128]{1,0:T(8,128)(2,1)S(1)}, bf16[288,128]{1,0:T(8,128)(2,1)S(1)}, u32[]{:S(2)}, u32[]{:S(2)}) collective-permute-start(bf16[288,128]{1,0:T(8,128)(2,1)S(1)} %collective-permute-done.15.refs_5_.refs_16_), channel_id=1, source_target_pairs={{0,6},{1,7},{2,4},{3,5},{4,2},{5,3},{6,0},{7,1},{8,14},{9,15},{10,... | collective-permute-start | bytes 221192 | tf_op jit(solution)/shard_map/ppermute | solution.py:41
  37.5 1.0 %collective-permute-start.17 = (bf16[288,128]{1,0:T(8,128)(2,1)S(1)}, bf16[288,128]{1,0:T(8,128)(2,1)S(1)}, u32[]{:S(2)}, u32[]{:S(2)}) collective-permute-start(bf16[288,128]{1,0:T(8,128)(2,1)S(1)} %collective-permute-done.15.refs_5_.refs_16_), channel_id=1, source_target_pairs={{0,4},{1,5},{2,6},{3,7},{4,0},{5,1},{6,2},{7,3},{8,12},{9,13},{10,... | collective-permute-start | bytes 221192 | tf_op jit(solution)/shard_map/ppermute | solution.py:41
  38.5 0.5 %collective-permute-start.16 = (bf16[288,128]{1,0:T(8,128)(2,1)S(1)}, bf16[288,128]{1,0:T(8,128)(2,1)S(1)}, u32[]{:S(2)}, u32[]{:S(2)}) collective-permute-start(bf16[288,128]{1,0:T(8,128)(2,1)S(1)} %collective-permute-done.15.refs_5_.refs_16_), channel_id=1, source_target_pairs={{0,2},{1,3},{2,0},{3,1},{4,6},{5,7},{6,4},{7,5},{8,10},{9,11},{10,... | collective-permute-start | bytes 221192 | tf_op jit(solution)/shard_map/ppermute | solution.py:41
  39.1 0.0 collective-permute-done.12.refs_4_.refs_11_
  39.1 0.5 shard_map.104.refs_4_
  39.6 0.0 collective-permute-done.20.refs_1_
  39.6 0.0 copy-start.1
  39.6 2.1 %collective-permute-start.21 = (bf16[1088,128]{1,0:T(8,128)(2,1)S(1)}, bf16[1088,128]{1,0:T(8,128)(2,1)S(1)}, u32[]{:S(2)}, u32[]{:S(2)}) collective-permute-start(bf16[1088,128]{1,0:T(8,128)(2,1)S(1)} %shard_map.108), channel_id=1, source_target_pairs={{0,4},{1,3},{2,6},{3,1},{4,0},{5,7},{6,2},{7,5},{8,12},{9,11},{10,... | collective-permute-start | bytes 835592 | tf_op jit(solution)/shard_map/ppermute | solution.py:41
  41.7 0.9 %collective-permute-done.18.refs_8_.refs_19_ = bf16[288,128]{1,0:T(8,128)(2,1)S(1)} collective-permute-done((bf16[288,128]{1,0:T(8,128)(2,1)S(1)}, bf16[288,128]{1,0:T(8,128)(2,1)S(1)}, u32[]{:S(2)}, u32[]{:S(2)}) %collective-permute-start.18) | collective-permute-done | bytes 73760 | tf_op jit(solution)/shard_map/ppermute | solution.py:41
  42.7 0.0 collective-permute-done.17.refs_7_.refs_18_
  42.7 1.1 %collective-permute-done.16.refs_6_.refs_17_ = bf16[288,128]{1,0:T(8,128)(2,1)S(1)} collective-permute-done((bf16[288,128]{1,0:T(8,128)(2,1)S(1)}, bf16[288,128]{1,0:T(8,128)(2,1)S(1)}, u32[]{:S(2)}, u32[]{:S(2)}) %collective-permute-start.16) | collective-permute-done | bytes 73760 | tf_op jit(solution)/shard_map/ppermute | solution.py:41
  43.7 0.3 shard_map.105.refs_0_
  44.1 1.6 %collective-permute-start.25 = (bf16[288,128]{1,0:T(8,128)(2,1)S(1)}, bf16[288,128]{1,0:T(8,128)(2,1)S(1)}, u32[]{:S(2)}, u32[]{:S(2)}) collective-permute-start(bf16[288,128]{1,0:T(8,128)(2,1)S(1)} %shard_map.105.refs_0_), channel_id=1, source_target_pairs={{0,6},{1,7},{2,4},{3,5},{4,2},{5,3},{6,0},{7,1},{8,14},{9,15},{10,... | collective-permute-start | bytes 221192 | tf_op jit(solution)/shard_map/ppermute | solution.py:41
  45.7 0.7 %collective-permute-start.24 = (bf16[288,128]{1,0:T(8,128)(2,1)S(1)}, bf16[288,128]{1,0:T(8,128)(2,1)S(1)}, u32[]{:S(2)}, u32[]{:S(2)}) collective-permute-start(bf16[288,128]{1,0:T(8,128)(2,1)S(1)} %shard_map.105.refs_0_), channel_id=1, source_target_pairs={{0,4},{1,5},{2,6},{3,7},{4,0},{5,1},{6,2},{7,3},{8,12},{9,13},{10,... | collective-permute-start | bytes 221192 | tf_op jit(solution)/shard_map/ppermute | solution.py:41
  46.4 1.3 %collective-permute-start.23 = (bf16[288,128]{1,0:T(8,128)(2,1)S(1)}, bf16[288,128]{1,0:T(8,128)(2,1)S(1)}, u32[]{:S(2)}, u32[]{:S(2)}) collective-permute-start(bf16[288,128]{1,0:T(8,128)(2,1)S(1)} %shard_map.105.refs_0_), channel_id=1, source_target_pairs={{0,2},{1,3},{2,0},{3,1},{4,6},{5,7},{6,4},{7,5},{8,10},{9,11},{10,... | collective-permute-start | bytes 221192 | tf_op jit(solution)/shard_map/ppermute | solution.py:41
  47.6 2.1 %shard_map.106 = (f32[256,384]{1,0:T(8,128)S(1)}, bf16[256,384]{1,0:T(8,128)(2,1)S(1)}) custom-call(bf16[256,2048]{1,0:T(8,128)(2,1)S(1)} %bitcast.9, bf16[256,2048]{1,0:T(8,128)(2,1)S(1)} %collective-permute-done.refs_1_, bf16[512,128]{1,0:T(8,128)(2,1)S(1)} %shard_map.95.refs_4_.refs_2_, bf16[512,128]{1,0:T(8,128)(2,1)S(1)} %collective-permute-done.2.refs_5_.refs_3_, ...), custom_call_target="tpu_custom_call" | custom-call | flops 1000 | bytes 1 | tf_op jit(solution)/shard_map/pallas_call | solution.py:271
  49.8 0.1 collective-permute-start.19
  49.9 0.3 shard_map.109
  50.2 0.0 collective-permute-done.24.refs_2_
  50.2 0.5 %collective-permute-done.23.refs_1_ = bf16[288,128]{1,0:T(8,128)(2,1)S(1)} collective-permute-done((bf16[288,128]{1,0:T(8,128)(2,1)S(1)}, bf16[288,128]{1,0:T(8,128)(2,1)S(1)}, u32[]{:S(2)}, u32[]{:S(2)}) %collective-permute-start.23) | collective-permute-done | bytes 73760 | tf_op jit(solution)/shard_map/ppermute | solution.py:41
  50.7 0.2 shard_map.110
  51.0 0.1 collective-permute-start.26
  51.1 0.5 collective-permute-start.22
  51.6 0.0 collective-permute-done.19.refs_1_
  51.6 0.9 %shard_map.107 = f32[256,768]{1,0:T(8,128)} custom-call(f32[256,384]{1,0:T(8,128)S(1)} %get-tuple-element.29.refs_0_, bf16[256,384]{1,0:T(8,128)(2,1)S(1)} %collective-permute-done.19.refs_1_), custom_call_target="tpu_custom_call" | custom-call | flops 1000 | bytes 1 | tf_op jit(solution)/shard_map/pallas_call | solution.py:271
  52.5 0.0 collective-permute-done.26.refs_3_
  52.5 0.1 collective-permute-done.22.refs_1_
  52.6 0.9 %shard_map.111 = f32[256,768]{1,0:T(8,128)} custom-call(f32[256,256]{1,0:T(8,128)S(1)} %get-tuple-element.34.refs_0_, bf16[256,256]{1,0:T(8,128)(2,1)S(1)} %collective-permute-done.22.refs_1_, f32[256,128]{1,0:T(8,128)S(1)} %get-tuple-element.37.refs_2_, f32[256,128]{1,0:T(8,128)S(1)} %collective-permute-done.26.refs_3_), custom_call_target="tpu_custom_call" | custom-call | flops 1000 | bytes 1 | tf_op jit(solution)/shard_map/pallas_call | solution.py:271
  (18 shorter events, 0.2 us)
Async XLA Ops:
  0.6 12.6 %collective-permute-start = (bf16[256,2048]{1,0:T(8,128)(2,1)}, bf16[256,2048]{1,0:T(8,128)(2,1)S(1)}, u32[]{:S(2)}, u32[]{:S(2)}) collective-permute-start(bf16[256,2048]{1,0:T(8,128)(2,1)} %bitcast.8), channel_id=1, source_target_pairs={{0,1},{1,0},{2,3},{3,2},{4,5},{5,4},{6,7},{7,6},{8,9},{9,8},{10,11... | collective-permute-start | bytes 3145736 | tf_op jit(solution)/shard_map/ppermute | solution.py:45
  1.1 8.8 %collective-permute-start.5 = (bf16[128,2048]{1,0:T(8,128)(2,1)}, bf16[128,2048]{1,0:T(8,128)(2,1)S(1)}, u32[]{:S(2)}, u32[]{:S(2)}) collective-permute-start(bf16[128,2048]{1,0:T(8,128)(2,1)} %bitcast.2), channel_id=1, source_target_pairs={{0,1},{1,0},{2,3},{3,2},{4,5},{5,4},{6,7},{7,6},{8,9},{9,8},{10,11... | collective-permute-start | bytes 1572872 | tf_op jit(solution)/shard_map/ppermute | solution.py:45
  2.6 1.7 %collective-permute-start.1 = (bf16[256,128]{1,0:T(8,128)(2,1)S(1)}, bf16[256,128]{1,0:T(8,128)(2,1)S(1)}, u32[]{:S(2)}, u32[]{:S(2)}) collective-permute-start(bf16[256,128]{1,0:T(8,128)(2,1)S(1)} %get-tuple-element.47), channel_id=1, source_target_pairs={{0,1},{1,0},{2,3},{3,2},{4,5},{5,4},{6,7},{7,6},{8,9},{9,8},{10,11... | collective-permute-start | bytes 196616 | tf_op jit(solution)/shard_map/ppermute | solution.py:45
  3.1 10.1 %collective-permute-start.7 = (bf16[512,128]{1,0:T(8,128)(2,1)S(1)}, bf16[512,128]{1,0:T(8,128)(2,1)S(1)}, u32[]{:S(2)}, u32[]{:S(2)}) collective-permute-start(bf16[512,128]{1,0:T(8,128)(2,1)S(1)} %pad_maximum_fusion.1), channel_id=1, source_target_pairs={{0,1},{1,0},{2,3},{3,2},{4,5},{5,4},{6,7},{7,6},{8,9},{9,8},{10,11... | collective-permute-start | bytes 393224 | tf_op jit(solution)/shard_map/ppermute | solution.py:45
  4.3 11.0 %copy-start = (bf16[1,1,128,2048]{3,2,1,0:T(8,128)(2,1)S(1)}, bf16[1,1,128,2048]{3,2,1,0:T(8,128)(2,1)}, u32[]{:S(2)}) copy-start(bf16[1,1,128,2048]{3,2,1,0:T(8,128)(2,1)} %param.12) | copy-start | bytes 1572868
  4.3 9.0 %collective-permute-start.4 = (bf16[512,128]{1,0:T(8,128)(2,1)S(1)}, bf16[512,128]{1,0:T(8,128)(2,1)S(1)}, u32[]{:S(2)}, u32[]{:S(2)}) collective-permute-start(bf16[512,128]{1,0:T(8,128)(2,1)S(1)} %shard_map.95.refs_4_.refs_2_), channel_id=1, source_target_pairs={{0,6},{1,7},{2,4},{3,5},{4,2},{5,3},{6,0},{7,1},{8,14},{9,15},{10,... | collective-permute-start | bytes 393224 | tf_op jit(solution)/shard_map/ppermute | solution.py:41
  8.2 1.2 %collective-permute-start.6 = (s32[1,1]{1,0:T(1,128)}, s32[1,1]{1,0:T(1,128)}, u32[]{:S(2)}, u32[]{:S(2)}) collective-permute-start(s32[1,1]{1,0:T(1,128)} %param.13), channel_id=1, source_target_pairs={{0,1},{1,0},{2,3},{3,2},{4,5},{5,4},{6,7},{7,6},{8,9},{9,8},{10,11... | collective-permute-start | bytes 20 | tf_op jit(solution)/shard_map/ppermute | solution.py:45
  9.4 5.9 %collective-permute-start.3 = (bf16[512,128]{1,0:T(8,128)(2,1)S(1)}, bf16[512,128]{1,0:T(8,128)(2,1)S(1)}, u32[]{:S(2)}, u32[]{:S(2)}) collective-permute-start(bf16[512,128]{1,0:T(8,128)(2,1)S(1)} %shard_map.95.refs_4_.refs_2_), channel_id=1, source_target_pairs={{0,4},{1,5},{2,6},{3,7},{4,0},{5,1},{6,2},{7,3},{8,12},{9,13},{10,... | collective-permute-start | bytes 393224 | tf_op jit(solution)/shard_map/ppermute | solution.py:41
  9.9 5.4 %collective-permute-start.2 = (bf16[512,128]{1,0:T(8,128)(2,1)S(1)}, bf16[512,128]{1,0:T(8,128)(2,1)S(1)}, u32[]{:S(2)}, u32[]{:S(2)}) collective-permute-start(bf16[512,128]{1,0:T(8,128)(2,1)S(1)} %shard_map.95.refs_4_.refs_2_), channel_id=1, source_target_pairs={{0,2},{1,3},{2,0},{3,1},{4,6},{5,7},{6,4},{7,5},{8,10},{9,11},{10,... | collective-permute-start | bytes 393224 | tf_op jit(solution)/shard_map/ppermute | solution.py:41
  11.4 0.7 %copy-start.2 = (s32[1,8]{1,0:T(1,128)S(1)}, s32[1,8]{1,0:T(1,128)}, u32[]{:S(2)}) copy-start(s32[1,8]{1,0:T(1,128)} %order.1) | copy-start | bytes 100
  13.3 6.4 %collective-permute-start.8 = (bf16[1024,128]{1,0:T(8,128)(2,1)S(1)}, bf16[1024,128]{1,0:T(8,128)(2,1)S(1)}, u32[]{:S(2)}, u32[]{:S(2)}) collective-permute-start(bf16[1024,128]{1,0:T(8,128)(2,1)S(1)} %shard_map.97.refs_0_.refs_2_.refs_6_.refs_9_), channel_id=1, source_target_pairs={{0,2},{1,5},{2,0},{3,7},{4,6},{5,1},{6,4},{7,3},{8,10},{9,13},{10,... | collective-permute-start | bytes 786440 | tf_op jit(solution)/shard_map/ppermute | solution.py:41
  15.8 6.0 %collective-permute-start.10 = (bf16[288,128]{1,0:T(8,128)(2,1)S(1)}, bf16[288,128]{1,0:T(8,128)(2,1)S(1)}, u32[]{:S(2)}, u32[]{:S(2)}) collective-permute-start(bf16[288,128]{1,0:T(8,128)(2,1)S(1)} %shard_map.98.refs_9_), channel_id=1, source_target_pairs={{0,8},{1,9},{2,10},{3,11},{4,12},{5,13},{6,14},{7,15},{8,16},{9,17... | collective-permute-start | bytes 221192 | tf_op jit(solution)/shard_map/ppermute | solution.py:41
  19.8 8.8 %collective-permute-start.9 = (bf16[1024,128]{1,0:T(8,128)(2,1)S(1)}, bf16[1024,128]{1,0:T(8,128)(2,1)S(1)}, u32[]{:S(2)}, u32[]{:S(2)}) collective-permute-start(bf16[1024,128]{1,0:T(8,128)(2,1)S(1)} %shard_map.99), channel_id=1, source_target_pairs={{0,4},{1,3},{2,6},{3,1},{4,0},{5,7},{6,2},{7,5},{8,12},{9,11},{10,... | collective-permute-start | bytes 786440 | tf_op jit(solution)/shard_map/ppermute | solution.py:41
  21.8 6.0 %collective-permute-start.11 = (bf16[288,128]{1,0:T(8,128)(2,1)S(1)}, bf16[288,128]{1,0:T(8,128)(2,1)S(1)}, u32[]{:S(2)}, u32[]{:S(2)}) collective-permute-start(bf16[288,128]{1,0:T(8,128)(2,1)S(1)} %shard_map.100.refs_5_.refs_12_), channel_id=1, source_target_pairs={{0,6},{1,7},{2,4},{3,5},{4,2},{5,3},{6,0},{7,1},{8,14},{9,15},{10,... | collective-permute-start | bytes 221192 | tf_op jit(solution)/shard_map/ppermute | solution.py:41
  23.4 6.0 %collective-permute-start.14 = (bf16[288,128]{1,0:T(8,128)(2,1)S(1)}, bf16[288,128]{1,0:T(8,128)(2,1)S(1)}, u32[]{:S(2)}, u32[]{:S(2)}) collective-permute-start(bf16[288,128]{1,0:T(8,128)(2,1)S(1)} %shard_map.100.refs_5_.refs_12_), channel_id=1, source_target_pairs={{0,4},{1,5},{2,6},{3,7},{4,0},{5,1},{6,2},{7,3},{8,12},{9,13},{10,... | collective-permute-start | bytes 221192 | tf_op jit(solution)/shard_map/ppermute | solution.py:41
  24.8 4.8 %collective-permute-start.13 = (bf16[288,128]{1,0:T(8,128)(2,1)S(1)}, bf16[288,128]{1,0:T(8,128)(2,1)S(1)}, u32[]{:S(2)}, u32[]{:S(2)}) collective-permute-start(bf16[288,128]{1,0:T(8,128)(2,1)S(1)} %shard_map.100.refs_5_.refs_12_), channel_id=1, source_target_pairs={{0,2},{1,3},{2,0},{3,1},{4,6},{5,7},{6,4},{7,5},{8,10},{9,11},{10,... | collective-permute-start | bytes 221192 | tf_op jit(solution)/shard_map/ppermute | solution.py:41
  27.8 11.2 %collective-permute-start.12 = (bf16[1024,128]{1,0:T(8,128)(2,1)S(1)}, bf16[1024,128]{1,0:T(8,128)(2,1)S(1)}, u32[]{:S(2)}, u32[]{:S(2)}) collective-permute-start(bf16[1024,128]{1,0:T(8,128)(2,1)S(1)} %shard_map.101), channel_id=1, source_target_pairs={{0,4},{1,3},{2,6},{3,1},{4,0},{5,7},{6,2},{7,5},{8,12},{9,11},{10,... | collective-permute-start | bytes 786440 | tf_op jit(solution)/shard_map/ppermute | solution.py:41
  29.9 5.7 %collective-permute-start.15 = (bf16[288,128]{1,0:T(8,128)(2,1)S(1)}, bf16[288,128]{1,0:T(8,128)(2,1)S(1)}, u32[]{:S(2)}, u32[]{:S(2)}) collective-permute-start(bf16[288,128]{1,0:T(8,128)(2,1)S(1)} %get-tuple-element.27), channel_id=1, source_target_pairs={{0,8},{1,9},{2,10},{3,11},{4,12},{5,13},{6,14},{7,15},{8,16},{9,17... | collective-permute-start | bytes 221192 | tf_op jit(solution)/shard_map/ppermute | solution.py:41
  33.6 5.9 %collective-permute-start.20 = (bf16[544,128]{1,0:T(8,128)(2,1)S(1)}, bf16[544,128]{1,0:T(8,128)(2,1)S(1)}, u32[]{:S(2)}, u32[]{:S(2)}) collective-permute-start(bf16[544,128]{1,0:T(8,128)(2,1)S(1)} %get-tuple-element.32.refs_0_), channel_id=1, source_target_pairs={{0,2},{1,5},{2,0},{3,7},{4,6},{5,1},{6,4},{7,3},{8,10},{9,13},{10,... | collective-permute-start | bytes 417800 | tf_op jit(solution)/shard_map/ppermute | solution.py:41
  35.6 7.1 %collective-permute-start.18 = (bf16[288,128]{1,0:T(8,128)(2,1)S(1)}, bf16[288,128]{1,0:T(8,128)(2,1)S(1)}, u32[]{:S(2)}, u32[]{:S(2)}) collective-permute-start(bf16[288,128]{1,0:T(8,128)(2,1)S(1)} %collective-permute-done.15.refs_5_.refs_16_), channel_id=1, source_target_pairs={{0,6},{1,7},{2,4},{3,5},{4,2},{5,3},{6,0},{7,1},{8,14},{9,15},{10,... | collective-permute-start | bytes 221192 | tf_op jit(solution)/shard_map/ppermute | solution.py:41
  37.5 5.1 %collective-permute-start.17 = (bf16[288,128]{1,0:T(8,128)(2,1)S(1)}, bf16[288,128]{1,0:T(8,128)(2,1)S(1)}, u32[]{:S(2)}, u32[]{:S(2)}) collective-permute-start(bf16[288,128]{1,0:T(8,128)(2,1)S(1)} %collective-permute-done.15.refs_5_.refs_16_), channel_id=1, source_target_pairs={{0,4},{1,5},{2,6},{3,7},{4,0},{5,1},{6,2},{7,3},{8,12},{9,13},{10,... | collective-permute-start | bytes 221192 | tf_op jit(solution)/shard_map/ppermute | solution.py:41
  38.5 5.2 %collective-permute-start.16 = (bf16[288,128]{1,0:T(8,128)(2,1)S(1)}, bf16[288,128]{1,0:T(8,128)(2,1)S(1)}, u32[]{:S(2)}, u32[]{:S(2)}) collective-permute-start(bf16[288,128]{1,0:T(8,128)(2,1)S(1)} %collective-permute-done.15.refs_5_.refs_16_), channel_id=1, source_target_pairs={{0,2},{1,3},{2,0},{3,1},{4,6},{5,7},{6,4},{7,5},{8,10},{9,11},{10,... | collective-permute-start | bytes 221192 | tf_op jit(solution)/shard_map/ppermute | solution.py:41
  39.6 8.1 %copy-start.1 = (bf16[1,256,2048]{2,1,0:T(8,128)(2,1)S(1)}, bf16[1,256,2048]{2,1,0:T(8,128)(2,1)}, u32[]{:S(2)}) copy-start(bf16[1,256,2048]{2,1,0:T(8,128)(2,1)} %param.11) | copy-start | bytes 3145732
  39.6 10.2 %collective-permute-start.21 = (bf16[1088,128]{1,0:T(8,128)(2,1)S(1)}, bf16[1088,128]{1,0:T(8,128)(2,1)S(1)}, u32[]{:S(2)}, u32[]{:S(2)}) collective-permute-start(bf16[1088,128]{1,0:T(8,128)(2,1)S(1)} %shard_map.108), channel_id=1, source_target_pairs={{0,4},{1,3},{2,6},{3,1},{4,0},{5,7},{6,2},{7,5},{8,12},{9,11},{10,... | collective-permute-start | bytes 835592 | tf_op jit(solution)/shard_map/ppermute | solution.py:41
  44.1 6.1 %collective-permute-start.25 = (bf16[288,128]{1,0:T(8,128)(2,1)S(1)}, bf16[288,128]{1,0:T(8,128)(2,1)S(1)}, u32[]{:S(2)}, u32[]{:S(2)}) collective-permute-start(bf16[288,128]{1,0:T(8,128)(2,1)S(1)} %shard_map.105.refs_0_), channel_id=1, source_target_pairs={{0,6},{1,7},{2,4},{3,5},{4,2},{5,3},{6,0},{7,1},{8,14},{9,15},{10,... | collective-permute-start | bytes 221192 | tf_op jit(solution)/shard_map/ppermute | solution.py:41
  45.7 4.5 %collective-permute-start.24 = (bf16[288,128]{1,0:T(8,128)(2,1)S(1)}, bf16[288,128]{1,0:T(8,128)(2,1)S(1)}, u32[]{:S(2)}, u32[]{:S(2)}) collective-permute-start(bf16[288,128]{1,0:T(8,128)(2,1)S(1)} %shard_map.105.refs_0_), channel_id=1, source_target_pairs={{0,4},{1,5},{2,6},{3,7},{4,0},{5,1},{6,2},{7,3},{8,12},{9,13},{10,... | collective-permute-start | bytes 221192 | tf_op jit(solution)/shard_map/ppermute | solution.py:41
  46.4 4.4 %collective-permute-start.23 = (bf16[288,128]{1,0:T(8,128)(2,1)S(1)}, bf16[288,128]{1,0:T(8,128)(2,1)S(1)}, u32[]{:S(2)}, u32[]{:S(2)}) collective-permute-start(bf16[288,128]{1,0:T(8,128)(2,1)S(1)} %shard_map.105.refs_0_), channel_id=1, source_target_pairs={{0,2},{1,3},{2,0},{3,1},{4,6},{5,7},{6,4},{7,5},{8,10},{9,11},{10,... | collective-permute-start | bytes 221192 | tf_op jit(solution)/shard_map/ppermute | solution.py:41
  49.8 1.8 %collective-permute-start.19 = (bf16[256,384]{1,0:T(8,128)(2,1)S(1)}, bf16[256,384]{1,0:T(8,128)(2,1)S(1)}, u32[]{:S(2)}, u32[]{:S(2)}) collective-permute-start(bf16[256,384]{1,0:T(8,128)(2,1)S(1)} %get-tuple-element.30), channel_id=1, source_target_pairs={{0,1},{1,0},{2,3},{3,2},{4,5},{5,4},{6,7},{7,6},{8,9},{9,8},{10,11... | collective-permute-start | bytes 589832 | tf_op jit(solution)/shard_map/ppermute | solution.py:45
  51.0 1.5 %collective-permute-start.26 = (f32[256,128]{1,0:T(8,128)S(1)}, f32[256,128]{1,0:T(8,128)S(1)}, u32[]{:S(2)}, u32[]{:S(2)}) collective-permute-start(f32[256,128]{1,0:T(8,128)S(1)} %get-tuple-element.38), channel_id=1, source_target_pairs={{0,1},{1,0},{2,3},{3,2},{4,5},{5,4},{6,7},{7,6},{8,9},{9,8},{10,11... | collective-permute-start | bytes 393224 | tf_op jit(solution)/shard_map/ppermute | solution.py:45
  51.1 1.5 %collective-permute-start.22 = (bf16[256,256]{1,0:T(8,128)(2,1)S(1)}, bf16[256,256]{1,0:T(8,128)(2,1)S(1)}, u32[]{:S(2)}, u32[]{:S(2)}) collective-permute-start(bf16[256,256]{1,0:T(8,128)(2,1)S(1)} %get-tuple-element.35), channel_id=1, source_target_pairs={{0,1},{1,0},{2,3},{3,2},{4,5},{5,4},{6,7},{7,6},{8,9},{9,8},{10,11... | collective-permute-start | bytes 393224 | tf_op jit(solution)/shard_map/ppermute | solution.py:45

commit v6 on v5

--- a/solution.py
+++ b/solution.py
@@ -12,6 +12,7 @@
 CORES = 2
 WIDE = jnp.float32
 NARROW = jnp.bfloat16
+LITTLE, SOME, LONG = 1 << 20, 4 << 20, 8 << 20
 
 
 def partner(chip, offset, chips):
@@ -154,13 +155,13 @@
         first += size
 
 
-def first_kernel(chips, tile, *refs):
-    own, mate, notes, alive = refs[:4]
-    pieces, out, whole = refs[4:-2], refs[-2], refs[-1]
-    lay_pairs(whole, slice(0, whole.shape[1]), pieces, straight(chips), chips)
+def lay_kernel(chips, *refs):
+    lay_pairs(refs[-1], slice(0, refs[-1].shape[1]), refs[:-1], straight(chips), chips)
+
+
+def first_kernel(tile, own, mate, notes, alive, whole, out):
     tiles = jnp.concatenate([own[...], mate[...]], axis=0)
-    products = multiply(tiles, whole[...])
-    write_tiles(out, products, notes, alive, tile)
+    write_tiles(out, multiply(tiles, whole[...]), notes, alive, tile)
 
 
 def ahead_kernel(chips, origins, starts, *refs):
@@ -263,7 +264,7 @@
             tick += 1
 
 
-def call(kernel, out_shape, args, scratch=(), moved=1):
+def call(kernel, out_shape, args, scratch=(), weight=1):
     in_specs = [
         pl.BlockSpec(memory_space=pltpu.SMEM if a.dtype == jnp.int32 else pltpu.VMEM)
         for a in args
@@ -275,7 +276,7 @@
         out_specs=jax.tree.map(lambda _: pl.BlockSpec(memory_space=pltpu.VMEM), out_shape),
         scratch_shapes=list(scratch),
         compiler_params=pltpu.CompilerParams(vmem_limit_bytes=40 * 1024 * 1024),
-        cost_estimate=pl.CostEstimate(flops=moved * 1000, bytes_accessed=moved, transcendentals=0),
+        cost_estimate=pl.CostEstimate(flops=weight * 1000, bytes_accessed=weight, transcendentals=0),
     )(*args)
 
 
@@ -336,24 +337,22 @@
             shape(CORES * slots, half, WIDE),
         ),
         (target_row_blocks, mate_target, tile_usage_order, live_tile_count),
-        (),
-        1,
     )
     rest = [
         (panel(t) - is_first * first_updates[:, (t - 1) * PW : t * PW]).astype(NARROW)
         for t in range(1, ticks)
     ]
-    rest = after(pair_up(rest, mate, mate_inverse, marks[1]), *heads[3:])
+    rest = after(pair_up(rest, marks[1]), *heads[3:])
     pair_rows = CORES * height
     origins, phases = doubling(chips)
 
     def phase(block, index):
         return hop(block, lambda core: phases[index][core], 0, ends)
 
-    def stacked(parts, args, moved=1):
+    def stacked(parts, args, weight=1):
         rows_in_all = sum(size for _, size in parts)
         kernel = functools.partial(stack_kernel, parts)
-        return call(kernel, shape(rows_in_all, half, NARROW), args, (), moved)
+        return call(kernel, shape(rows_in_all, half, NARROW), args, (), weight)
 
     begun = phase(rest, 0)
 
@@ -383,19 +382,26 @@
     block_rows = CORES * slots * (tile + NOTE)
     block = shape(block_rows, half, NARROW)
     tile_rows = CORES * slots * tile
+    whole = call(
+        functools.partial(lay_kernel, chips),
+        shape(separator, half, NARROW),
+        tuple(heads),
+        (),
+        LONG,
+    )
     product = call(
-        functools.partial(first_kernel, chips, tile),
+        functools.partial(first_kernel, tile),
         block,
-        (own, mate, *marks, *heads),
-        [pltpu.VMEM((separator, half), NARROW)],
-        8388608,
+        (after(own, mate_inverse), mate, *marks, whole),
+        (),
+        LONG,
     )
     came, past, shared, laters = [], [], [], []
     for tick in range(1, ticks):
         past.append(product)
         arrived = hop(product, lambda core: 0, 1, ends)
         if tick == 1:
-            arrived = stacked([(0, block_rows)], (arrived,), 8388608)
+            arrived = stacked([(0, block_rows)], (arrived,), LONG)
         sent = [arrived, *around(arrived)]
         came += sent
         if shared:
@@ -417,7 +423,7 @@
             (block, history) if earlier else (block,),
             (own, mate, *marks, ahead, *sent, *earlier),
             (),
-            1048576 if tick == 1 else 4194304,
+            LITTLE if tick == 1 else SOME,
         )
         if tick == ticks - 2:
             shared = history
@@ -432,23 +438,21 @@
         (shape(height, ticks * half, WIDE), shape(height, ticks * half, NARROW)),
         (inverse, mate_inverse, *columns_of, *came[:-1], after(came[-1], product)),
         [pltpu.VMEM((separator, ticks * half), NARROW)],
-        1,
     )
     out = shape(height, ticks * PW, WIDE)
     solved = call(join_kernel, out, (mine, swap(other, rows)))
 
-    def add_up(count, blocks, kind, moved=1):
+    def add_up(count, blocks, kind):
         mine, other = call(
             functools.partial(update_kernel, tile, count, CORES * slots),
             (shape(height, count * half, WIDE), shape(height, count * half, kind)),
             tuple(blocks),
             [pltpu.VMEM((CORES * height, count * half), WIDE)],
-            moved,
         )
         return mine, swap(other, rows)
 
     early = add_up(ticks - 1, [after(shared[0], product), *shared[1:]], NARROW)
-    passed = (*early, *add_up(1, [after(product, early[0]), *last[1:]], WIDE, 1))
+    passed = (*early, *add_up(1, [after(product, early[0]), *last[1:]], WIDE))
     passed = call(join_kernel, out, passed[:-1] + (after(passed[-1], solved),))
     return solved, passed
 

time: 53.8 us -> 53.4 us (level)
  starting transfers between devices: 32.3 us -> 31.5 us
    ppermute x19, waiting for transfers between devices: 6.77 us -> 8.05 us  [hop(): return lax.ppermute(block, ('chain', 'rows'), route)]
    ppermute x8, waiting for transfers between devices: 2.31 us -> 1.33 us  [swap(): return lax.ppermute(block, 'rows', [(i, i ^ 1) for i in range(rows)])]
    ppermute x19, starting transfers between devices: 30.4 us -> 29.6 us  [hop(): return lax.ppermute(block, ('chain', 'rows'), route)]
    pallas_call x17 -> x18, Pallas kernels: 7.98 us -> 8 us  [call(): pl.pallas_call(kernel, out_shape=out_shape, in_specs=in_specs, out_specs=...]
where the time goes in v6:
time: 53.4 us; the launch traced here: 53.2 us
  starting transfers between devices  31.5 us (59%)
  waiting for transfers between devices  9.38 us (18%)
  Pallas kernels  8 us (15%)
  between operations  2.2 us (4%)
  other arithmetic  1.41 us (3%)
  local copies, waits for them, and re-layouts  0.64 us (1%)
    ppermute x19, starting transfers between devices, hop(): return lax.ppermute(block, ('chain', 'rows'), route)  29.6 us
    ppermute x19, waiting for transfers between devices, hop(): return lax.ppermute(block, ('chain', 'rows'), route)  8.05 us
    pallas_call x18, Pallas kernels, call(): pl.pallas_call(kernel, out_shape=out_shape, in_specs=in_specs, out_specs=...  8 us
    ppermute x8, starting transfers between devices, swap(): return lax.ppermute(block, 'rows', [(i, i ^ 1) for i in range(rows)])  1.94 us
    convert_element_type x1, other arithmetic, body(): (panel(t) - is_first * first_updates[:, (t - 1) * PW:t * PW]).astype(NARROW)  1.35 us
    ppermute x8, waiting for transfers between devices, swap(): return lax.ppermute(block, 'rows', [(i, i ^ 1) for i in range(rows)])  1.33 us
  transfers between devices with their start and end apart: 27, of which 12 were waited for; matrix products, arithmetic and copies ran while one was open for 3% of the time, Pallas kernels for 13%

profile of v6, /device:TPU:0, one launch (start us, length us, event | category | flops | bytes accessed | tf_op | source)
XLA Modules:
  0.0 53.2 jit_solution(177735425874907257)
XLA Ops:
  0.6 0.5 collective-permute-start
  1.1 1.3 %subtract_convert_fusion.1 = (bf16[256,256]{1,0:T(8,128)(2,1)S(1)}, bf16[256,256]{1,0:T(8,128)(2,1)S(1)}, bf16[256,256]{1,0:T(8,128)(2,1)S(1)}) fusion(f32[256,512]{1,0:T(8,128)} %param.10, f32[]{:T(128)S(6)} %convert_element_type.24, bf16[256,768]{1,0:T(8,128)(2,1)} %param.8, f32[256,256]{1,0:T(8,128)} %param.9), kind=kLoop, calls=%fused_computation.1 | loop fusion | flops 720896 | bytes 1572868 | tf_op jit(solution)/shard_map/convert_element_type | solution.py:342
  2.5 0.1 collective-permute-start.1
  2.7 0.0 copy-start
  2.7 0.5 collective-permute-start.6
  3.2 0.6 %collective-permute-done.1.mate = bf16[256,128]{1,0:T(8,128)(2,1)S(1)} collective-permute-done((bf16[256,128]{1,0:T(8,128)(2,1)S(1)}, bf16[256,128]{1,0:T(8,128)(2,1)S(1)}, u32[]{:S(2)}, u32[]{:S(2)}) %collective-permute-start.1) | collective-permute-done | bytes 65568 | tf_op jit(solution)/shard_map/ppermute | solution.py:46
  3.9 3.7 %collective-permute-start.4 = (bf16[512,128]{1,0:T(8,128)(2,1)S(1)}, bf16[512,128]{1,0:T(8,128)(2,1)S(1)}, u32[]{:S(2)}, u32[]{:S(2)}) collective-permute-start(bf16[512,128]{1,0:T(8,128)(2,1)S(1)} %shard_map.95.refs_0_.refs_2_), channel_id=1, source_target_pairs={{0,6},{1,7},{2,4},{3,5},{4,2},{5,3},{6,0},{7,1},{8,14},{9,15},{10,... | collective-permute-start | bytes 393224 | tf_op jit(solution)/shard_map/ppermute | solution.py:42
  7.5 0.1 collective-permute-start.5
  7.6 0.5 %collective-permute-start.2 = (bf16[512,128]{1,0:T(8,128)(2,1)S(1)}, bf16[512,128]{1,0:T(8,128)(2,1)S(1)}, u32[]{:S(2)}, u32[]{:S(2)}) collective-permute-start(bf16[512,128]{1,0:T(8,128)(2,1)S(1)} %shard_map.95.refs_0_.refs_2_), channel_id=1, source_target_pairs={{0,2},{1,3},{2,0},{3,1},{4,6},{5,7},{6,4},{7,5},{8,10},{9,11},{10,... | collective-permute-start | bytes 393224 | tf_op jit(solution)/shard_map/ppermute | solution.py:42
  8.1 0.6 %collective-permute-done.5.mate_target = s32[1,1]{1,0:T(1,128)} collective-permute-done((s32[1,1]{1,0:T(1,128)}, s32[1,1]{1,0:T(1,128)}, u32[]{:S(2)}, u32[]{:S(2)}) %collective-permute-start.5) | collective-permute-done | bytes 36 | tf_op jit(solution)/shard_map/ppermute | solution.py:46
  8.8 0.5 collective-permute-start.3
  10.6 0.0 copy-start.2
  10.6 0.6 %copy-done.2 = s32[1,8]{1,0:T(1,128)S(1)} copy-done((s32[1,8]{1,0:T(1,128)S(1)}, s32[1,8]{1,0:T(1,128)}, u32[]{:S(2)}) %copy-start.2) | copy-done | bytes 56
  11.2 1.2 %shard_map.96 = (bf16[32,128]{1,0:T(8,128)(2,1)S(1)}, f32[2,128]{1,0:T(2,128)S(1)}) custom-call(s32[1,1]{1,0:T(1,128)S(6)} %copy.10.own_target, s32[1,1]{1,0:T(1,128)} %collective-permute-done.5.mate_target, s32[1,8]{1,0:T(1,128)S(1)} %copy-done.2, s32[1]{0:T(128)S(6)} %copy.11.count), custom_call_target="tpu_custom_call" | custom-call | flops 1000 | bytes 1 | tf_op jit(solution)/shard_map/pallas_call | solution.py:272
  12.5 0.1 collective-permute-start.8
  12.6 0.0 collective-permute-done.4.refs_3_.refs_5_
  12.6 1.2 %collective-permute-start.7 = (bf16[1024,128]{1,0:T(8,128)(2,1)S(1)}, bf16[1024,128]{1,0:T(8,128)(2,1)S(1)}, u32[]{:S(2)}, u32[]{:S(2)}) collective-permute-start(bf16[1024,128]{1,0:T(8,128)(2,1)S(1)} %shard_map.97.refs_0_.refs_2_.refs_6_.refs_9_), channel_id=1, source_target_pairs={{0,2},{1,5},{2,0},{3,7},{4,6},{5,1},{6,4},{7,3},{8,10},{9,13},{10,... | collective-permute-start | bytes 786440 | tf_op jit(solution)/shard_map/ppermute | solution.py:42
  13.8 0.8 %collective-permute-done.2.refs_1_.refs_3_ = bf16[512,128]{1,0:T(8,128)(2,1)S(1)} collective-permute-done((bf16[512,128]{1,0:T(8,128)(2,1)S(1)}, bf16[512,128]{1,0:T(8,128)(2,1)S(1)}, u32[]{:S(2)}, u32[]{:S(2)}) %collective-permute-start.2) | collective-permute-done | bytes 131104 | tf_op jit(solution)/shard_map/ppermute | solution.py:42
  14.6 0.0 collective-permute-done.3.refs_2_.refs_4_
  14.6 0.0 collective-permute-done.refs_1_
  14.7 0.0 collective-permute-done.8.mate.refs_1_
  14.7 0.4 shard_map.99.refs_9_
  15.1 3.6 %collective-permute-start.10 = (bf16[288,128]{1,0:T(8,128)(2,1)S(1)}, bf16[288,128]{1,0:T(8,128)(2,1)S(1)}, u32[]{:S(2)}, u32[]{:S(2)}) collective-permute-start(bf16[288,128]{1,0:T(8,128)(2,1)S(1)} %shard_map.99.refs_9_), channel_id=1, source_target_pairs={{0,8},{1,9},{2,10},{3,11},{4,12},{5,13},{6,14},{7,15},{8,16},{9,17... | collective-permute-start | bytes 221192 | tf_op jit(solution)/shard_map/ppermute | solution.py:42
  18.7 0.3 collective-permute-done.7.refs_1_.refs_3_.refs_7_.refs_10_
  19.1 1.6 %collective-permute-start.9 = (bf16[1024,128]{1,0:T(8,128)(2,1)S(1)}, bf16[1024,128]{1,0:T(8,128)(2,1)S(1)}, u32[]{:S(2)}, u32[]{:S(2)}) collective-permute-start(bf16[1024,128]{1,0:T(8,128)(2,1)S(1)} %shard_map.100), channel_id=1, source_target_pairs={{0,4},{1,3},{2,6},{3,1},{4,0},{5,7},{6,2},{7,5},{8,12},{9,11},{10,... | collective-permute-start | bytes 786440 | tf_op jit(solution)/shard_map/ppermute | solution.py:42
  20.7 0.0 collective-permute-done.10.refs_0_
  20.7 2.2 %collective-permute-start.11 = (bf16[288,128]{1,0:T(8,128)(2,1)S(1)}, bf16[288,128]{1,0:T(8,128)(2,1)S(1)}, u32[]{:S(2)}, u32[]{:S(2)}) collective-permute-start(bf16[288,128]{1,0:T(8,128)(2,1)S(1)} %shard_map.101.refs_5_.refs_12_), channel_id=1, source_target_pairs={{0,6},{1,7},{2,4},{3,5},{4,2},{5,3},{6,0},{7,1},{8,14},{9,15},{10,... | collective-permute-start | bytes 221192 | tf_op jit(solution)/shard_map/ppermute | solution.py:42
  22.9 0.5 %collective-permute-start.13 = (bf16[288,128]{1,0:T(8,128)(2,1)S(1)}, bf16[288,128]{1,0:T(8,128)(2,1)S(1)}, u32[]{:S(2)}, u32[]{:S(2)}) collective-permute-start(bf16[288,128]{1,0:T(8,128)(2,1)S(1)} %shard_map.101.refs_5_.refs_12_), channel_id=1, source_target_pairs={{0,2},{1,3},{2,0},{3,1},{4,6},{5,7},{6,4},{7,5},{8,10},{9,11},{10,... | collective-permute-start | bytes 221192 | tf_op jit(solution)/shard_map/ppermute | solution.py:42
  23.5 0.7 %collective-permute-start.14 = (bf16[288,128]{1,0:T(8,128)(2,1)S(1)}, bf16[288,128]{1,0:T(8,128)(2,1)S(1)}, u32[]{:S(2)}, u32[]{:S(2)}) collective-permute-start(bf16[288,128]{1,0:T(8,128)(2,1)S(1)} %shard_map.101.refs_5_.refs_12_), channel_id=1, source_target_pairs={{0,4},{1,5},{2,6},{3,7},{4,0},{5,1},{6,2},{7,3},{8,12},{9,13},{10,... | collective-permute-start | bytes 221192 | tf_op jit(solution)/shard_map/ppermute | solution.py:42
  24.2 2.7 %collective-permute-done.11.refs_8_.refs_15_ = bf16[288,128]{1,0:T(8,128)(2,1)S(1)} collective-permute-done((bf16[288,128]{1,0:T(8,128)(2,1)S(1)}, bf16[288,128]{1,0:T(8,128)(2,1)S(1)}, u32[]{:S(2)}, u32[]{:S(2)}) %collective-permute-start.11) | collective-permute-done | bytes 73760 | tf_op jit(solution)/shard_map/ppermute | solution.py:42
  26.9 1.2 %collective-permute-start.12 = (bf16[1024,128]{1,0:T(8,128)(2,1)S(1)}, bf16[1024,128]{1,0:T(8,128)(2,1)S(1)}, u32[]{:S(2)}, u32[]{:S(2)}) collective-permute-start(bf16[1024,128]{1,0:T(8,128)(2,1)S(1)} %shard_map.102), channel_id=1, source_target_pairs={{0,4},{1,3},{2,6},{3,1},{4,0},{5,7},{6,2},{7,5},{8,12},{9,11},{10,... | collective-permute-start | bytes 786440 | tf_op jit(solution)/shard_map/ppermute | solution.py:42
  28.1 0.5 shard_map.103.refs_4_
  28.6 0.0 collective-permute-done.13.refs_6_.refs_13_
  28.6 0.1 collective-permute-done.14.refs_7_.refs_14_
  28.7 0.4 shard_map.104
  29.0 3.6 %collective-permute-start.15 = (bf16[288,128]{1,0:T(8,128)(2,1)S(1)}, bf16[288,128]{1,0:T(8,128)(2,1)S(1)}, u32[]{:S(2)}, u32[]{:S(2)}) collective-permute-start(bf16[288,128]{1,0:T(8,128)(2,1)S(1)} %get-tuple-element.29), channel_id=1, source_target_pairs={{0,8},{1,9},{2,10},{3,11},{4,12},{5,13},{6,14},{7,15},{8,16},{9,17... | collective-permute-start | bytes 221192 | tf_op jit(solution)/shard_map/ppermute | solution.py:42
  32.6 1.5 %collective-permute-start.20 = (bf16[544,128]{1,0:T(8,128)(2,1)S(1)}, bf16[544,128]{1,0:T(8,128)(2,1)S(1)}, u32[]{:S(2)}, u32[]{:S(2)}) collective-permute-start(bf16[544,128]{1,0:T(8,128)(2,1)S(1)} %get-tuple-element.34.refs_0_), channel_id=1, source_target_pairs={{0,2},{1,5},{2,0},{3,7},{4,6},{5,1},{6,4},{7,3},{8,10},{9,13},{10,... | collective-permute-start | bytes 417800 | tf_op jit(solution)/shard_map/ppermute | solution.py:42
  34.2 0.4 collective-permute-done.15.refs_5_.refs_16_
  34.6 1.5 %collective-permute-start.16 = (bf16[288,128]{1,0:T(8,128)(2,1)S(1)}, bf16[288,128]{1,0:T(8,128)(2,1)S(1)}, u32[]{:S(2)}, u32[]{:S(2)}) collective-permute-start(bf16[288,128]{1,0:T(8,128)(2,1)S(1)} %collective-permute-done.15.refs_5_.refs_16_), channel_id=1, source_target_pairs={{0,2},{1,3},{2,0},{3,1},{4,6},{5,7},{6,4},{7,5},{8,10},{9,11},{10,... | collective-permute-start | bytes 221192 | tf_op jit(solution)/shard_map/ppermute | solution.py:42
  36.0 1.0 %collective-permute-start.17 = (bf16[288,128]{1,0:T(8,128)(2,1)S(1)}, bf16[288,128]{1,0:T(8,128)(2,1)S(1)}, u32[]{:S(2)}, u32[]{:S(2)}) collective-permute-start(bf16[288,128]{1,0:T(8,128)(2,1)S(1)} %collective-permute-done.15.refs_5_.refs_16_), channel_id=1, source_target_pairs={{0,4},{1,5},{2,6},{3,7},{4,0},{5,1},{6,2},{7,3},{8,12},{9,13},{10,... | collective-permute-start | bytes 221192 | tf_op jit(solution)/shard_map/ppermute | solution.py:42
  37.1 1.0 %collective-permute-start.18 = (bf16[288,128]{1,0:T(8,128)(2,1)S(1)}, bf16[288,128]{1,0:T(8,128)(2,1)S(1)}, u32[]{:S(2)}, u32[]{:S(2)}) collective-permute-start(bf16[288,128]{1,0:T(8,128)(2,1)S(1)} %collective-permute-done.15.refs_5_.refs_16_), channel_id=1, source_target_pairs={{0,6},{1,7},{2,4},{3,5},{4,2},{5,3},{6,0},{7,1},{8,14},{9,15},{10,... | collective-permute-start | bytes 221192 | tf_op jit(solution)/shard_map/ppermute | solution.py:42
  38.1 0.1 collective-permute-done.20.refs_1_
  38.2 1.6 %collective-permute-start.21 = (bf16[1088,128]{1,0:T(8,128)(2,1)S(1)}, bf16[1088,128]{1,0:T(8,128)(2,1)S(1)}, u32[]{:S(2)}, u32[]{:S(2)}) collective-permute-start(bf16[1088,128]{1,0:T(8,128)(2,1)S(1)} %shard_map.109), channel_id=1, source_target_pairs={{0,4},{1,3},{2,6},{3,1},{4,0},{5,7},{6,2},{7,5},{8,12},{9,11},{10,... | collective-permute-start | bytes 835592 | tf_op jit(solution)/shard_map/ppermute | solution.py:42
  39.8 0.5 shard_map.105.refs_4_
  40.3 0.0 copy-start.1
  40.3 0.0 collective-permute-done.16.refs_6_.refs_17_
  40.3 0.1 collective-permute-done.17.refs_7_.refs_18_
  40.4 2.8 %collective-permute-done.18.refs_8_.refs_19_ = bf16[288,128]{1,0:T(8,128)(2,1)S(1)} collective-permute-done((bf16[288,128]{1,0:T(8,128)(2,1)S(1)}, bf16[288,128]{1,0:T(8,128)(2,1)S(1)}, u32[]{:S(2)}, u32[]{:S(2)}) %collective-permute-start.18) | collective-permute-done | bytes 73760 | tf_op jit(solution)/shard_map/ppermute | solution.py:42
  43.2 0.3 shard_map.106.refs_0_
  43.5 1.0 %collective-permute-start.23 = (bf16[288,128]{1,0:T(8,128)(2,1)S(1)}, bf16[288,128]{1,0:T(8,128)(2,1)S(1)}, u32[]{:S(2)}, u32[]{:S(2)}) collective-permute-start(bf16[288,128]{1,0:T(8,128)(2,1)S(1)} %shard_map.106.refs_0_), channel_id=1, source_target_pairs={{0,2},{1,3},{2,0},{3,1},{4,6},{5,7},{6,4},{7,5},{8,10},{9,11},{10,... | collective-permute-start | bytes 221192 | tf_op jit(solution)/shard_map/ppermute | solution.py:42
  44.5 0.6 %collective-permute-start.24 = (bf16[288,128]{1,0:T(8,128)(2,1)S(1)}, bf16[288,128]{1,0:T(8,128)(2,1)S(1)}, u32[]{:S(2)}, u32[]{:S(2)}) collective-permute-start(bf16[288,128]{1,0:T(8,128)(2,1)S(1)} %shard_map.106.refs_0_), channel_id=1, source_target_pairs={{0,4},{1,5},{2,6},{3,7},{4,0},{5,1},{6,2},{7,3},{8,12},{9,13},{10,... | collective-permute-start | bytes 221192 | tf_op jit(solution)/shard_map/ppermute | solution.py:42
  45.1 2.0 %collective-permute-start.25 = (bf16[288,128]{1,0:T(8,128)(2,1)S(1)}, bf16[288,128]{1,0:T(8,128)(2,1)S(1)}, u32[]{:S(2)}, u32[]{:S(2)}) collective-permute-start(bf16[288,128]{1,0:T(8,128)(2,1)S(1)} %shard_map.106.refs_0_), channel_id=1, source_target_pairs={{0,6},{1,7},{2,4},{3,5},{4,2},{5,3},{6,0},{7,1},{8,14},{9,15},{10,... | collective-permute-start | bytes 221192 | tf_op jit(solution)/shard_map/ppermute | solution.py:42
  47.1 2.1 %shard_map.107 = (f32[256,384]{1,0:T(8,128)S(1)}, bf16[256,384]{1,0:T(8,128)(2,1)S(1)}) custom-call(bf16[256,2048]{1,0:T(8,128)(2,1)S(1)} %bitcast.9, bf16[256,2048]{1,0:T(8,128)(2,1)S(1)} %collective-permute-done.refs_1_, bf16[512,128]{1,0:T(8,128)(2,1)S(1)} %shard_map.95.refs_0_.refs_2_, bf16[512,128]{1,0:T(8,128)(2,1)S(1)} %collective-permute-done.2.refs_1_.refs_3_, ...), custom_call_target="tpu_custom_call" | custom-call | flops 1000 | bytes 1 | tf_op jit(solution)/shard_map/pallas_call | solution.py:272
  49.2 0.1 collective-permute-start.19
  49.3 0.0 collective-permute-done.21.refs_2_
  49.3 0.3 shard_map.110
  49.7 0.0 collective-permute-done.24.refs_2_
  49.7 0.7 %collective-permute-done.25.refs_3_ = bf16[288,128]{1,0:T(8,128)(2,1)S(1)} collective-permute-done((bf16[288,128]{1,0:T(8,128)(2,1)S(1)}, bf16[288,128]{1,0:T(8,128)(2,1)S(1)}, u32[]{:S(2)}, u32[]{:S(2)}) %collective-permute-start.25) | collective-permute-done | bytes 73760 | tf_op jit(solution)/shard_map/ppermute | solution.py:42
  50.4 0.2 shard_map.111
  50.6 0.1 collective-permute-start.26
  50.7 0.5 collective-permute-start.22
  51.2 0.9 %shard_map.108 = f32[256,768]{1,0:T(8,128)} custom-call(f32[256,384]{1,0:T(8,128)S(1)} %get-tuple-element.31.refs_0_, bf16[256,384]{1,0:T(8,128)(2,1)S(1)} %collective-permute-done.19.refs_1_), custom_call_target="tpu_custom_call" | custom-call | flops 1000 | bytes 1 | tf_op jit(solution)/shard_map/pallas_call | solution.py:272
  52.2 0.1 collective-permute-done.22.refs_1_
  52.2 0.9 %shard_map.112 = f32[256,768]{1,0:T(8,128)} custom-call(f32[256,256]{1,0:T(8,128)S(1)} %get-tuple-element.36.refs_0_, bf16[256,256]{1,0:T(8,128)(2,1)S(1)} %collective-permute-done.22.refs_1_, f32[256,128]{1,0:T(8,128)S(1)} %get-tuple-element.39.refs_2_, f32[256,128]{1,0:T(8,128)S(1)} %collective-permute-done.26.refs_3_), custom_call_target="tpu_custom_call" | custom-call | flops 1000 | bytes 1 | tf_op jit(solution)/shard_map/pallas_call | solution.py:272
  (19 shorter events, 0.2 us)
Async XLA Ops:
  0.6 14.0 %collective-permute-start = (bf16[256,2048]{1,0:T(8,128)(2,1)}, bf16[256,2048]{1,0:T(8,128)(2,1)S(1)}, u32[]{:S(2)}, u32[]{:S(2)}) collective-permute-start(bf16[256,2048]{1,0:T(8,128)(2,1)} %bitcast.8), channel_id=1, source_target_pairs={{0,1},{1,0},{2,3},{3,2},{4,5},{5,4},{6,7},{7,6},{8,9},{9,8},{10,11... | collective-permute-start | bytes 3145736 | tf_op jit(solution)/shard_map/ppermute | solution.py:46
  2.5 1.3 %collective-permute-start.1 = (bf16[256,128]{1,0:T(8,128)(2,1)S(1)}, bf16[256,128]{1,0:T(8,128)(2,1)S(1)}, u32[]{:S(2)}, u32[]{:S(2)}) collective-permute-start(bf16[256,128]{1,0:T(8,128)(2,1)S(1)} %get-tuple-element.49), channel_id=1, source_target_pairs={{0,1},{1,0},{2,3},{3,2},{4,5},{5,4},{6,7},{7,6},{8,9},{9,8},{10,11... | collective-permute-start | bytes 196616 | tf_op jit(solution)/shard_map/ppermute | solution.py:46
  2.7 9.8 %copy-start = (bf16[1,1,128,2048]{3,2,1,0:T(8,128)(2,1)S(1)}, bf16[1,1,128,2048]{3,2,1,0:T(8,128)(2,1)}, u32[]{:S(2)}) copy-start(bf16[1,1,128,2048]{3,2,1,0:T(8,128)(2,1)} %param.12) | copy-start | bytes 1572868
  2.7 9.8 %collective-permute-start.6 = (bf16[512,128]{1,0:T(8,128)(2,1)S(1)}, bf16[512,128]{1,0:T(8,128)(2,1)S(1)}, u32[]{:S(2)}, u32[]{:S(2)}) collective-permute-start(bf16[512,128]{1,0:T(8,128)(2,1)S(1)} %pad_maximum_fusion.1), channel_id=1, source_target_pairs={{0,1},{1,0},{2,3},{3,2},{4,5},{5,4},{6,7},{7,6},{8,9},{9,8},{10,11... | collective-permute-start | bytes 393224 | tf_op jit(solution)/shard_map/ppermute | solution.py:46
  3.9 8.7 %collective-permute-start.4 = (bf16[512,128]{1,0:T(8,128)(2,1)S(1)}, bf16[512,128]{1,0:T(8,128)(2,1)S(1)}, u32[]{:S(2)}, u32[]{:S(2)}) collective-permute-start(bf16[512,128]{1,0:T(8,128)(2,1)S(1)} %shard_map.95.refs_0_.refs_2_), channel_id=1, source_target_pairs={{0,6},{1,7},{2,4},{3,5},{4,2},{5,3},{6,0},{7,1},{8,14},{9,15},{10,... | collective-permute-start | bytes 393224 | tf_op jit(solution)/shard_map/ppermute | solution.py:42
  7.5 1.2 %collective-permute-start.5 = (s32[1,1]{1,0:T(1,128)}, s32[1,1]{1,0:T(1,128)}, u32[]{:S(2)}, u32[]{:S(2)}) collective-permute-start(s32[1,1]{1,0:T(1,128)} %param.13), channel_id=1, source_target_pairs={{0,1},{1,0},{2,3},{3,2},{4,5},{5,4},{6,7},{7,6},{8,9},{9,8},{10,11... | collective-permute-start | bytes 20 | tf_op jit(solution)/shard_map/ppermute | solution.py:46
  7.6 7.0 %collective-permute-start.2 = (bf16[512,128]{1,0:T(8,128)(2,1)S(1)}, bf16[512,128]{1,0:T(8,128)(2,1)S(1)}, u32[]{:S(2)}, u32[]{:S(2)}) collective-permute-start(bf16[512,128]{1,0:T(8,128)(2,1)S(1)} %shard_map.95.refs_0_.refs_2_), channel_id=1, source_target_pairs={{0,2},{1,3},{2,0},{3,1},{4,6},{5,7},{6,4},{7,5},{8,10},{9,11},{10,... | collective-permute-start | bytes 393224 | tf_op jit(solution)/shard_map/ppermute | solution.py:42
  8.8 5.8 %collective-permute-start.3 = (bf16[512,128]{1,0:T(8,128)(2,1)S(1)}, bf16[512,128]{1,0:T(8,128)(2,1)S(1)}, u32[]{:S(2)}, u32[]{:S(2)}) collective-permute-start(bf16[512,128]{1,0:T(8,128)(2,1)S(1)} %shard_map.95.refs_0_.refs_2_), channel_id=1, source_target_pairs={{0,4},{1,5},{2,6},{3,7},{4,0},{5,1},{6,2},{7,3},{8,12},{9,13},{10,... | collective-permute-start | bytes 393224 | tf_op jit(solution)/shard_map/ppermute | solution.py:42
  10.6 0.7 %copy-start.2 = (s32[1,8]{1,0:T(1,128)S(1)}, s32[1,8]{1,0:T(1,128)}, u32[]{:S(2)}) copy-start(s32[1,8]{1,0:T(1,128)} %order.1) | copy-start | bytes 100
  12.5 2.2 %collective-permute-start.8 = (bf16[128,2048]{1,0:T(8,128)(2,1)S(1)}, bf16[128,2048]{1,0:T(8,128)(2,1)S(1)}, u32[]{:S(2)}, u32[]{:S(2)}) collective-permute-start(bf16[128,2048]{1,0:T(8,128)(2,1)S(1)} %bitcast.2), channel_id=1, source_target_pairs={{0,1},{1,0},{2,3},{3,2},{4,5},{5,4},{6,7},{7,6},{8,9},{9,8},{10,11... | collective-permute-start | bytes 1572872 | tf_op jit(solution)/shard_map/ppermute | solution.py:46
  12.6 6.4 %collective-permute-start.7 = (bf16[1024,128]{1,0:T(8,128)(2,1)S(1)}, bf16[1024,128]{1,0:T(8,128)(2,1)S(1)}, u32[]{:S(2)}, u32[]{:S(2)}) collective-permute-start(bf16[1024,128]{1,0:T(8,128)(2,1)S(1)} %shard_map.97.refs_0_.refs_2_.refs_6_.refs_9_), channel_id=1, source_target_pairs={{0,2},{1,5},{2,0},{3,7},{4,6},{5,1},{6,4},{7,3},{8,10},{9,13},{10,... | collective-permute-start | bytes 786440 | tf_op jit(solution)/shard_map/ppermute | solution.py:42
  15.1 5.6 %collective-permute-start.10 = (bf16[288,128]{1,0:T(8,128)(2,1)S(1)}, bf16[288,128]{1,0:T(8,128)(2,1)S(1)}, u32[]{:S(2)}, u32[]{:S(2)}) collective-permute-start(bf16[288,128]{1,0:T(8,128)(2,1)S(1)} %shard_map.99.refs_9_), channel_id=1, source_target_pairs={{0,8},{1,9},{2,10},{3,11},{4,12},{5,13},{6,14},{7,15},{8,16},{9,17... | collective-permute-start | bytes 221192 | tf_op jit(solution)/shard_map/ppermute | solution.py:42
  19.1 9.0 %collective-permute-start.9 = (bf16[1024,128]{1,0:T(8,128)(2,1)S(1)}, bf16[1024,128]{1,0:T(8,128)(2,1)S(1)}, u32[]{:S(2)}, u32[]{:S(2)}) collective-permute-start(bf16[1024,128]{1,0:T(8,128)(2,1)S(1)} %shard_map.100), channel_id=1, source_target_pairs={{0,4},{1,3},{2,6},{3,1},{4,0},{5,7},{6,2},{7,5},{8,12},{9,11},{10,... | collective-permute-start | bytes 786440 | tf_op jit(solution)/shard_map/ppermute | solution.py:42
  20.7 6.2 %collective-permute-start.11 = (bf16[288,128]{1,0:T(8,128)(2,1)S(1)}, bf16[288,128]{1,0:T(8,128)(2,1)S(1)}, u32[]{:S(2)}, u32[]{:S(2)}) collective-permute-start(bf16[288,128]{1,0:T(8,128)(2,1)S(1)} %shard_map.101.refs_5_.refs_12_), channel_id=1, source_target_pairs={{0,6},{1,7},{2,4},{3,5},{4,2},{5,3},{6,0},{7,1},{8,14},{9,15},{10,... | collective-permute-start | bytes 221192 | tf_op jit(solution)/shard_map/ppermute | solution.py:42
  22.9 5.6 %collective-permute-start.13 = (bf16[288,128]{1,0:T(8,128)(2,1)S(1)}, bf16[288,128]{1,0:T(8,128)(2,1)S(1)}, u32[]{:S(2)}, u32[]{:S(2)}) collective-permute-start(bf16[288,128]{1,0:T(8,128)(2,1)S(1)} %shard_map.101.refs_5_.refs_12_), channel_id=1, source_target_pairs={{0,2},{1,3},{2,0},{3,1},{4,6},{5,7},{6,4},{7,5},{8,10},{9,11},{10,... | collective-permute-start | bytes 221192 | tf_op jit(solution)/shard_map/ppermute | solution.py:42
  23.5 5.2 %collective-permute-start.14 = (bf16[288,128]{1,0:T(8,128)(2,1)S(1)}, bf16[288,128]{1,0:T(8,128)(2,1)S(1)}, u32[]{:S(2)}, u32[]{:S(2)}) collective-permute-start(bf16[288,128]{1,0:T(8,128)(2,1)S(1)} %shard_map.101.refs_5_.refs_12_), channel_id=1, source_target_pairs={{0,4},{1,5},{2,6},{3,7},{4,0},{5,1},{6,2},{7,3},{8,12},{9,13},{10,... | collective-permute-start | bytes 221192 | tf_op jit(solution)/shard_map/ppermute | solution.py:42
  26.9 12.9 %collective-permute-start.12 = (bf16[1024,128]{1,0:T(8,128)(2,1)S(1)}, bf16[1024,128]{1,0:T(8,128)(2,1)S(1)}, u32[]{:S(2)}, u32[]{:S(2)}) collective-permute-start(bf16[1024,128]{1,0:T(8,128)(2,1)S(1)} %shard_map.102), channel_id=1, source_target_pairs={{0,4},{1,3},{2,6},{3,1},{4,0},{5,7},{6,2},{7,5},{8,12},{9,11},{10,... | collective-permute-start | bytes 786440 | tf_op jit(solution)/shard_map/ppermute | solution.py:42
  29.0 5.5 %collective-permute-start.15 = (bf16[288,128]{1,0:T(8,128)(2,1)S(1)}, bf16[288,128]{1,0:T(8,128)(2,1)S(1)}, u32[]{:S(2)}, u32[]{:S(2)}) collective-permute-start(bf16[288,128]{1,0:T(8,128)(2,1)S(1)} %get-tuple-element.29), channel_id=1, source_target_pairs={{0,8},{1,9},{2,10},{3,11},{4,12},{5,13},{6,14},{7,15},{8,16},{9,17... | collective-permute-start | bytes 221192 | tf_op jit(solution)/shard_map/ppermute | solution.py:42
  32.6 5.6 %collective-permute-start.20 = (bf16[544,128]{1,0:T(8,128)(2,1)S(1)}, bf16[544,128]{1,0:T(8,128)(2,1)S(1)}, u32[]{:S(2)}, u32[]{:S(2)}) collective-permute-start(bf16[544,128]{1,0:T(8,128)(2,1)S(1)} %get-tuple-element.34.refs_0_), channel_id=1, source_target_pairs={{0,2},{1,5},{2,0},{3,7},{4,6},{5,1},{6,4},{7,3},{8,10},{9,13},{10,... | collective-permute-start | bytes 417800 | tf_op jit(solution)/shard_map/ppermute | solution.py:42
  34.6 5.7 %collective-permute-start.16 = (bf16[288,128]{1,0:T(8,128)(2,1)S(1)}, bf16[288,128]{1,0:T(8,128)(2,1)S(1)}, u32[]{:S(2)}, u32[]{:S(2)}) collective-permute-start(bf16[288,128]{1,0:T(8,128)(2,1)S(1)} %collective-permute-done.15.refs_5_.refs_16_), channel_id=1, source_target_pairs={{0,2},{1,3},{2,0},{3,1},{4,6},{5,7},{6,4},{7,5},{8,10},{9,11},{10,... | collective-permute-start | bytes 221192 | tf_op jit(solution)/shard_map/ppermute | solution.py:42
  36.0 4.4 %collective-permute-start.17 = (bf16[288,128]{1,0:T(8,128)(2,1)S(1)}, bf16[288,128]{1,0:T(8,128)(2,1)S(1)}, u32[]{:S(2)}, u32[]{:S(2)}) collective-permute-start(bf16[288,128]{1,0:T(8,128)(2,1)S(1)} %collective-permute-done.15.refs_5_.refs_16_), channel_id=1, source_target_pairs={{0,4},{1,5},{2,6},{3,7},{4,0},{5,1},{6,2},{7,3},{8,12},{9,13},{10,... | collective-permute-start | bytes 221192 | tf_op jit(solution)/shard_map/ppermute | solution.py:42
  37.1 6.1 %collective-permute-start.18 = (bf16[288,128]{1,0:T(8,128)(2,1)S(1)}, bf16[288,128]{1,0:T(8,128)(2,1)S(1)}, u32[]{:S(2)}, u32[]{:S(2)}) collective-permute-start(bf16[288,128]{1,0:T(8,128)(2,1)S(1)} %collective-permute-done.15.refs_5_.refs_16_), channel_id=1, source_target_pairs={{0,6},{1,7},{2,4},{3,5},{4,2},{5,3},{6,0},{7,1},{8,14},{9,15},{10,... | collective-permute-start | bytes 221192 | tf_op jit(solution)/shard_map/ppermute | solution.py:42
  38.2 11.1 %collective-permute-start.21 = (bf16[1088,128]{1,0:T(8,128)(2,1)S(1)}, bf16[1088,128]{1,0:T(8,128)(2,1)S(1)}, u32[]{:S(2)}, u32[]{:S(2)}) collective-permute-start(bf16[1088,128]{1,0:T(8,128)(2,1)S(1)} %shard_map.109), channel_id=1, source_target_pairs={{0,4},{1,3},{2,6},{3,1},{4,0},{5,7},{6,2},{7,5},{8,12},{9,11},{10,... | collective-permute-start | bytes 835592 | tf_op jit(solution)/shard_map/ppermute | solution.py:42
  40.3 6.8 %copy-start.1 = (bf16[1,256,2048]{2,1,0:T(8,128)(2,1)S(1)}, bf16[1,256,2048]{2,1,0:T(8,128)(2,1)}, u32[]{:S(2)}) copy-start(bf16[1,256,2048]{2,1,0:T(8,128)(2,1)} %param.11) | copy-start | bytes 3145732
  43.5 6.1 %collective-permute-start.23 = (bf16[288,128]{1,0:T(8,128)(2,1)S(1)}, bf16[288,128]{1,0:T(8,128)(2,1)S(1)}, u32[]{:S(2)}, u32[]{:S(2)}) collective-permute-start(bf16[288,128]{1,0:T(8,128)(2,1)S(1)} %shard_map.106.refs_0_), channel_id=1, source_target_pairs={{0,2},{1,3},{2,0},{3,1},{4,6},{5,7},{6,4},{7,5},{8,10},{9,11},{10,... | collective-permute-start | bytes 221192 | tf_op jit(solution)/shard_map/ppermute | solution.py:42
  44.5 5.1 %collective-permute-start.24 = (bf16[288,128]{1,0:T(8,128)(2,1)S(1)}, bf16[288,128]{1,0:T(8,128)(2,1)S(1)}, u32[]{:S(2)}, u32[]{:S(2)}) collective-permute-start(bf16[288,128]{1,0:T(8,128)(2,1)S(1)} %shard_map.106.refs_0_), channel_id=1, source_target_pairs={{0,4},{1,5},{2,6},{3,7},{4,0},{5,1},{6,2},{7,3},{8,12},{9,13},{10,... | collective-permute-start | bytes 221192 | tf_op jit(solution)/shard_map/ppermute | solution.py:42
  45.1 5.3 %collective-permute-start.25 = (bf16[288,128]{1,0:T(8,128)(2,1)S(1)}, bf16[288,128]{1,0:T(8,128)(2,1)S(1)}, u32[]{:S(2)}, u32[]{:S(2)}) collective-permute-start(bf16[288,128]{1,0:T(8,128)(2,1)S(1)} %shard_map.106.refs_0_), channel_id=1, source_target_pairs={{0,6},{1,7},{2,4},{3,5},{4,2},{5,3},{6,0},{7,1},{8,14},{9,15},{10,... | collective-permute-start | bytes 221192 | tf_op jit(solution)/shard_map/ppermute | solution.py:42
  49.2 2.0 %collective-permute-start.19 = (bf16[256,384]{1,0:T(8,128)(2,1)S(1)}, bf16[256,384]{1,0:T(8,128)(2,1)S(1)}, u32[]{:S(2)}, u32[]{:S(2)}) collective-permute-start(bf16[256,384]{1,0:T(8,128)(2,1)S(1)} %get-tuple-element.32), channel_id=1, source_target_pairs={{0,1},{1,0},{2,3},{3,2},{4,5},{5,4},{6,7},{7,6},{8,9},{9,8},{10,11... | collective-permute-start | bytes 589832 | tf_op jit(solution)/shard_map/ppermute | solution.py:46
  50.6 1.5 %collective-permute-start.26 = (f32[256,128]{1,0:T(8,128)S(1)}, f32[256,128]{1,0:T(8,128)S(1)}, u32[]{:S(2)}, u32[]{:S(2)}) collective-permute-start(f32[256,128]{1,0:T(8,128)S(1)} %get-tuple-element.40), channel_id=1, source_target_pairs={{0,1},{1,0},{2,3},{3,2},{4,5},{5,4},{6,7},{7,6},{8,9},{9,8},{10,11... | collective-permute-start | bytes 393224 | tf_op jit(solution)/shard_map/ppermute | solution.py:46
  50.7 1.5 %collective-permute-start.22 = (bf16[256,256]{1,0:T(8,128)(2,1)S(1)}, bf16[256,256]{1,0:T(8,128)(2,1)S(1)}, u32[]{:S(2)}, u32[]{:S(2)}) collective-permute-start(bf16[256,256]{1,0:T(8,128)(2,1)S(1)} %get-tuple-element.37), channel_id=1, source_target_pairs={{0,1},{1,0},{2,3},{3,2},{4,5},{5,4},{6,7},{7,6},{8,9},{9,8},{10,11... | collective-permute-start | bytes 393224 | tf_op jit(solution)/shard_map/ppermute | solution.py:46

commit v7 on v6

--- a/solution.py
+++ b/solution.py
@@ -405,7 +405,7 @@
         sent = [arrived, *around(arrived)]
         came += sent
         if shared:
-            shared = gather(shared[0], (arrived,))
+            shared = gather(shared[0], (sent[-1],))
         if tick == 1:
             laters.append(go_on(0, product))
             laters += [go_on(panel, sent[-1]) for panel in range(1, ticks - 1)]

time: 53.4 us -> 52.6 us (0.985)
    ppermute x19, starting transfers between devices: 29.6 us -> 29 us  [hop(): return lax.ppermute(block, ('chain', 'rows'), route)]
where the time goes in v7:
time: 52.6 us; the launch traced here: 52.4 us
  starting transfers between devices  31 us (59%)
  waiting for transfers between devices  9.16 us (17%)
  Pallas kernels  8 us (15%)
  between operations  2.2 us (4%)
  other arithmetic  1.41 us (3%)
  local copies, waits for them, and re-layouts  0.64 us (1%)
    ppermute x19, starting transfers between devices, hop(): return lax.ppermute(block, ('chain', 'rows'), route)  29 us
    pallas_call x18, Pallas kernels, call(): pl.pallas_call(kernel, out_shape=out_shape, in_specs=in_specs, out_specs=...  8 us
    ppermute x19, waiting for transfers between devices, hop(): return lax.ppermute(block, ('chain', 'rows'), route)  7.83 us
    ppermute x8, starting transfers between devices, swap(): return lax.ppermute(block, 'rows', [(i, i ^ 1) for i in range(rows)])  1.94 us
    convert_element_type x1, other arithmetic, body(): (panel(t) - is_first * first_updates[:, (t - 1) * PW:t * PW]).astype(NARROW)  1.35 us
    ppermute x8, waiting for transfers between devices, swap(): return lax.ppermute(block, 'rows', [(i, i ^ 1) for i in range(rows)])  1.33 us
  transfers between devices with their start and end apart: 27, of which 12 were waited for; matrix products, arithmetic and copies ran while one was open for 3% of the time, Pallas kernels for 13%

profile of v7, /device:TPU:0, one launch (start us, length us, event | category | flops | bytes accessed | tf_op | source)
XLA Modules:
  0.0 52.4 jit_solution(16703378656323790035)
XLA Ops:
  0.6 0.5 collective-permute-start
  1.1 1.3 %subtract_convert_fusion.1 = (bf16[256,256]{1,0:T(8,128)(2,1)S(1)}, bf16[256,256]{1,0:T(8,128)(2,1)S(1)}, bf16[256,256]{1,0:T(8,128)(2,1)S(1)}) fusion(f32[256,512]{1,0:T(8,128)} %param.10, f32[]{:T(128)S(6)} %convert_element_type.24, bf16[256,768]{1,0:T(8,128)(2,1)} %param.8, f32[256,256]{1,0:T(8,128)} %param.9), kind=kLoop, calls=%fused_computation.1 | loop fusion | flops 720896 | bytes 1572868 | tf_op jit(solution)/shard_map/convert_element_type | solution.py:342
  2.5 0.1 collective-permute-start.1
  2.7 0.0 copy-start
  2.7 0.5 collective-permute-start.6
  3.2 0.6 %collective-permute-done.1.mate = bf16[256,128]{1,0:T(8,128)(2,1)S(1)} collective-permute-done((bf16[256,128]{1,0:T(8,128)(2,1)S(1)}, bf16[256,128]{1,0:T(8,128)(2,1)S(1)}, u32[]{:S(2)}, u32[]{:S(2)}) %collective-permute-start.1) | collective-permute-done | bytes 65568 | tf_op jit(solution)/shard_map/ppermute | solution.py:46
  3.9 3.7 %collective-permute-start.4 = (bf16[512,128]{1,0:T(8,128)(2,1)S(1)}, bf16[512,128]{1,0:T(8,128)(2,1)S(1)}, u32[]{:S(2)}, u32[]{:S(2)}) collective-permute-start(bf16[512,128]{1,0:T(8,128)(2,1)S(1)} %shard_map.95.refs_0_.refs_2_), channel_id=1, source_target_pairs={{0,6},{1,7},{2,4},{3,5},{4,2},{5,3},{6,0},{7,1},{8,14},{9,15},{10,... | collective-permute-start | bytes 393224 | tf_op jit(solution)/shard_map/ppermute | solution.py:42
  7.5 0.1 collective-permute-start.5
  7.6 0.5 %collective-permute-start.2 = (bf16[512,128]{1,0:T(8,128)(2,1)S(1)}, bf16[512,128]{1,0:T(8,128)(2,1)S(1)}, u32[]{:S(2)}, u32[]{:S(2)}) collective-permute-start(bf16[512,128]{1,0:T(8,128)(2,1)S(1)} %shard_map.95.refs_0_.refs_2_), channel_id=1, source_target_pairs={{0,2},{1,3},{2,0},{3,1},{4,6},{5,7},{6,4},{7,5},{8,10},{9,11},{10,... | collective-permute-start | bytes 393224 | tf_op jit(solution)/shard_map/ppermute | solution.py:42
  8.1 0.6 %collective-permute-done.5.mate_target = s32[1,1]{1,0:T(1,128)} collective-permute-done((s32[1,1]{1,0:T(1,128)}, s32[1,1]{1,0:T(1,128)}, u32[]{:S(2)}, u32[]{:S(2)}) %collective-permute-start.5) | collective-permute-done | bytes 36 | tf_op jit(solution)/shard_map/ppermute | solution.py:46
  8.8 0.5 collective-permute-start.3
  10.6 0.0 copy-start.2
  10.6 0.6 %copy-done.2 = s32[1,8]{1,0:T(1,128)S(1)} copy-done((s32[1,8]{1,0:T(1,128)S(1)}, s32[1,8]{1,0:T(1,128)}, u32[]{:S(2)}) %copy-start.2) | copy-done | bytes 56
  11.2 1.2 %shard_map.96 = (bf16[32,128]{1,0:T(8,128)(2,1)S(1)}, f32[2,128]{1,0:T(2,128)S(1)}) custom-call(s32[1,1]{1,0:T(1,128)S(6)} %copy.10.own_target, s32[1,1]{1,0:T(1,128)} %collective-permute-done.5.mate_target, s32[1,8]{1,0:T(1,128)S(1)} %copy-done.2, s32[1]{0:T(128)S(6)} %copy.11.count), custom_call_target="tpu_custom_call" | custom-call | flops 1000 | bytes 1 | tf_op jit(solution)/shard_map/pallas_call | solution.py:272
  12.5 0.0 collective-permute-done.6.mate
  12.5 0.1 collective-permute-start.8
  12.6 0.0 collective-permute-done.4.refs_3_.refs_5_
  12.6 1.2 %collective-permute-start.7 = (bf16[1024,128]{1,0:T(8,128)(2,1)S(1)}, bf16[1024,128]{1,0:T(8,128)(2,1)S(1)}, u32[]{:S(2)}, u32[]{:S(2)}) collective-permute-start(bf16[1024,128]{1,0:T(8,128)(2,1)S(1)} %shard_map.97.refs_0_.refs_2_.refs_6_.refs_9_), channel_id=1, source_target_pairs={{0,2},{1,5},{2,0},{3,7},{4,6},{5,1},{6,4},{7,3},{8,10},{9,13},{10,... | collective-permute-start | bytes 786440 | tf_op jit(solution)/shard_map/ppermute | solution.py:42
  13.8 0.8 %collective-permute-done.2.refs_1_.refs_3_ = bf16[512,128]{1,0:T(8,128)(2,1)S(1)} collective-permute-done((bf16[512,128]{1,0:T(8,128)(2,1)S(1)}, bf16[512,128]{1,0:T(8,128)(2,1)S(1)}, u32[]{:S(2)}, u32[]{:S(2)}) %collective-permute-start.2) | collective-permute-done | bytes 131104 | tf_op jit(solution)/shard_map/ppermute | solution.py:42
  14.6 0.0 collective-permute-done.3.refs_2_.refs_4_
  14.6 0.0 collective-permute-done.refs_1_
  14.7 0.0 collective-permute-done.8.mate.refs_1_
  14.7 0.4 shard_map.99.refs_9_
  15.1 3.6 %collective-permute-start.10 = (bf16[288,128]{1,0:T(8,128)(2,1)S(1)}, bf16[288,128]{1,0:T(8,128)(2,1)S(1)}, u32[]{:S(2)}, u32[]{:S(2)}) collective-permute-start(bf16[288,128]{1,0:T(8,128)(2,1)S(1)} %shard_map.99.refs_9_), channel_id=1, source_target_pairs={{0,8},{1,9},{2,10},{3,11},{4,12},{5,13},{6,14},{7,15},{8,16},{9,17... | collective-permute-start | bytes 221192 | tf_op jit(solution)/shard_map/ppermute | solution.py:42
  18.7 0.3 collective-permute-done.7.refs_1_.refs_3_.refs_7_.refs_10_
  19.1 1.6 %collective-permute-start.9 = (bf16[1024,128]{1,0:T(8,128)(2,1)S(1)}, bf16[1024,128]{1,0:T(8,128)(2,1)S(1)}, u32[]{:S(2)}, u32[]{:S(2)}) collective-permute-start(bf16[1024,128]{1,0:T(8,128)(2,1)S(1)} %shard_map.100), channel_id=1, source_target_pairs={{0,4},{1,3},{2,6},{3,1},{4,0},{5,7},{6,2},{7,5},{8,12},{9,11},{10,... | collective-permute-start | bytes 786440 | tf_op jit(solution)/shard_map/ppermute | solution.py:42
  20.7 0.0 collective-permute-done.10.refs_0_
  20.7 2.2 %collective-permute-start.11 = (bf16[288,128]{1,0:T(8,128)(2,1)S(1)}, bf16[288,128]{1,0:T(8,128)(2,1)S(1)}, u32[]{:S(2)}, u32[]{:S(2)}) collective-permute-start(bf16[288,128]{1,0:T(8,128)(2,1)S(1)} %shard_map.101.refs_5_.refs_12_), channel_id=1, source_target_pairs={{0,6},{1,7},{2,4},{3,5},{4,2},{5,3},{6,0},{7,1},{8,14},{9,15},{10,... | collective-permute-start | bytes 221192 | tf_op jit(solution)/shard_map/ppermute | solution.py:42
  22.9 0.5 %collective-permute-start.13 = (bf16[288,128]{1,0:T(8,128)(2,1)S(1)}, bf16[288,128]{1,0:T(8,128)(2,1)S(1)}, u32[]{:S(2)}, u32[]{:S(2)}) collective-permute-start(bf16[288,128]{1,0:T(8,128)(2,1)S(1)} %shard_map.101.refs_5_.refs_12_), channel_id=1, source_target_pairs={{0,2},{1,3},{2,0},{3,1},{4,6},{5,7},{6,4},{7,5},{8,10},{9,11},{10,... | collective-permute-start | bytes 221192 | tf_op jit(solution)/shard_map/ppermute | solution.py:42
  23.5 0.7 %collective-permute-start.14 = (bf16[288,128]{1,0:T(8,128)(2,1)S(1)}, bf16[288,128]{1,0:T(8,128)(2,1)S(1)}, u32[]{:S(2)}, u32[]{:S(2)}) collective-permute-start(bf16[288,128]{1,0:T(8,128)(2,1)S(1)} %shard_map.101.refs_5_.refs_12_), channel_id=1, source_target_pairs={{0,4},{1,5},{2,6},{3,7},{4,0},{5,1},{6,2},{7,3},{8,12},{9,13},{10,... | collective-permute-start | bytes 221192 | tf_op jit(solution)/shard_map/ppermute | solution.py:42
  24.2 2.7 %collective-permute-done.11.refs_8_.refs_15_ = bf16[288,128]{1,0:T(8,128)(2,1)S(1)} collective-permute-done((bf16[288,128]{1,0:T(8,128)(2,1)S(1)}, bf16[288,128]{1,0:T(8,128)(2,1)S(1)}, u32[]{:S(2)}, u32[]{:S(2)}) %collective-permute-start.11) | collective-permute-done | bytes 73760 | tf_op jit(solution)/shard_map/ppermute | solution.py:42
  26.9 1.2 %collective-permute-start.12 = (bf16[1024,128]{1,0:T(8,128)(2,1)S(1)}, bf16[1024,128]{1,0:T(8,128)(2,1)S(1)}, u32[]{:S(2)}, u32[]{:S(2)}) collective-permute-start(bf16[1024,128]{1,0:T(8,128)(2,1)S(1)} %shard_map.102), channel_id=1, source_target_pairs={{0,4},{1,3},{2,6},{3,1},{4,0},{5,7},{6,2},{7,5},{8,12},{9,11},{10,... | collective-permute-start | bytes 786440 | tf_op jit(solution)/shard_map/ppermute | solution.py:42
  28.1 0.5 shard_map.103.refs_4_
  28.6 0.0 collective-permute-done.13.refs_6_.refs_13_
  28.6 0.1 collective-permute-done.14.refs_7_.refs_14_
  28.7 0.4 shard_map.104
  29.0 3.6 %collective-permute-start.15 = (bf16[288,128]{1,0:T(8,128)(2,1)S(1)}, bf16[288,128]{1,0:T(8,128)(2,1)S(1)}, u32[]{:S(2)}, u32[]{:S(2)}) collective-permute-start(bf16[288,128]{1,0:T(8,128)(2,1)S(1)} %get-tuple-element.29), channel_id=1, source_target_pairs={{0,8},{1,9},{2,10},{3,11},{4,12},{5,13},{6,14},{7,15},{8,16},{9,17... | collective-permute-start | bytes 221192 | tf_op jit(solution)/shard_map/ppermute | solution.py:42
  32.6 1.6 %collective-permute-start.20 = (bf16[544,128]{1,0:T(8,128)(2,1)S(1)}, bf16[544,128]{1,0:T(8,128)(2,1)S(1)}, u32[]{:S(2)}, u32[]{:S(2)}) collective-permute-start(bf16[544,128]{1,0:T(8,128)(2,1)S(1)} %get-tuple-element.34.refs_0_), channel_id=1, source_target_pairs={{0,2},{1,5},{2,0},{3,7},{4,6},{5,1},{6,4},{7,3},{8,10},{9,13},{10,... | collective-permute-start | bytes 417800 | tf_op jit(solution)/shard_map/ppermute | solution.py:42
  34.2 0.4 collective-permute-done.15.refs_5_.refs_16_
  34.6 2.0 %collective-permute-start.18 = (bf16[288,128]{1,0:T(8,128)(2,1)S(1)}, bf16[288,128]{1,0:T(8,128)(2,1)S(1)}, u32[]{:S(2)}, u32[]{:S(2)}) collective-permute-start(bf16[288,128]{1,0:T(8,128)(2,1)S(1)} %collective-permute-done.15.refs_5_.refs_16_), channel_id=1, source_target_pairs={{0,6},{1,7},{2,4},{3,5},{4,2},{5,3},{6,0},{7,1},{8,14},{9,15},{10,... | collective-permute-start | bytes 221192 | tf_op jit(solution)/shard_map/ppermute | solution.py:42
  36.5 0.9 %collective-permute-start.16 = (bf16[288,128]{1,0:T(8,128)(2,1)S(1)}, bf16[288,128]{1,0:T(8,128)(2,1)S(1)}, u32[]{:S(2)}, u32[]{:S(2)}) collective-permute-start(bf16[288,128]{1,0:T(8,128)(2,1)S(1)} %collective-permute-done.15.refs_5_.refs_16_), channel_id=1, source_target_pairs={{0,2},{1,3},{2,0},{3,1},{4,6},{5,7},{6,4},{7,5},{8,10},{9,11},{10,... | collective-permute-start | bytes 221192 | tf_op jit(solution)/shard_map/ppermute | solution.py:42
  37.5 0.6 %collective-permute-start.17 = (bf16[288,128]{1,0:T(8,128)(2,1)S(1)}, bf16[288,128]{1,0:T(8,128)(2,1)S(1)}, u32[]{:S(2)}, u32[]{:S(2)}) collective-permute-start(bf16[288,128]{1,0:T(8,128)(2,1)S(1)} %collective-permute-done.15.refs_5_.refs_16_), channel_id=1, source_target_pairs={{0,4},{1,5},{2,6},{3,7},{4,0},{5,1},{6,2},{7,3},{8,12},{9,13},{10,... | collective-permute-start | bytes 221192 | tf_op jit(solution)/shard_map/ppermute | solution.py:42
  38.1 1.0 %collective-permute-done.20.refs_1_ = bf16[544,128]{1,0:T(8,128)(2,1)S(1)} collective-permute-done((bf16[544,128]{1,0:T(8,128)(2,1)S(1)}, bf16[544,128]{1,0:T(8,128)(2,1)S(1)}, u32[]{:S(2)}, u32[]{:S(2)}) %collective-permute-start.20) | collective-permute-done | bytes 139296 | tf_op jit(solution)/shard_map/ppermute | solution.py:42
  39.0 1.3 %collective-permute-done.18.refs_8_.refs_19_ = bf16[288,128]{1,0:T(8,128)(2,1)S(1)} collective-permute-done((bf16[288,128]{1,0:T(8,128)(2,1)S(1)}, bf16[288,128]{1,0:T(8,128)(2,1)S(1)}, u32[]{:S(2)}, u32[]{:S(2)}) %collective-permute-start.18) | collective-permute-done | bytes 73760 | tf_op jit(solution)/shard_map/ppermute | solution.py:42
  40.3 1.1 %collective-permute-start.21 = (bf16[1088,128]{1,0:T(8,128)(2,1)S(1)}, bf16[1088,128]{1,0:T(8,128)(2,1)S(1)}, u32[]{:S(2)}, u32[]{:S(2)}) collective-permute-start(bf16[1088,128]{1,0:T(8,128)(2,1)S(1)} %shard_map.109), channel_id=1, source_target_pairs={{0,4},{1,3},{2,6},{3,1},{4,0},{5,7},{6,2},{7,5},{8,12},{9,11},{10,... | collective-permute-start | bytes 835592 | tf_op jit(solution)/shard_map/ppermute | solution.py:42
  41.4 0.5 shard_map.105.refs_4_
  41.9 0.0 copy-start.1
  41.9 0.0 collective-permute-done.16.refs_6_.refs_17_
  41.9 0.0 collective-permute-done.17.refs_7_.refs_18_
  41.9 0.3 shard_map.106.refs_0_
  42.2 1.3 %collective-permute-start.23 = (bf16[288,128]{1,0:T(8,128)(2,1)S(1)}, bf16[288,128]{1,0:T(8,128)(2,1)S(1)}, u32[]{:S(2)}, u32[]{:S(2)}) collective-permute-start(bf16[288,128]{1,0:T(8,128)(2,1)S(1)} %shard_map.106.refs_0_), channel_id=1, source_target_pairs={{0,2},{1,3},{2,0},{3,1},{4,6},{5,7},{6,4},{7,5},{8,10},{9,11},{10,... | collective-permute-start | bytes 221192 | tf_op jit(solution)/shard_map/ppermute | solution.py:42
  43.5 0.8 %collective-permute-start.24 = (bf16[288,128]{1,0:T(8,128)(2,1)S(1)}, bf16[288,128]{1,0:T(8,128)(2,1)S(1)}, u32[]{:S(2)}, u32[]{:S(2)}) collective-permute-start(bf16[288,128]{1,0:T(8,128)(2,1)S(1)} %shard_map.106.refs_0_), channel_id=1, source_target_pairs={{0,4},{1,5},{2,6},{3,7},{4,0},{5,1},{6,2},{7,3},{8,12},{9,13},{10,... | collective-permute-start | bytes 221192 | tf_op jit(solution)/shard_map/ppermute | solution.py:42
  44.3 1.4 %collective-permute-start.25 = (bf16[288,128]{1,0:T(8,128)(2,1)S(1)}, bf16[288,128]{1,0:T(8,128)(2,1)S(1)}, u32[]{:S(2)}, u32[]{:S(2)}) collective-permute-start(bf16[288,128]{1,0:T(8,128)(2,1)S(1)} %shard_map.106.refs_0_), channel_id=1, source_target_pairs={{0,6},{1,7},{2,4},{3,5},{4,2},{5,3},{6,0},{7,1},{8,14},{9,15},{10,... | collective-permute-start | bytes 221192 | tf_op jit(solution)/shard_map/ppermute | solution.py:42
  45.8 2.1 %shard_map.107 = (f32[256,384]{1,0:T(8,128)S(1)}, bf16[256,384]{1,0:T(8,128)(2,1)S(1)}) custom-call(bf16[256,2048]{1,0:T(8,128)(2,1)S(1)} %bitcast.9, bf16[256,2048]{1,0:T(8,128)(2,1)S(1)} %collective-permute-done.refs_1_, bf16[512,128]{1,0:T(8,128)(2,1)S(1)} %shard_map.95.refs_0_.refs_2_, bf16[512,128]{1,0:T(8,128)(2,1)S(1)} %collective-permute-done.2.refs_1_.refs_3_, ...), custom_call_target="tpu_custom_call" | custom-call | flops 1000 | bytes 1 | tf_op jit(solution)/shard_map/pallas_call | solution.py:272
  47.9 0.1 collective-permute-start.19
  48.0 0.3 shard_map.110
  48.3 0.2 collective-permute-done.24.refs_2_
  48.5 1.1 %collective-permute-done.25.refs_3_ = bf16[288,128]{1,0:T(8,128)(2,1)S(1)} collective-permute-done((bf16[288,128]{1,0:T(8,128)(2,1)S(1)}, bf16[288,128]{1,0:T(8,128)(2,1)S(1)}, u32[]{:S(2)}, u32[]{:S(2)}) %collective-permute-start.25) | collective-permute-done | bytes 73760 | tf_op jit(solution)/shard_map/ppermute | solution.py:42
  49.6 0.2 shard_map.111
  49.8 0.1 collective-permute-start.26
  49.9 0.5 collective-permute-start.22
  50.4 0.9 %shard_map.108 = f32[256,768]{1,0:T(8,128)} custom-call(f32[256,384]{1,0:T(8,128)S(1)} %get-tuple-element.31.refs_0_, bf16[256,384]{1,0:T(8,128)(2,1)S(1)} %collective-permute-done.19.refs_1_), custom_call_target="tpu_custom_call" | custom-call | flops 1000 | bytes 1 | tf_op jit(solution)/shard_map/pallas_call | solution.py:272
  51.4 0.1 collective-permute-done.22.refs_1_
  51.4 0.9 %shard_map.112 = f32[256,768]{1,0:T(8,128)} custom-call(f32[256,256]{1,0:T(8,128)S(1)} %get-tuple-element.36.refs_0_, bf16[256,256]{1,0:T(8,128)(2,1)S(1)} %collective-permute-done.22.refs_1_, f32[256,128]{1,0:T(8,128)S(1)} %get-tuple-element.39.refs_2_, f32[256,128]{1,0:T(8,128)S(1)} %collective-permute-done.26.refs_3_), custom_call_target="tpu_custom_call" | custom-call | flops 1000 | bytes 1 | tf_op jit(solution)/shard_map/pallas_call | solution.py:272
  (19 shorter events, 0.2 us)
Async XLA Ops:
  0.6 14.0 %collective-permute-start = (bf16[256,2048]{1,0:T(8,128)(2,1)}, bf16[256,2048]{1,0:T(8,128)(2,1)S(1)}, u32[]{:S(2)}, u32[]{:S(2)}) collective-permute-start(bf16[256,2048]{1,0:T(8,128)(2,1)} %bitcast.8), channel_id=1, source_target_pairs={{0,1},{1,0},{2,3},{3,2},{4,5},{5,4},{6,7},{7,6},{8,9},{9,8},{10,11... | collective-permute-start | bytes 3145736 | tf_op jit(solution)/shard_map/ppermute | solution.py:46
  2.5 1.3 %collective-permute-start.1 = (bf16[256,128]{1,0:T(8,128)(2,1)S(1)}, bf16[256,128]{1,0:T(8,128)(2,1)S(1)}, u32[]{:S(2)}, u32[]{:S(2)}) collective-permute-start(bf16[256,128]{1,0:T(8,128)(2,1)S(1)} %get-tuple-element.49), channel_id=1, source_target_pairs={{0,1},{1,0},{2,3},{3,2},{4,5},{5,4},{6,7},{7,6},{8,9},{9,8},{10,11... | collective-permute-start | bytes 196616 | tf_op jit(solution)/shard_map/ppermute | solution.py:46
  2.7 9.8 %copy-start = (bf16[1,1,128,2048]{3,2,1,0:T(8,128)(2,1)S(1)}, bf16[1,1,128,2048]{3,2,1,0:T(8,128)(2,1)}, u32[]{:S(2)}) copy-start(bf16[1,1,128,2048]{3,2,1,0:T(8,128)(2,1)} %param.12) | copy-start | bytes 1572868
  2.7 9.8 %collective-permute-start.6 = (bf16[512,128]{1,0:T(8,128)(2,1)S(1)}, bf16[512,128]{1,0:T(8,128)(2,1)S(1)}, u32[]{:S(2)}, u32[]{:S(2)}) collective-permute-start(bf16[512,128]{1,0:T(8,128)(2,1)S(1)} %pad_maximum_fusion.1), channel_id=1, source_target_pairs={{0,1},{1,0},{2,3},{3,2},{4,5},{5,4},{6,7},{7,6},{8,9},{9,8},{10,11... | collective-permute-start | bytes 393224 | tf_op jit(solution)/shard_map/ppermute | solution.py:46
  3.9 8.7 %collective-permute-start.4 = (bf16[512,128]{1,0:T(8,128)(2,1)S(1)}, bf16[512,128]{1,0:T(8,128)(2,1)S(1)}, u32[]{:S(2)}, u32[]{:S(2)}) collective-permute-start(bf16[512,128]{1,0:T(8,128)(2,1)S(1)} %shard_map.95.refs_0_.refs_2_), channel_id=1, source_target_pairs={{0,6},{1,7},{2,4},{3,5},{4,2},{5,3},{6,0},{7,1},{8,14},{9,15},{10,... | collective-permute-start | bytes 393224 | tf_op jit(solution)/shard_map/ppermute | solution.py:42
  7.5 1.2 %collective-permute-start.5 = (s32[1,1]{1,0:T(1,128)}, s32[1,1]{1,0:T(1,128)}, u32[]{:S(2)}, u32[]{:S(2)}) collective-permute-start(s32[1,1]{1,0:T(1,128)} %param.13), channel_id=1, source_target_pairs={{0,1},{1,0},{2,3},{3,2},{4,5},{5,4},{6,7},{7,6},{8,9},{9,8},{10,11... | collective-permute-start | bytes 20 | tf_op jit(solution)/shard_map/ppermute | solution.py:46
  7.6 7.0 %collective-permute-start.2 = (bf16[512,128]{1,0:T(8,128)(2,1)S(1)}, bf16[512,128]{1,0:T(8,128)(2,1)S(1)}, u32[]{:S(2)}, u32[]{:S(2)}) collective-permute-start(bf16[512,128]{1,0:T(8,128)(2,1)S(1)} %shard_map.95.refs_0_.refs_2_), channel_id=1, source_target_pairs={{0,2},{1,3},{2,0},{3,1},{4,6},{5,7},{6,4},{7,5},{8,10},{9,11},{10,... | collective-permute-start | bytes 393224 | tf_op jit(solution)/shard_map/ppermute | solution.py:42
  8.8 5.8 %collective-permute-start.3 = (bf16[512,128]{1,0:T(8,128)(2,1)S(1)}, bf16[512,128]{1,0:T(8,128)(2,1)S(1)}, u32[]{:S(2)}, u32[]{:S(2)}) collective-permute-start(bf16[512,128]{1,0:T(8,128)(2,1)S(1)} %shard_map.95.refs_0_.refs_2_), channel_id=1, source_target_pairs={{0,4},{1,5},{2,6},{3,7},{4,0},{5,1},{6,2},{7,3},{8,12},{9,13},{10,... | collective-permute-start | bytes 393224 | tf_op jit(solution)/shard_map/ppermute | solution.py:42
  10.6 0.7 %copy-start.2 = (s32[1,8]{1,0:T(1,128)S(1)}, s32[1,8]{1,0:T(1,128)}, u32[]{:S(2)}) copy-start(s32[1,8]{1,0:T(1,128)} %order.1) | copy-start | bytes 100
  12.5 2.2 %collective-permute-start.8 = (bf16[128,2048]{1,0:T(8,128)(2,1)S(1)}, bf16[128,2048]{1,0:T(8,128)(2,1)S(1)}, u32[]{:S(2)}, u32[]{:S(2)}) collective-permute-start(bf16[128,2048]{1,0:T(8,128)(2,1)S(1)} %bitcast.2), channel_id=1, source_target_pairs={{0,1},{1,0},{2,3},{3,2},{4,5},{5,4},{6,7},{7,6},{8,9},{9,8},{10,11... | collective-permute-start | bytes 1572872 | tf_op jit(solution)/shard_map/ppermute | solution.py:46
  12.6 6.4 %collective-permute-start.7 = (bf16[1024,128]{1,0:T(8,128)(2,1)S(1)}, bf16[1024,128]{1,0:T(8,128)(2,1)S(1)}, u32[]{:S(2)}, u32[]{:S(2)}) collective-permute-start(bf16[1024,128]{1,0:T(8,128)(2,1)S(1)} %shard_map.97.refs_0_.refs_2_.refs_6_.refs_9_), channel_id=1, source_target_pairs={{0,2},{1,5},{2,0},{3,7},{4,6},{5,1},{6,4},{7,3},{8,10},{9,13},{10,... | collective-permute-start | bytes 786440 | tf_op jit(solution)/shard_map/ppermute | solution.py:42
  15.1 5.6 %collective-permute-start.10 = (bf16[288,128]{1,0:T(8,128)(2,1)S(1)}, bf16[288,128]{1,0:T(8,128)(2,1)S(1)}, u32[]{:S(2)}, u32[]{:S(2)}) collective-permute-start(bf16[288,128]{1,0:T(8,128)(2,1)S(1)} %shard_map.99.refs_9_), channel_id=1, source_target_pairs={{0,8},{1,9},{2,10},{3,11},{4,12},{5,13},{6,14},{7,15},{8,16},{9,17... | collective-permute-start | bytes 221192 | tf_op jit(solution)/shard_map/ppermute | solution.py:42
  19.1 9.0 %collective-permute-start.9 = (bf16[1024,128]{1,0:T(8,128)(2,1)S(1)}, bf16[1024,128]{1,0:T(8,128)(2,1)S(1)}, u32[]{:S(2)}, u32[]{:S(2)}) collective-permute-start(bf16[1024,128]{1,0:T(8,128)(2,1)S(1)} %shard_map.100), channel_id=1, source_target_pairs={{0,4},{1,3},{2,6},{3,1},{4,0},{5,7},{6,2},{7,5},{8,12},{9,11},{10,... | collective-permute-start | bytes 786440 | tf_op jit(solution)/shard_map/ppermute | solution.py:42
  20.7 6.2 %collective-permute-start.11 = (bf16[288,128]{1,0:T(8,128)(2,1)S(1)}, bf16[288,128]{1,0:T(8,128)(2,1)S(1)}, u32[]{:S(2)}, u32[]{:S(2)}) collective-permute-start(bf16[288,128]{1,0:T(8,128)(2,1)S(1)} %shard_map.101.refs_5_.refs_12_), channel_id=1, source_target_pairs={{0,6},{1,7},{2,4},{3,5},{4,2},{5,3},{6,0},{7,1},{8,14},{9,15},{10,... | collective-permute-start | bytes 221192 | tf_op jit(solution)/shard_map/ppermute | solution.py:42
  22.9 5.6 %collective-permute-start.13 = (bf16[288,128]{1,0:T(8,128)(2,1)S(1)}, bf16[288,128]{1,0:T(8,128)(2,1)S(1)}, u32[]{:S(2)}, u32[]{:S(2)}) collective-permute-start(bf16[288,128]{1,0:T(8,128)(2,1)S(1)} %shard_map.101.refs_5_.refs_12_), channel_id=1, source_target_pairs={{0,2},{1,3},{2,0},{3,1},{4,6},{5,7},{6,4},{7,5},{8,10},{9,11},{10,... | collective-permute-start | bytes 221192 | tf_op jit(solution)/shard_map/ppermute | solution.py:42
  23.5 5.2 %collective-permute-start.14 = (bf16[288,128]{1,0:T(8,128)(2,1)S(1)}, bf16[288,128]{1,0:T(8,128)(2,1)S(1)}, u32[]{:S(2)}, u32[]{:S(2)}) collective-permute-start(bf16[288,128]{1,0:T(8,128)(2,1)S(1)} %shard_map.101.refs_5_.refs_12_), channel_id=1, source_target_pairs={{0,4},{1,5},{2,6},{3,7},{4,0},{5,1},{6,2},{7,3},{8,12},{9,13},{10,... | collective-permute-start | bytes 221192 | tf_op jit(solution)/shard_map/ppermute | solution.py:42
  26.9 14.5 %collective-permute-start.12 = (bf16[1024,128]{1,0:T(8,128)(2,1)S(1)}, bf16[1024,128]{1,0:T(8,128)(2,1)S(1)}, u32[]{:S(2)}, u32[]{:S(2)}) collective-permute-start(bf16[1024,128]{1,0:T(8,128)(2,1)S(1)} %shard_map.102), channel_id=1, source_target_pairs={{0,4},{1,3},{2,6},{3,1},{4,0},{5,7},{6,2},{7,5},{8,12},{9,11},{10,... | collective-permute-start | bytes 786440 | tf_op jit(solution)/shard_map/ppermute | solution.py:42
  29.0 5.6 %collective-permute-start.15 = (bf16[288,128]{1,0:T(8,128)(2,1)S(1)}, bf16[288,128]{1,0:T(8,128)(2,1)S(1)}, u32[]{:S(2)}, u32[]{:S(2)}) collective-permute-start(bf16[288,128]{1,0:T(8,128)(2,1)S(1)} %get-tuple-element.29), channel_id=1, source_target_pairs={{0,8},{1,9},{2,10},{3,11},{4,12},{5,13},{6,14},{7,15},{8,16},{9,17... | collective-permute-start | bytes 221192 | tf_op jit(solution)/shard_map/ppermute | solution.py:42
  32.6 6.4 %collective-permute-start.20 = (bf16[544,128]{1,0:T(8,128)(2,1)S(1)}, bf16[544,128]{1,0:T(8,128)(2,1)S(1)}, u32[]{:S(2)}, u32[]{:S(2)}) collective-permute-start(bf16[544,128]{1,0:T(8,128)(2,1)S(1)} %get-tuple-element.34.refs_0_), channel_id=1, source_target_pairs={{0,2},{1,5},{2,0},{3,7},{4,6},{5,1},{6,4},{7,3},{8,10},{9,13},{10,... | collective-permute-start | bytes 417800 | tf_op jit(solution)/shard_map/ppermute | solution.py:42
  34.6 5.7 %collective-permute-start.18 = (bf16[288,128]{1,0:T(8,128)(2,1)S(1)}, bf16[288,128]{1,0:T(8,128)(2,1)S(1)}, u32[]{:S(2)}, u32[]{:S(2)}) collective-permute-start(bf16[288,128]{1,0:T(8,128)(2,1)S(1)} %collective-permute-done.15.refs_5_.refs_16_), channel_id=1, source_target_pairs={{0,6},{1,7},{2,4},{3,5},{4,2},{5,3},{6,0},{7,1},{8,14},{9,15},{10,... | collective-permute-start | bytes 221192 | tf_op jit(solution)/shard_map/ppermute | solution.py:42
  36.5 5.3 %collective-permute-start.16 = (bf16[288,128]{1,0:T(8,128)(2,1)S(1)}, bf16[288,128]{1,0:T(8,128)(2,1)S(1)}, u32[]{:S(2)}, u32[]{:S(2)}) collective-permute-start(bf16[288,128]{1,0:T(8,128)(2,1)S(1)} %collective-permute-done.15.refs_5_.refs_16_), channel_id=1, source_target_pairs={{0,2},{1,3},{2,0},{3,1},{4,6},{5,7},{6,4},{7,5},{8,10},{9,11},{10,... | collective-permute-start | bytes 221192 | tf_op jit(solution)/shard_map/ppermute | solution.py:42
  37.5 4.4 %collective-permute-start.17 = (bf16[288,128]{1,0:T(8,128)(2,1)S(1)}, bf16[288,128]{1,0:T(8,128)(2,1)S(1)}, u32[]{:S(2)}, u32[]{:S(2)}) collective-permute-start(bf16[288,128]{1,0:T(8,128)(2,1)S(1)} %collective-permute-done.15.refs_5_.refs_16_), channel_id=1, source_target_pairs={{0,4},{1,5},{2,6},{3,7},{4,0},{5,1},{6,2},{7,3},{8,12},{9,13},{10,... | collective-permute-start | bytes 221192 | tf_op jit(solution)/shard_map/ppermute | solution.py:42
  40.3 7.7 %collective-permute-start.21 = (bf16[1088,128]{1,0:T(8,128)(2,1)S(1)}, bf16[1088,128]{1,0:T(8,128)(2,1)S(1)}, u32[]{:S(2)}, u32[]{:S(2)}) collective-permute-start(bf16[1088,128]{1,0:T(8,128)(2,1)S(1)} %shard_map.109), channel_id=1, source_target_pairs={{0,4},{1,3},{2,6},{3,1},{4,0},{5,7},{6,2},{7,5},{8,12},{9,11},{10,... | collective-permute-start | bytes 835592 | tf_op jit(solution)/shard_map/ppermute | solution.py:42
  41.9 3.9 %copy-start.1 = (bf16[1,256,2048]{2,1,0:T(8,128)(2,1)S(1)}, bf16[1,256,2048]{2,1,0:T(8,128)(2,1)}, u32[]{:S(2)}) copy-start(bf16[1,256,2048]{2,1,0:T(8,128)(2,1)} %param.11) | copy-start | bytes 3145732
  42.2 6.1 %collective-permute-start.23 = (bf16[288,128]{1,0:T(8,128)(2,1)S(1)}, bf16[288,128]{1,0:T(8,128)(2,1)S(1)}, u32[]{:S(2)}, u32[]{:S(2)}) collective-permute-start(bf16[288,128]{1,0:T(8,128)(2,1)S(1)} %shard_map.106.refs_0_), channel_id=1, source_target_pairs={{0,2},{1,3},{2,0},{3,1},{4,6},{5,7},{6,4},{7,5},{8,10},{9,11},{10,... | collective-permute-start | bytes 221192 | tf_op jit(solution)/shard_map/ppermute | solution.py:42
  43.5 5.0 %collective-permute-start.24 = (bf16[288,128]{1,0:T(8,128)(2,1)S(1)}, bf16[288,128]{1,0:T(8,128)(2,1)S(1)}, u32[]{:S(2)}, u32[]{:S(2)}) collective-permute-start(bf16[288,128]{1,0:T(8,128)(2,1)S(1)} %shard_map.106.refs_0_), channel_id=1, source_target_pairs={{0,4},{1,5},{2,6},{3,7},{4,0},{5,1},{6,2},{7,3},{8,12},{9,13},{10,... | collective-permute-start | bytes 221192 | tf_op jit(solution)/shard_map/ppermute | solution.py:42
  44.3 5.3 %collective-permute-start.25 = (bf16[288,128]{1,0:T(8,128)(2,1)S(1)}, bf16[288,128]{1,0:T(8,128)(2,1)S(1)}, u32[]{:S(2)}, u32[]{:S(2)}) collective-permute-start(bf16[288,128]{1,0:T(8,128)(2,1)S(1)} %shard_map.106.refs_0_), channel_id=1, source_target_pairs={{0,6},{1,7},{2,4},{3,5},{4,2},{5,3},{6,0},{7,1},{8,14},{9,15},{10,... | collective-permute-start | bytes 221192 | tf_op jit(solution)/shard_map/ppermute | solution.py:42
  47.9 2.5 %collective-permute-start.19 = (bf16[256,384]{1,0:T(8,128)(2,1)S(1)}, bf16[256,384]{1,0:T(8,128)(2,1)S(1)}, u32[]{:S(2)}, u32[]{:S(2)}) collective-permute-start(bf16[256,384]{1,0:T(8,128)(2,1)S(1)} %get-tuple-element.32), channel_id=1, source_target_pairs={{0,1},{1,0},{2,3},{3,2},{4,5},{5,4},{6,7},{7,6},{8,9},{9,8},{10,11... | collective-permute-start | bytes 589832 | tf_op jit(solution)/shard_map/ppermute | solution.py:46
  49.8 1.5 %collective-permute-start.26 = (f32[256,128]{1,0:T(8,128)S(1)}, f32[256,128]{1,0:T(8,128)S(1)}, u32[]{:S(2)}, u32[]{:S(2)}) collective-permute-start(f32[256,128]{1,0:T(8,128)S(1)} %get-tuple-element.40), channel_id=1, source_target_pairs={{0,1},{1,0},{2,3},{3,2},{4,5},{5,4},{6,7},{7,6},{8,9},{9,8},{10,11... | collective-permute-start | bytes 393224 | tf_op jit(solution)/shard_map/ppermute | solution.py:46
  49.9 1.5 %collective-permute-start.22 = (bf16[256,256]{1,0:T(8,128)(2,1)S(1)}, bf16[256,256]{1,0:T(8,128)(2,1)S(1)}, u32[]{:S(2)}, u32[]{:S(2)}) collective-permute-start(bf16[256,256]{1,0:T(8,128)(2,1)S(1)} %get-tuple-element.37), channel_id=1, source_target_pairs={{0,1},{1,0},{2,3},{3,2},{4,5},{5,4},{6,7},{7,6},{8,9},{9,8},{10,11... | collective-permute-start | bytes 393224 | tf_op jit(solution)/shard_map/ppermute | solution.py:46
